TPU v7x, 256 devices: a whole 4x4x8 slice. The times are simulated.
256 devices in a mesh: narrow: 8 (over y, core), wide: 32 (over x, z).
Axes of the slice: x: 4, y: 4, z: 8, core: 2. Of those that a mesh axis runs over, the one named last changes fastest.
Arguments:
- image_emb: bfloat16 [16384, 1024], P(('narrow', 'wide')), may hold values from -0.5 to 0.5
- text_emb: bfloat16 [16384, 1024], P(('wide', 'narrow')), may hold values from -0.5 to 0.5
- caption_group: int32 [16384], replicated, may hold values from 0 to 8191, as said below
Outputs:
- image_grad: float32 [16384, 1024], P(('narrow', 'wide'))
- text_grad: float32 [16384, 1024], P(('wide', 'narrow'))
Inputs may be any that keep to these rules, and one draw needn't show every extreme that they name: `caption_group`: ids 0 and 8191 both occur.
All inputs are finite; a program needn't handle non-finite values.
Results may differ from a plain program's by a relative error of at most 0.002.
Values may be sent and summed in bfloat16 or wider, within the bound.
No kernel may reach another device: no remote copies, remote signals or barrier semaphores. Data moves between devices by JAX's collectives and lax.ppermute only.
A program may use at most 64 MiB of HBM per device.

v0:
```python
import jax
import jax.numpy as jnp
from jax import lax
from jax.sharding import PartitionSpec as P

logit_scale = 100.0
floor_value = -1e30


def masked_logits(rows_emb, cols_emb, row_index, col_index, row_group, col_group):
    scores = logit_scale * lax.dot_general(
        rows_emb, cols_emb, (((1,), (1,)), ((), ())), preferred_element_type=jnp.float32
    )
    diagonal = row_index[:, None] == col_index[None, :]
    repeated = row_group[:, None] == col_group[None, :]
    valid = jnp.logical_or(jnp.logical_not(repeated), diagonal)
    return (scores, valid, diagonal)


def grad_tile(scores, valid, diagonal, row_lse, col_lse):
    weight = jnp.exp(scores - row_lse[:, None]) + jnp.exp(scores - col_lse[None, :])
    grad = 0.5 * jnp.where(valid, weight, 0.0) - jnp.where(diagonal, 1.0, 0.0)
    return grad.astype(jnp.bfloat16)


def tile_stats(rows_emb, cols_emb, row_index, col_index, row_group, col_group):
    rows = rows_emb.shape[0]
    cols = cols_emb.shape[0]
    block = min(512, rows)
    count = rows // block

    def tile_step(carry, pieces):
        col_peak, col_total = carry
        emb, index, group = pieces
        scores, valid, diagonal = masked_logits(emb, cols_emb, index, col_index, group, col_group)
        kept = jnp.where(valid, scores, floor_value)
        row_peak = jnp.max(kept, axis=1)
        row_total = jnp.sum(jnp.where(valid, jnp.exp(kept - row_peak[:, None]), 0.0), axis=1)
        top = jnp.maximum(col_peak, jnp.max(kept, axis=0))
        block_total = jnp.sum(jnp.where(valid, jnp.exp(kept - top[None, :]), 0.0), axis=0)
        col_total = col_total * jnp.exp(col_peak - top) + block_total
        return ((top, col_total), (row_peak, row_total))

    init = (jnp.full((cols,), floor_value, jnp.float32), jnp.zeros((cols,), jnp.float32))
    pieces = (
        rows_emb.reshape(count, block, rows_emb.shape[1]),
        row_index.reshape(count, block),
        row_group.reshape(count, block),
    )
    (col_peak, col_total), (row_peak, row_total) = lax.scan(tile_step, init, pieces)
    return (row_peak.reshape(rows), row_total.reshape(rows), col_peak, col_total)


def merge_wide(peak, total):
    top = lax.pmax(peak, "wide")
    total = lax.psum(total * jnp.exp(peak - top), "wide")
    peak = top
    return peak + jnp.log(total)


def merge_narrow(peak, total):
    top = lax.pmax(peak, "narrow")
    total = lax.psum(total * jnp.exp(peak - top), "narrow")
    peak = top
    return peak + jnp.log(total)


def gather_wide(values):
    return lax.all_gather(values, "wide", axis=0, tiled=True)


def gather_narrow(values):
    return lax.all_gather(values, "narrow", axis=0, tiled=True)


def scatter_wide(term, span):
    return lax.psum_scatter(
        term(jnp.int32(0), span * lax.axis_size("wide")), "wide", scatter_dimension=0, tiled=True
    )


def scatter_narrow(term, span):
    return lax.psum_scatter(
        term(jnp.int32(0), span * lax.axis_size("narrow")),
        "narrow",
        scatter_dimension=0,
        tiled=True,
    )


def full_grad(rows_emb, cols_emb, row_index, col_index, row_group, col_group, row_lse, col_lse):
    rows = rows_emb.shape[0]
    block = min(512, rows)
    count = rows // block

    def full_step(carry, pieces):
        emb, index, group, lse = pieces
        scores, valid, diagonal = masked_logits(emb, cols_emb, index, col_index, group, col_group)
        return (carry, grad_tile(scores, valid, diagonal, lse, col_lse))

    pieces = (
        rows_emb.reshape(count, block, rows_emb.shape[1]),
        row_index.reshape(count, block),
        row_group.reshape(count, block),
        row_lse.reshape(count, block),
    )
    unused, tiles = lax.scan(full_step, jnp.zeros((), jnp.float32), pieces)
    return tiles.reshape(rows, cols_emb.shape[0])


def make_terms(rows_emb, cols_emb, row_index, col_index, row_group, col_group, row_lse, col_lse):
    grad = full_grad(
        rows_emb, cols_emb, row_index, col_index, row_group, col_group, row_lse, col_lse
    )

    def row_term(start, count):
        return logit_scale * jnp.dot(grad, cols_emb, preferred_element_type=jnp.float32)

    def col_term(start, count):
        return logit_scale * lax.dot_general(
            grad, rows_emb, (((0,), (0,)), ((), ())), preferred_element_type=jnp.float32
        )

    return (row_term, col_term)


def per_device(image_emb, text_emb, caption_group):
    span = image_emb.shape[0]
    n_wide = lax.axis_size("wide")
    n_narrow = lax.axis_size("narrow")
    at_wide = lax.axis_index("wide")
    at_narrow = lax.axis_index("narrow")
    rows_emb = gather_wide(image_emb)
    cols_emb = gather_narrow(text_emb)
    row_index = at_narrow * (n_wide * span) + jnp.arange(n_wide * span, dtype=jnp.int32)
    col_index = at_wide * (n_narrow * span) + jnp.arange(n_narrow * span, dtype=jnp.int32)
    row_group = jnp.take(caption_group, row_index)
    col_group = jnp.take(caption_group, col_index)
    row_peak, row_total, col_peak, col_total = tile_stats(
        rows_emb, cols_emb, row_index, col_index, row_group, col_group
    )
    row_lse = merge_wide(row_peak, row_total)
    col_lse = merge_narrow(col_peak, col_total)
    row_term, col_term = make_terms(
        rows_emb, cols_emb, row_index, col_index, row_group, col_group, row_lse, col_lse
    )
    image_grad = scatter_wide(row_term, span)
    text_grad = scatter_narrow(col_term, span)
    return (image_grad, text_grad)


def solution(mesh):
    return jax.shard_map(
        per_device,
        mesh=mesh,
        in_specs=(P(("narrow", "wide"), None), P(("wide", "narrow"), None), P()),
        out_specs=(P(("narrow", "wide"), None), P(("wide", "narrow"), None)),
        check_vma=False,
    )
```

profile of v0, /device:TPU:8, one launch (start us, length us, event | category | flops | bytes accessed | tf_op | source)
XLA Modules:
  0.0 591.1 jit_solution(12833182041759766373)
XLA Ops:
  7.2 0.7 all-gather.5.cloned.1.call-update
  8.0 0.7 all-gather.3.cloned.1.call-update
  8.8 3.1 gather_fusion.1
  12.0 11.8 %gather_fusion = s32[2048]{0:T(1024)S(1)} fusion(s32[16384]{0:T(1024)S(1)} %copy-done, s32[2048]{0:T(1024)S(1)} %broadcast_clamp_fusion), kind=kCustom, calls=%fused_computation | custom fusion | bytes 24576 | tf_op jit(solution)/shard_map/jit(_take)/gather | solution.py:137
  23.8 13.2 %all-gather.5.cloned.1.call-done = bf16[512,1024]{1,0:T(8,128)(2,1)} async-done(((bf16[64,1024]{1,0:T(8,128)(2,1)}), bf16[512,1024]{1,0:T(8,128)(2,1)}) %all-gather.5.cloned.1.call-update) | async-done | bytes 1048592 | tf_op jit(solution)/shard_map/all_gather | solution.py:73
  37.0 85.9 %all-gather.3.cloned.1.call-done = bf16[2048,1024]{1,0:T(8,128)(2,1)} async-done(((bf16[64,1024]{1,0:T(8,128)(2,1)}), bf16[2048,1024]{1,0:T(8,128)(2,1)}) %all-gather.3.cloned.1.call-update) | async-done | bytes 4194320 | tf_op jit(solution)/shard_map/all_gather | solution.py:69
  123.0 14.1 %while.29 = (s32[]{:T(128)}, f32[512]{0:T(512)S(1)}, f32[512]{0:T(512)S(1)}, f32[4,512]{1,0:T(4,128)S(1)}, f32[4,512]{1,0:T(4,128)S(1)}, /*index=5*/s32[4,512]{1...) while((s32[]{:T(128)}, f32[512]{0:T(512)S(1)}, ...), condition=%wide.region_5.6_spmd.clone, body=%wide.region_0.5_spmd.clone.sunk | while | flops 541591552 | bytes 4262052 | solution.py:50
  123.0 2.5 fusion.43
  125.5 0.8 select_reduce_fusion.3
  126.4 0.1 dynamic_update_slice.20
  126.4 0.1 dynamic_update_slice.19
  126.5 2.5 fusion.43
  129.1 0.8 select_reduce_fusion.3
  129.9 0.1 dynamic_update_slice.20
  130.0 2.5 fusion.43
  132.6 0.8 select_reduce_fusion.3
  133.6 2.5 fusion.43
  136.1 0.8 select_reduce_fusion.3
  137.1 10.0 %pmax.15 = f32[512]{0:T(512)S(1)} all-reduce(f32[512]{0:T(512)S(1)} %get-tuple-element.116), channel_id=1, replica_groups=mesh['narrow'=8,'wide'=32] {'narrow'}, use_global_device_ids=true, to_apply=%region_8.9 | all-reduce | flops 512 | bytes 4096 | tf_op jit(solution)/shard_map/pmax | solution.py:62
  147.1 12.4 %psum.15 = f32[512]{0:T(512)S(1)} all-reduce(f32[512]{0:T(512)S(1)} %exponential_multiply_fusion.1), channel_id=1, replica_groups=mesh['narrow'=8,'wide'=32] {'narrow'}, use_global_device_ids=true, to_apply=%region_9.10 | all-reduce | flops 512 | bytes 4096 | tf_op jit(solution)/shard_map/psum | solution.py:63
  159.5 73.6 %pmax.14 = f32[2048]{0:T(1024)S(1)} all-reduce(f32[2048]{0:T(1024)S(1)} %bitcast.69), channel_id=1, replica_groups=mesh['narrow'=8,'wide'=32] {'wide'}, use_global_device_ids=true, to_apply=%region_6.7 | all-reduce | flops 2048 | bytes 16384 | tf_op jit(solution)/shard_map/pmax | solution.py:55
  233.2 70.8 %psum.14 = f32[2048]{0:T(1024)S(1)} all-reduce(f32[2048]{0:T(1024)S(1)} %exponential_multiply_fusion), channel_id=1, replica_groups=mesh['narrow'=8,'wide'=32] {'wide'}, use_global_device_ids=true, to_apply=%region_7.8 | all-reduce | flops 2048 | bytes 16384 | tf_op jit(solution)/shard_map/psum | solution.py:56
  304.0 11.2 %while.28 = (s32[]{:T(128)}, bf16[4,512,512]{2,1,0:T(8,128)(2,1)S(1)}, s32[4,512]{1,0:T(4,128)S(1)}, s32[512]{0:T(512)S(1)}, s32[4,512]{1,0:T(4,128)S(1)}, /*ind...) while((s32[]{:T(128)}, ...), condition=%wide.region_11.12_spmd.clone, body=%wide.region_10.11_spmd.clone.sunk | while | flops 540279296 | bytes 2649217 | solution.py:107
  304.0 2.7 fusion.41
  306.8 2.7 fusion.41
  309.6 2.7 fusion.41
  312.4 2.7 fusion.41
  315.2 6.0 %convolution_multiply_fusion.3 = f32[512,1024]{1,0:T(8,128)} fusion(bf16[2048,512]{1,0:T(8,128)(2,1)S(1)} %bitcast.81, bf16[2048,1024]{1,0:T(8,128)(2,1)} %bitcast.80), kind=kOutput, calls=%fused_computation.33 | convolution fusion | flops 2148007936 | bytes 8388608 | tf_op jit(solution)/shard_map/dot_general | solution.py:120
  321.2 1.1 copy-done.1
  322.4 5.6 convolution_multiply_fusion.2
  328.0 21.2 %reduce-scatter.5.cloned.1.call-done = f32[64,1024]{1,0:T(8,128)} async-done(((f32[512,1024]{1,0:T(8,128)}), f32[64,1024]{1,0:T(8,128)}) %reduce-scatter.5.cloned.1.call-update) | async-done | bytes 262160 | tf_op jit(solution)/shard_map/reduce_scatter | solution.py:83
  349.2 235.3 %reduce-scatter.3.cloned.1.call-done = f32[64,1024]{1,0:T(8,128)} async-done(((f32[2048,1024]{1,0:T(8,128)}), f32[64,1024]{1,0:T(8,128)}) %reduce-scatter.3.cloned.1.call-update) | async-done | bytes 262160 | tf_op jit(solution)/shard_map/reduce_scatter | solution.py:77
  (65 shorter events, 0.8 us)
Async XLA Ops:
  7.2 1.6 copy-start
  7.2 29.9 %all-gather.5.cloned.1.call-start = ((), (), s32[]{:S(2)}) async-start(), calls=%async_computation.3 | async-start | bytes 1179648 | tf_op jit(solution)/shard_map/all_gather | solution.py:73
  7.9 115.1 %all-gather.3.cloned.1.call-start = ((), (), s32[]{:S(2)}) async-start(), calls=%async_computation.2 | async-start | bytes 4325376 | tf_op jit(solution)/shard_map/all_gather | solution.py:69
  8.7 340.6 %reduce-scatter.5.cloned.1.call-start = ((), (), s32[]{:S(2)}) async-start(), calls=%async_computation.5 | async-start | bytes 2359296 | tf_op jit(solution)/shard_map/reduce_scatter | solution.py:83
  321.1 1.2 copy-start.1
  321.2 263.4 %reduce-scatter.3.cloned.1.call-start = ((), (), s32[]{:S(2)}) async-start(), calls=%async_computation.4 | async-start | bytes 8650752 | tf_op jit(solution)/shard_map/reduce_scatter | solution.py:77
Sparse Core Ops, SparseCore 0:
  9.9 27.1 all-gather.4
  39.6 83.2 all-gather.2
  321.3 27.8 reduce-scatter.4
  353.7 230.8 reduce-scatter.2
where the time goes:
time: 592 us; the launch traced here: 591 us
  waiting for transfers between devices  357 us (60%)
  blocking collectives  167 us (28%)
  matrix products  32.7 us (6%)
  local copies, waits for them, and re-layouts  16.6 us (3%)
  between operations  13.9 us (2%)
    reduce_scatter x1, waiting for transfers between devices, scatter_wide(): lax.psum_scatter(term(jnp.int32(0), span * lax.axis_size('wide')), 'wide'...  235 us
    all_gather x1, waiting for transfers between devices, gather_wide(): return lax.all_gather(values, 'wide', axis=0, tiled=True)  85.9 us
    pmax x1, blocking collectives, merge_wide(): top = lax.pmax(peak, 'wide')  73.6 us
    psum x1, blocking collectives, merge_wide(): total = lax.psum(total * jnp.exp(peak - top), 'wide')  70.8 us
    reduce_scatter x1, waiting for transfers between devices, scatter_narrow(): lax.psum_scatter(term(jnp.int32(0), span * lax.axis_size('narrow')), 'nar...  21.2 us
    dot_general x8, matrix products, masked_logits(): lax.dot_general(rows_emb, cols_emb, (((1,), (1,)), ((), ())), preferred_e...  21.1 us
    all_gather x1, waiting for transfers between devices, gather_narrow(): return lax.all_gather(values, 'narrow', axis=0, tiled=True)  13.2 us
    psum x1, blocking collectives, merge_narrow(): total = lax.psum(total * jnp.exp(peak - top), 'narrow')  12.4 us
  transfers between devices with their start and end apart: 4, of which 4 were waited for; matrix products, arithmetic and copies ran while one was open for 3% of the time, Pallas kernels for 0%

commit v1 on v0

v1 whole, which is shorter than its diff:
```python
import jax
import jax.numpy as jnp
from jax import lax
from jax.experimental import pallas as pl
from jax.experimental.pallas import tpu as pltpu
from jax.sharding import Mesh, PartitionSpec as P

logit_scale = 100.0
floor_value = -1e30
mib = 1024 * 1024

axes = ("y", "core", "x", "z")
plane = ("y", "x")


def shift(values, axis, step):
    size = lax.axis_size(axis)
    return lax.ppermute(values, axis, [(i, (i + step) % size) for i in range(size)])


def z_order(size):
    order = [size // 2]
    for step in range(size // 2 - 1, 0, -1):
        order += [step, size - step]
    return order


def spread_plane(values, count):
    return lax.all_to_all(jnp.broadcast_to(values[None], (count,) + values.shape), plane, 0, 0)


def stats_kernel(rows_ref, cols_ref, ri_ref, rg_ref, ci_ref, cg_ref, kept_ref, row_ref, col_ref, peak, total):
    step = pl.program_id(0)
    scores = logit_scale * lax.dot_general(
        rows_ref[...], cols_ref[...], (((1,), (1,)), ((), ())), preferred_element_type=jnp.float32
    )
    valid = jnp.logical_or(rg_ref[...] != cg_ref[...], ri_ref[...] == ci_ref[...])
    kept = jnp.where(valid, scores, floor_value)
    kept_ref[...] = kept

    row_peak = jnp.max(kept, axis=1, keepdims=True)
    row_total = jnp.sum(jnp.exp(kept - row_peak), axis=1, keepdims=True)
    row_lse = row_peak + jnp.log(row_total)
    row_ref[...] = jnp.broadcast_to(row_lse, (row_lse.shape[0], 128)).T[0:1, :]

    @pl.when(step == 0)
    def _():
        peak[...] = jnp.full_like(peak, floor_value)
        total[...] = jnp.zeros_like(total)

    old = peak[...]
    top = jnp.maximum(old, jnp.max(kept, axis=0, keepdims=True))
    summed = total[...] * jnp.exp(old - top) + jnp.sum(jnp.exp(kept - top), axis=0, keepdims=True)
    peak[...] = top
    total[...] = summed

    @pl.when(step == pl.num_programs(0) - 1)
    def _():
        col_ref[...] = top + jnp.log(summed)


def block_stats(rows, cols, ri, rg, ci, cg):
    n_rows, width = rows.shape
    n_cols = cols.shape[0]
    block = 256
    return pl.pallas_call(
        stats_kernel,
        grid=(n_rows // block,),
        in_specs=[
            pl.BlockSpec((block, width), lambda i: (i, 0)),
            pl.BlockSpec((n_cols, width), lambda i: (0, 0)),
            pl.BlockSpec((block, 1), lambda i: (i, 0)),
            pl.BlockSpec((block, 1), lambda i: (i, 0)),
            pl.BlockSpec((1, n_cols), lambda i: (0, 0)),
            pl.BlockSpec((1, n_cols), lambda i: (0, 0)),
        ],
        out_specs=[
            pl.BlockSpec((block, n_cols), lambda i: (i, 0)),
            pl.BlockSpec((1, block), lambda i: (0, i)),
            pl.BlockSpec((1, n_cols), lambda i: (0, 0)),
        ],
        out_shape=[
            jax.ShapeDtypeStruct((n_rows, n_cols), jnp.float32),
            jax.ShapeDtypeStruct((1, n_rows), jnp.float32),
            jax.ShapeDtypeStruct((1, n_cols), jnp.float32),
        ],
        scratch_shapes=[pltpu.VMEM((1, n_cols), jnp.float32), pltpu.VMEM((1, n_cols), jnp.float32)],
        compiler_params=pltpu.CompilerParams(vmem_limit_bytes=32 * mib),
        cost_estimate=pl.CostEstimate(
            flops=2 * n_rows * n_cols * width, bytes_accessed=8 * mib, transcendentals=2 * n_rows * n_cols
        ),
        name="stats",
    )(rows, cols, ri, rg, ci, cg)


def merge(parts):
    top = jnp.max(parts, axis=0, keepdims=True)
    return top + jnp.log(jnp.sum(jnp.exp(parts - top), axis=0, keepdims=True))


def grad_kernel(kept_ref, rows_ref, row_parts, col_parts, ri_ref, ci_ref, grad_ref, text_ref):
    step = pl.program_id(0)
    row_lse = merge(row_parts[...])
    row_lse = jnp.broadcast_to(row_lse, (128, row_lse.shape[1])).T[:, 0:1]
    col_lse = merge(col_parts[...])
    kept = kept_ref[...]
    weight = jnp.exp(kept - row_lse) + jnp.exp(kept - col_lse)
    grad = 0.5 * weight - jnp.where(ri_ref[...] == ci_ref[...], 1.0, 0.0)
    grad = grad.astype(jnp.bfloat16)
    grad_ref[...] = grad
    part = lax.dot_general(grad, rows_ref[...], (((0,), (0,)), ((), ())), preferred_element_type=jnp.float32)

    @pl.when(step == 0)
    def _():
        text_ref[...] = part

    @pl.when(step > 0)
    def _():
        text_ref[...] += part


def block_grad(kept, rows, row_parts, col_parts, ri, ci):
    n_rows, width = rows.shape
    n_cols = kept.shape[1]
    block = 256
    return pl.pallas_call(
        grad_kernel,
        grid=(n_rows // block,),
        in_specs=[
            pl.BlockSpec((block, n_cols), lambda i: (i, 0)),
            pl.BlockSpec((block, width), lambda i: (i, 0)),
            pl.BlockSpec((row_parts.shape[0], block), lambda i: (0, i)),
            pl.BlockSpec((col_parts.shape[0], n_cols), lambda i: (0, 0)),
            pl.BlockSpec((block, 1), lambda i: (i, 0)),
            pl.BlockSpec((1, n_cols), lambda i: (0, 0)),
        ],
        out_specs=[
            pl.BlockSpec((block, n_cols), lambda i: (i, 0)),
            pl.BlockSpec((n_cols, width), lambda i: (0, 0)),
        ],
        out_shape=[
            jax.ShapeDtypeStruct((n_rows, n_cols), jnp.bfloat16),
            jax.ShapeDtypeStruct((n_cols, width), jnp.float32),
        ],
        compiler_params=pltpu.CompilerParams(vmem_limit_bytes=32 * mib),
        cost_estimate=pl.CostEstimate(
            flops=2 * n_rows * n_cols * width, bytes_accessed=12 * mib, transcendentals=2 * n_rows * n_cols
        ),
        name="grad",
    )(kept, rows, row_parts, col_parts, ri, ci)


def per_device(image_emb, text_emb, caption_group):
    span, width = image_emb.shape
    n_y, n_core, n_x, n_z = (lax.axis_size(a) for a in axes)
    y, core, x, z = (lax.axis_index(a) for a in axes)
    n_plane = n_y * n_x
    place = jnp.arange(span, dtype=jnp.int32)

    rows = spread_plane(image_emb, n_plane).reshape(n_plane * span, width)
    near = {0: text_emb}
    for step in z_order(n_z):
        near[step] = shift(text_emb, "z", -step)
    near = jnp.concatenate([near[k] for k in range(n_z)], axis=0)
    far = shift(near, "core", 1)
    cols = jnp.concatenate([near, far], axis=0)

    at_y = jnp.arange(n_y, dtype=jnp.int32)[:, None, None]
    at_x = jnp.arange(n_x, dtype=jnp.int32)[None, :, None]
    row_index = ((((at_y * n_core + core) * n_x + at_x) * n_z + z) * span + place).reshape(-1)
    at_core = jnp.stack([core, 1 - core])[:, None, None]
    at_z = ((z + jnp.arange(n_z, dtype=jnp.int32)) % n_z)[None, :, None]
    col_index = ((((x * n_z + at_z) * n_y + y) * n_core + at_core) * span + place).reshape(-1)
    blocks = caption_group.reshape(-1, span)
    row_group = jnp.take(blocks, row_index[::span] // span, axis=0).reshape(-1)
    col_group = jnp.take(blocks, col_index[::span] // span, axis=0).reshape(-1)
    ri, rg = row_index[:, None], row_group[:, None]
    ci, cg = col_index[None, :], col_group[None, :]

    kept, row_part, col_part = block_stats(rows, cols, ri, rg, ci, cg)
    row_parts = spread_plane(row_part[0], n_plane)
    own = col_part.reshape(n_core, n_z, span)
    other = shift(jnp.flip(own, axis=0), "core", 1)
    pair = jnp.stack([own, other])
    doubled = jnp.concatenate([pair, pair], axis=2)
    start = (n_z - z) % n_z
    common = lax.dynamic_slice_in_dim(doubled, start, n_z, axis=2)
    parts = lax.all_to_all(jnp.broadcast_to(common[None], (n_z,) + common.shape), "z", 0, 0)
    parts = parts.reshape(n_z * n_core, n_core, n_z, span)
    parts = lax.dynamic_slice_in_dim(jnp.concatenate([parts, parts], axis=2), z, n_z, axis=2)
    col_parts = parts.reshape(n_z * n_core, -1)

    grad, text_part = block_grad(kept, rows, row_parts, col_parts, ri, ci)
    half = n_z * span
    text_part = text_part[:half] + shift(text_part[half:], "core", 1)
    image_part = jnp.dot(grad, cols, preferred_element_type=jnp.float32)
    image_parts = lax.all_to_all(
        image_part.astype(jnp.bfloat16).reshape(n_plane, span, width), plane, 0, 0
    )
    image_grad = logit_scale * jnp.sum(image_parts.astype(jnp.float32), axis=0)
    text_part = text_part.reshape(n_z, span, width)
    text_sent = text_part.astype(jnp.bfloat16)
    text_grad = text_part[0]
    for step in z_order(n_z):
        text_grad = text_grad + shift(text_sent[step], "z", step).astype(jnp.float32)
    return (image_grad, logit_scale * text_grad)


def solution(mesh):
    fine = Mesh(mesh.devices.reshape(4, 2, 4, 8), axes)
    return jax.shard_map(
        per_device,
        mesh=fine,
        in_specs=(P(axes, None), P(("x", "z", "y", "core"), None), P()),
        out_specs=(P(axes, None), P(("x", "z", "y", "core"), None)),
        check_vma=False,
    )
```

time: 592 us -> 165 us (0.28)
  waiting for transfers between devices: 357 us -> 61 us
  blocking collectives: 167 us -> 0 us
  starting transfers between devices: 0.16 us -> 51.1 us
  matrix products: 32.7 us -> 3.75 us
  between operations: 13.9 us -> 0.85 us
  Pallas kernels: 0 us -> 11.9 us
  local copies, waits for them, and re-layouts: 16.6 us -> 25 us
  other arithmetic: 3.4 us -> 9.34 us
    reduce_scatter x2 -> x0, waiting for transfers between devices: 257 us -> none  [the longest x1 235 us: scatter_wide(): lax.psum_scatter(term(jnp.int32(0), span * lax.axis_size('wide')), 'wide'...]
    all_gather x2 -> x0, waiting for transfers between devices: 99.1 us -> none  [the longest x1 85.9 us: gather_wide(): return lax.all_gather(values, 'wide', axis=0, tiled=True)]
    pmax x2 -> x0, blocking collectives: 83.6 us -> none  [the longest x1 73.6 us: merge_wide(): top = lax.pmax(peak, 'wide')]
    psum x2 -> x0, blocking collectives: 83.2 us -> none  [the longest x1 70.8 us: merge_wide(): total = lax.psum(total * jnp.exp(peak - top), 'wide')]
    all_to_all x0 -> x4, waiting for transfers between devices: none -> 44.6 us  [the longest x1 24.9 us: per_device(): lax.all_to_all(image_part.astype(jnp.bfloat16).reshape(n_plane, span, wid...]
    ppermute x0 -> x17, starting transfers between devices: none -> 29 us  [shift(): lax.ppermute(values, axis, [(i, (i + step) % size) for i in range(size)])]
    dot_general x10 -> x1, matrix products: 32.7 us -> 3.75 us  [per_device(): image_part = jnp.dot(grad, cols, preferred_element_type=jnp.float32)]
    all_to_all x0 -> x4, starting transfers between devices: none -> 22 us  [the longest x2 13.1 us: spread_plane(): lax.all_to_all(jnp.broadcast_to(values[None], (count,) + values.shape), p...]
  transfers between devices with their start and end apart: 4 -> 21, of which waited for: 4 -> 11; matrix products, arithmetic and copies ran while one was open for 3% -> 16% of each run, Pallas kernels for 0% -> 0%
where the time goes in v1:
time: 165 us; the launch traced here: 163 us
  waiting for transfers between devices  61 us (37%)
  starting transfers between devices  51.1 us (31%)
  local copies, waits for them, and re-layouts  25 us (15%)
  Pallas kernels  11.9 us (7%)
  other arithmetic  9.34 us (6%)
  matrix products  3.75 us (2%)
    ppermute x17, starting transfers between devices, shift(): lax.ppermute(values, axis, [(i, (i + step) % size) for i in range(size)])  29 us
    all_to_all x1, waiting for transfers between devices, per_device(): lax.all_to_all(image_part.astype(jnp.bfloat16).reshape(n_plane, span, wid...  24.9 us
    ppermute x17, waiting for transfers between devices, shift(): lax.ppermute(values, axis, [(i, (i + step) % size) for i in range(size)])  16.4 us
    unnamed x24, local copies, waits for them, and re-layouts  13.1 us
    all_to_all x2, starting transfers between devices, spread_plane(): lax.all_to_all(jnp.broadcast_to(values[None], (count,) + values.shape), p...  13.1 us
    all_to_all x2, waiting for transfers between devices, spread_plane(): lax.all_to_all(jnp.broadcast_to(values[None], (count,) + values.shape), p...  11.4 us
    all_to_all x1, waiting for transfers between devices, per_device(): lax.all_to_all(jnp.broadcast_to(common[None], (n_z,) + common.shape), 'z'...  8.36 us
    pallas_call x1, Pallas kernels, block_grad(): pl.pallas_call(grad_kernel, grid=(n_rows // block,), in_specs=[pl.BlockSp...  6.49 us
  transfers between devices with their start and end apart: 21, of which 11 were waited for; matrix products, arithmetic and copies ran while one was open for 16% of the time, Pallas kernels for 0%

profile of v1, /device:TPU:8, one launch (start us, length us, event | category | flops | bytes accessed | tf_op | source)
XLA Modules:
  0.0 162.9 jit_solution(9341491375930116118)
XLA Ops:
  0.6 3.3 %collective-permute-start.5 = (bf16[64,1024]{1,0:T(8,128)(2,1)}, bf16[64,1024]{1,0:T(8,128)(2,1)S(1)}, u32[]{:S(2)}, u32[]{:S(2)}) collective-permute-start(bf16[64,1024]{1,0:T(8,128)(2,1)} %param.6), channel_id=1, source_target_pairs={{0,2},{1,3},{2,4},{3,5},{4,6},{5,7},{6,0},{7,1},{8,10},{9,11},{10,... | collective-permute-start | bytes 393224 | tf_op jit(solution)/shard_map/ppermute | solution.py:18
  4.0 4.9 %collective-permute-start.4 = (bf16[64,1024]{1,0:T(8,128)(2,1)}, bf16[64,1024]{1,0:T(8,128)(2,1)S(1)}, u32[]{:S(2)}, u32[]{:S(2)}) collective-permute-start(bf16[64,1024]{1,0:T(8,128)(2,1)} %param.6), channel_id=1, source_target_pairs={{0,3},{1,4},{2,5},{3,6},{4,7},{5,0},{6,1},{7,2},{8,11},{9,12},{10,... | collective-permute-start | bytes 393224 | tf_op jit(solution)/shard_map/ppermute | solution.py:18
  9.9 4.0 %collective-permute-start.1 = (bf16[64,1024]{1,0:T(8,128)(2,1)}, bf16[64,1024]{1,0:T(8,128)(2,1)S(1)}, u32[]{:S(2)}, u32[]{:S(2)}) collective-permute-start(bf16[64,1024]{1,0:T(8,128)(2,1)} %param.6), channel_id=1, source_target_pairs={{0,6},{1,7},{2,0},{3,1},{4,2},{5,3},{6,4},{7,5},{8,14},{9,15},{10,... | collective-permute-start | bytes 393224 | tf_op jit(solution)/shard_map/ppermute | solution.py:18
  15.0 2.5 %broadcast_in_dim.12 = bf16[16,64,1024]{2,1,0:T(8,128)(2,1)} broadcast(bf16[64,1024]{1,0:T(8,128)(2,1)} %param.5), dimensions={1,2} | broadcast | bytes 2228224 | tf_op jit(solution)/shard_map/broadcast_in_dim | solution.py:29
  17.5 7.5 %all-to-all-start = ((bf16[16,64,1024]{2,1,0:T(8,128)(2,1)}), bf16[16,64,1024]{2,1,0:T(8,128)(2,1)S(1)}, u32[]{:S(2)}, u32[]{:S(2)}) async-start(bf16[16,64,1024]{2,1,0:T(8,128)(2,1)} %broadcast_in_dim.12), calls=%async_computation | async-start | bytes 4194304 | tf_op jit(solution)/shard_map/all_to_all | solution.py:29
  26.2 2.6 %collective-permute-start.2 = (bf16[64,1024]{1,0:T(8,128)(2,1)S(1)}, bf16[64,1024]{1,0:T(8,128)(2,1)S(1)}, u32[]{:S(2)}, u32[]{:S(2)}) collective-permute-start(bf16[64,1024]{1,0:T(8,128)(2,1)S(1)} %copy-done.5), channel_id=1, source_target_pairs={{0,5},{1,6},{2,7},{3,0},{4,1},{5,2},{6,3},{7,4},{8,13},{9,14},{10,... | collective-permute-start | bytes 393224 | tf_op jit(solution)/shard_map/ppermute | solution.py:18
  29.6 1.5 collective-permute-start.6
  31.8 5.2 %collective-permute-done.2 = bf16[64,1024]{1,0:T(8,128)(2,1)S(1)} collective-permute-done((bf16[64,1024]{1,0:T(8,128)(2,1)S(1)}, bf16[64,1024]{1,0:T(8,128)(2,1)S(1)}, u32[]{:S(2)}, u32[]{:S(2)}) %collective-permute-start.2) | collective-permute-done | bytes 131104 | tf_op jit(solution)/shard_map/ppermute | solution.py:18
  43.7 2.4 %constant_dynamic-update-slice_fusion.8.cols_ref = bf16[1024,1024]{1,0:T(8,128)(2,1)} fusion(bf16[1024,1024]{1,0:T(8,128)(2,1)} %get-tuple-element.27, bf16[512,1024]{1,0:T(8,128)(2,1)} %collective-permute-done.7), kind=kLoop, calls=%fused_computation.26 | loop fusion | bytes 2097152 | tf_op jit(solution)/shard_map/concatenate | solution.py:166
  46.0 5.8 %all-to-all-done = bf16[16,64,1024]{2,1,0:T(8,128)(2,1)S(1)} async-done(((bf16[16,64,1024]{2,1,0:T(8,128)(2,1)}), bf16[16,64,1024]{2,1,0:T(8,128)(2,1)S(1)}, u32[]{:S(2)}, u32[]{:S(2)}) %all-to-all-start) | async-done | bytes 2097184 | tf_op jit(solution)/shard_map/all_to_all | solution.py:29
  51.9 1.6 copy-done.1
  53.5 5.4 %stats.1 = (f32[1024,1024]{1,0:T(8,128)S(1)}, f32[1,1024]{1,0:T(1,128)S(1)}, f32[1,1024]{1,0:T(1,128)S(1)}) custom-call(bf16[1024,1024]{1,0:T(8,128)(2,1)S(1)} %bitcast.15, bf16[1024,1024]{1,0:T(8,128)(2,1)S(1)} %copy-done.1, s32[1024,1]{1,0:T(8,128)S(1)} %add.234.ri_ref, s32[1024,1]{1,0:T(8,128)S(1)} %broadcast_in_dim_reshape.10.rg_ref, ...), custom_call_target="tpu_custom_call" | custom-call | flops 2147483648 | bytes 8388608 | tf_op jit(solution)/shard_map/stats/pallas_call | solution.py:66
  58.9 2.0 %copy-done.3 = f32[1024,1024]{1,0:T(8,128)} copy-done((f32[1024,1024]{1,0:T(8,128)}, f32[1024,1024]{1,0:T(8,128)S(1)}, u32[]{:S(2)}) %copy-start.3) | copy-done | bytes 4194328
  62.8 5.6 %all-to-all-start.1 = ((f32[16,1,1024]{2,1,0:T(1,128)}), f32[16,1,1024]{2,1,0:T(1,128)S(1)}, u32[]{:S(2)}, u32[]{:S(2)}) async-start(f32[16,1,1024]{2,1,0:T(1,128)} %broadcast_in_dim.16), calls=%async_computation.1 | async-start | bytes 131072 | tf_op jit(solution)/shard_map/all_to_all | solution.py:29
  69.2 5.5 %all-to-all-done.1 = f32[16,1,1024]{2,1,0:T(1,128)S(1)} async-done(((f32[16,1,1024]{2,1,0:T(1,128)}), f32[16,1,1024]{2,1,0:T(1,128)S(1)}, u32[]{:S(2)}, u32[]{:S(2)}) %all-to-all-start.1) | async-done | bytes 65568 | tf_op jit(solution)/shard_map/all_to_all | solution.py:29
  74.7 3.9 %all-to-all-start.2 = ((f32[8,1,2048]{2,1,0:T(1,128)}), f32[8,1,2048]{2,1,0:T(1,128)S(1)}, u32[]{:S(2)}, u32[]{:S(2)}) async-start(f32[8,1,2048]{2,1,0:T(1,128)} %reshape.242), calls=%async_computation.2 | async-start | bytes 131072 | tf_op jit(solution)/shard_map/all_to_all | solution.py:188
  78.6 8.4 %all-to-all-done.2 = f32[8,1,2048]{2,1,0:T(1,128)S(1)} async-done(((f32[8,1,2048]{2,1,0:T(1,128)}), f32[8,1,2048]{2,1,0:T(1,128)S(1)}, u32[]{:S(2)}, u32[]{:S(2)}) %all-to-all-start.2) | async-done | bytes 65568 | tf_op jit(solution)/shard_map/all_to_all | solution.py:188
  88.6 2.2 %copy-done.4 = f32[1024,1024]{1,0:T(8,128)S(1)} copy-done((f32[1024,1024]{1,0:T(8,128)S(1)}, f32[1024,1024]{1,0:T(8,128)}, u32[]{:S(2)}) %copy-start.4) | copy-done | bytes 4194328
  90.8 6.5 %grad.1 = (bf16[1024,1024]{1,0:T(8,128)(2,1)S(1)}, f32[1024,1024]{1,0:T(8,128)S(1)}) custom-call(f32[1024,1024]{1,0:T(8,128)S(1)} %copy-done.4, bf16[1024,1024]{1,0:T(8,128)(2,1)S(1)} %bitcast.16, f32[16,1024]{1,0:T(8,128)S(1)} %bitcast.17, f32[16,1024]{1,0:T(8,128)S(1)} %reshape.206.col_parts, s32[1024,1]{1,0:T(8,128)S(1)} %add.234.ri_ref, ...), custom_call_target="tpu_custom_call" | custom-call | flops 2147483648 | bytes 12582912 | tf_op jit(solution)/shard_map/grad/pallas_call | solution.py:126
  97.3 1.6 %slice.47 = f32[512,1024]{1,0:T(8,128)} slice(f32[1024,1024]{1,0:T(8,128)S(1)} %get-tuple-element.12), slice={[512:1024], [0:1024]} | slice | bytes 4194304 | tf_op jit(solution)/shard_map/slice | solution.py:195
  100.4 3.8 %convolution_convert_fusion = bf16[1024,1024]{1,0:T(8,128)(2,1)} fusion(bf16[1024,1024]{1,0:T(8,128)(2,1)S(1)} %get-tuple-element.11, bf16[1024,1024]{1,0:T(8,128)(2,1)S(1)} %copy-done.2), kind=kOutput, calls=%fused_computation.4 | convolution fusion | flops 2148532224 | bytes 6291456 | tf_op jit(solution)/shard_map/dot_general | solution.py:196
  104.1 5.0 %all-to-all-start.3 = ((bf16[16,64,1024]{2,1,0:T(8,128)(2,1)}), bf16[16,64,1024]{2,1,0:T(8,128)(2,1)S(1)}, u32[]{:S(2)}, u32[]{:S(2)}) async-start(bf16[16,64,1024]{2,1,0:T(8,128)(2,1)} %bitcast.20), calls=%async_computation.3 | async-start | bytes 4194304 | tf_op jit(solution)/shard_map/all_to_all | solution.py:197
  109.1 4.3 %fusion.16 = (bf16[512,1024]{1,0:T(8,128)(2,1)S(1)}, f32[512,1024]{1,0:T(8,128)}) fusion(f32[512,1024]{1,0:T(8,128)} %collective-permute-done.9, f32[1024,1024]{1,0:T(8,128)} %copy-done), kind=kLoop, calls=%fused_computation.72 | loop fusion | flops 1048576 | bytes 7340032 | tf_op jit(solution)/shard_map/convert_element_type | solution.py:202
  114.1 2.6 %collective-permute-start.16 = (bf16[64,1024]{1,0:T(8,128)(2,1)S(1)}, bf16[64,1024]{1,0:T(8,128)(2,1)S(1)}, u32[]{:S(2)}, u32[]{:S(2)}) collective-permute-start(bf16[64,1024]{1,0:T(8,128)(2,1)S(1)} %get-tuple-element.20), channel_id=1, source_target_pairs={{0,7},{1,0},{2,1},{3,2},{4,3},{5,4},{6,5},{7,6},{8,15},{9,8},{10,9... | collective-permute-start | bytes 393224 | tf_op jit(solution)/shard_map/ppermute | solution.py:18
  116.7 24.9 %all-to-all-done.3 = bf16[16,64,1024]{2,1,0:T(8,128)(2,1)S(1)} async-done(((bf16[16,64,1024]{2,1,0:T(8,128)(2,1)}), bf16[16,64,1024]{2,1,0:T(8,128)(2,1)S(1)}, u32[]{:S(2)}, u32[]{:S(2)}) %all-to-all-start.3) | async-done | bytes 2097184 | tf_op jit(solution)/shard_map/all_to_all | solution.py:197
  143.7 1.8 %collective-permute-start.13 = (bf16[64,1024]{1,0:T(8,128)(2,1)S(1)}, bf16[64,1024]{1,0:T(8,128)(2,1)S(1)}, u32[]{:S(2)}, u32[]{:S(2)}) collective-permute-start(bf16[64,1024]{1,0:T(8,128)(2,1)S(1)} %get-tuple-element.23), channel_id=1, source_target_pairs={{0,2},{1,3},{2,4},{3,5},{4,6},{5,7},{6,0},{7,1},{8,10},{9,11},{10,... | collective-permute-start | bytes 393224 | tf_op jit(solution)/shard_map/ppermute | solution.py:18
  145.5 2.1 %collective-permute-start.12 = (bf16[64,1024]{1,0:T(8,128)(2,1)S(1)}, bf16[64,1024]{1,0:T(8,128)(2,1)S(1)}, u32[]{:S(2)}, u32[]{:S(2)}) collective-permute-start(bf16[64,1024]{1,0:T(8,128)(2,1)S(1)} %get-tuple-element.24), channel_id=1, source_target_pairs={{0,5},{1,6},{2,7},{3,0},{4,1},{5,2},{6,3},{7,4},{8,13},{9,14},{10,... | collective-permute-start | bytes 393224 | tf_op jit(solution)/shard_map/ppermute | solution.py:18
  147.7 1.7 %collective-permute-start.11 = (bf16[64,1024]{1,0:T(8,128)(2,1)S(1)}, bf16[64,1024]{1,0:T(8,128)(2,1)S(1)}, u32[]{:S(2)}, u32[]{:S(2)}) collective-permute-start(bf16[64,1024]{1,0:T(8,128)(2,1)S(1)} %get-tuple-element.25), channel_id=1, source_target_pairs={{0,3},{1,4},{2,5},{3,6},{4,7},{5,0},{6,1},{7,2},{8,11},{9,12},{10,... | collective-permute-start | bytes 393224 | tf_op jit(solution)/shard_map/ppermute | solution.py:18
  153.0 1.5 collective-permute-done.13
  154.5 4.8 %collective-permute-done.12 = bf16[64,1024]{1,0:T(8,128)(2,1)S(1)} collective-permute-done((bf16[64,1024]{1,0:T(8,128)(2,1)S(1)}, bf16[64,1024]{1,0:T(8,128)(2,1)S(1)}, u32[]{:S(2)}, u32[]{:S(2)}) %collective-permute-start.12) | collective-permute-done | bytes 131104 | tf_op jit(solution)/shard_map/ppermute | solution.py:18
  159.3 1.8 %collective-permute-done.11 = bf16[64,1024]{1,0:T(8,128)(2,1)S(1)} collective-permute-done((bf16[64,1024]{1,0:T(8,128)(2,1)S(1)}, bf16[64,1024]{1,0:T(8,128)(2,1)S(1)}, u32[]{:S(2)}, u32[]{:S(2)}) %collective-permute-start.11) | collective-permute-done | bytes 131104 | tf_op jit(solution)/shard_map/ppermute | solution.py:18
  161.1 1.8 %fusion.6 = f32[64,1024]{1,0:T(8,128)} fusion(f32[512,1024]{1,0:T(8,128)} %get-tuple-element.14, bf16[64,1024]{1,0:T(8,128)(2,1)S(1)} %collective-permute-done.16, bf16[64,1024]{1,0:T(8,128)(2,1)S(1)} %collective-permute-done.15, bf16[64,1024]{1,0:T(8,128)(2,1)S(1)} %collective-permute-done.14, bf16[64,1024]{1,0:T(8,128)(2,1)S(1)} %collective-permute-done.13, ...), kind=kLoop, calls=%fused_computation.12 | loop fusion | flops 983040 | bytes 1441792 | tf_op jit(solution)/shard_map/mul | solution.py:206
  (81 shorter events, 23.4 us)
Async XLA Ops:
  0.6 38.6 %collective-permute-start.5 = (bf16[64,1024]{1,0:T(8,128)(2,1)}, bf16[64,1024]{1,0:T(8,128)(2,1)S(1)}, u32[]{:S(2)}, u32[]{:S(2)}) collective-permute-start(bf16[64,1024]{1,0:T(8,128)(2,1)} %param.6), channel_id=1, source_target_pairs={{0,2},{1,3},{2,4},{3,5},{4,6},{5,7},{6,0},{7,1},{8,10},{9,11},{10,... | collective-permute-start | bytes 393224 | tf_op jit(solution)/shard_map/ppermute | solution.py:18
  4.0 34.5 %collective-permute-start.4 = (bf16[64,1024]{1,0:T(8,128)(2,1)}, bf16[64,1024]{1,0:T(8,128)(2,1)S(1)}, u32[]{:S(2)}, u32[]{:S(2)}) collective-permute-start(bf16[64,1024]{1,0:T(8,128)(2,1)} %param.6), channel_id=1, source_target_pairs={{0,3},{1,4},{2,5},{3,6},{4,7},{5,0},{6,1},{7,2},{8,11},{9,12},{10,... | collective-permute-start | bytes 393224 | tf_op jit(solution)/shard_map/ppermute | solution.py:18
  8.9 28.9 %collective-permute-start.3 = (bf16[64,1024]{1,0:T(8,128)(2,1)}, bf16[64,1024]{1,0:T(8,128)(2,1)S(1)}, u32[]{:S(2)}, u32[]{:S(2)}) collective-permute-start(bf16[64,1024]{1,0:T(8,128)(2,1)} %param.6), channel_id=1, source_target_pairs={{0,4},{1,5},{2,6},{3,7},{4,0},{5,1},{6,2},{7,3},{8,12},{9,13},{10,... | collective-permute-start | bytes 393224 | tf_op jit(solution)/shard_map/ppermute | solution.py:18
  9.9 19.7 %collective-permute-start.1 = (bf16[64,1024]{1,0:T(8,128)(2,1)}, bf16[64,1024]{1,0:T(8,128)(2,1)S(1)}, u32[]{:S(2)}, u32[]{:S(2)}) collective-permute-start(bf16[64,1024]{1,0:T(8,128)(2,1)} %param.6), channel_id=1, source_target_pairs={{0,6},{1,7},{2,0},{3,1},{4,2},{5,3},{6,4},{7,5},{8,14},{9,15},{10,... | collective-permute-start | bytes 393224 | tf_op jit(solution)/shard_map/ppermute | solution.py:18
  14.0 12.3 %collective-permute-start = (bf16[64,1024]{1,0:T(8,128)(2,1)}, bf16[64,1024]{1,0:T(8,128)(2,1)S(1)}, u32[]{:S(2)}, u32[]{:S(2)}) collective-permute-start(bf16[64,1024]{1,0:T(8,128)(2,1)} %param.6), channel_id=1, source_target_pairs={{0,7},{1,0},{2,1},{3,2},{4,3},{5,4},{6,5},{7,6},{8,15},{9,8},{10,9... | collective-permute-start | bytes 393224 | tf_op jit(solution)/shard_map/ppermute | solution.py:18
  17.5 7.9 %copy-start.5 = (bf16[64,1024]{1,0:T(8,128)(2,1)S(1)}, bf16[64,1024]{1,0:T(8,128)(2,1)}, u32[]{:S(2)}) copy-start(bf16[64,1024]{1,0:T(8,128)(2,1)} %param.6) | copy-start | bytes 393220
  17.5 34.4 %all-to-all-start = ((bf16[16,64,1024]{2,1,0:T(8,128)(2,1)}), bf16[16,64,1024]{2,1,0:T(8,128)(2,1)S(1)}, u32[]{:S(2)}, u32[]{:S(2)}) async-start(bf16[16,64,1024]{2,1,0:T(8,128)(2,1)} %broadcast_in_dim.12), calls=%async_computation | async-start | bytes 4194304 | tf_op jit(solution)/shard_map/all_to_all | solution.py:29
  25.0 16.5 %copy-start.6 = (s32[16384]{0:T(1024)S(1)}, s32[16384]{0:T(1024)}, u32[]{:S(2)}) copy-start(s32[16384]{0:T(1024)} %param.7) | copy-start | bytes 196612
  26.2 10.8 %collective-permute-start.2 = (bf16[64,1024]{1,0:T(8,128)(2,1)S(1)}, bf16[64,1024]{1,0:T(8,128)(2,1)S(1)}, u32[]{:S(2)}, u32[]{:S(2)}) collective-permute-start(bf16[64,1024]{1,0:T(8,128)(2,1)S(1)} %copy-done.5), channel_id=1, source_target_pairs={{0,5},{1,6},{2,7},{3,0},{4,1},{5,2},{6,3},{7,4},{8,13},{9,14},{10,... | collective-permute-start | bytes 393224 | tf_op jit(solution)/shard_map/ppermute | solution.py:18
  29.6 10.4 %collective-permute-start.6 = (bf16[64,1024]{1,0:T(8,128)(2,1)S(1)}, bf16[64,1024]{1,0:T(8,128)(2,1)S(1)}, u32[]{:S(2)}, u32[]{:S(2)}) collective-permute-start(bf16[64,1024]{1,0:T(8,128)(2,1)S(1)} %copy-done.5), channel_id=1, source_target_pairs={{0,1},{1,2},{2,3},{3,4},{4,5},{5,6},{6,7},{7,0},{8,9},{9,10},{10,1... | collective-permute-start | bytes 393224 | tf_op jit(solution)/shard_map/ppermute | solution.py:18
  40.7 3.0 %collective-permute-start.7 = (bf16[512,1024]{1,0:T(8,128)(2,1)}, bf16[512,1024]{1,0:T(8,128)(2,1)}, u32[]{:S(2)}, u32[]{:S(2)}) collective-permute-start(bf16[512,1024]{1,0:T(8,128)(2,1)} %get-tuple-element.26), channel_id=1, source_target_pairs={{0,32},{32,0},{1,33},{33,1},{2,34},{34,2},{3,35},{35,3},{4,36},{36... | collective-permute-start | bytes 3145736 | tf_op jit(solution)/shard_map/ppermute | solution.py:18
  51.9 1.6 copy-start.1
  58.8 2.0 %copy-start.3 = (f32[1024,1024]{1,0:T(8,128)}, f32[1024,1024]{1,0:T(8,128)S(1)}, u32[]{:S(2)}) copy-start(f32[1024,1024]{1,0:T(8,128)S(1)} %get-tuple-element.8.kept_ref) | copy-start | bytes 12582916
  60.9 7.5 %collective-permute-start.8 = (f32[2,8,64]{2,1,0:T(8,128)S(1)}, f32[2,8,64]{2,1,0:T(8,128)S(1)}, u32[]{:S(2)}, u32[]{:S(2)}) collective-permute-start(f32[2,8,64]{2,1,0:T(8,128)S(1)} %rev.4), channel_id=1, source_target_pairs={{0,32},{32,0},{1,33},{33,1},{2,34},{34,2},{3,35},{35,3},{4,36},{36... | collective-permute-start | bytes 12296 | tf_op jit(solution)/shard_map/ppermute | solution.py:18
  62.8 11.9 %all-to-all-start.1 = ((f32[16,1,1024]{2,1,0:T(1,128)}), f32[16,1,1024]{2,1,0:T(1,128)S(1)}, u32[]{:S(2)}, u32[]{:S(2)}) async-start(f32[16,1,1024]{2,1,0:T(1,128)} %broadcast_in_dim.16), calls=%async_computation.1 | async-start | bytes 131072 | tf_op jit(solution)/shard_map/all_to_all | solution.py:29
  74.7 12.3 %all-to-all-start.2 = ((f32[8,1,2048]{2,1,0:T(1,128)}), f32[8,1,2048]{2,1,0:T(1,128)S(1)}, u32[]{:S(2)}, u32[]{:S(2)}) async-start(f32[8,1,2048]{2,1,0:T(1,128)} %reshape.242), calls=%async_computation.2 | async-start | bytes 131072 | tf_op jit(solution)/shard_map/all_to_all | solution.py:188
  88.6 2.2 %copy-start.4 = (f32[1024,1024]{1,0:T(8,128)S(1)}, f32[1024,1024]{1,0:T(8,128)}, u32[]{:S(2)}) copy-start(f32[1024,1024]{1,0:T(8,128)} %copy-done.3) | copy-start | bytes 12582916
  97.2 2.8 %copy-start = (f32[1024,1024]{1,0:T(8,128)}, f32[1024,1024]{1,0:T(8,128)S(1)}, u32[]{:S(2)}) copy-start(f32[1024,1024]{1,0:T(8,128)S(1)} %get-tuple-element.12) | copy-start | bytes 12582916
  97.3 3.1 %copy-start.2 = (bf16[1024,1024]{1,0:T(8,128)(2,1)S(1)}, bf16[1024,1024]{1,0:T(8,128)(2,1)}, u32[]{:S(2)}) copy-start(bf16[1024,1024]{1,0:T(8,128)(2,1)} %constant_dynamic-update-slice_fusion.8.cols_ref) | copy-start | bytes 6291460
  100.0 9.1 %collective-permute-start.9 = (f32[512,1024]{1,0:T(8,128)}, f32[512,1024]{1,0:T(8,128)}, u32[]{:S(2)}, u32[]{:S(2)}) collective-permute-start(f32[512,1024]{1,0:T(8,128)} %slice.47), channel_id=1, source_target_pairs={{0,32},{32,0},{1,33},{33,1},{2,34},{34,2},{3,35},{35,3},{4,36},{36... | collective-permute-start | bytes 6291464 | tf_op jit(solution)/shard_map/ppermute | solution.py:18
  104.1 37.5 %all-to-all-start.3 = ((bf16[16,64,1024]{2,1,0:T(8,128)(2,1)}), bf16[16,64,1024]{2,1,0:T(8,128)(2,1)S(1)}, u32[]{:S(2)}, u32[]{:S(2)}) async-start(bf16[16,64,1024]{2,1,0:T(8,128)(2,1)} %bitcast.20), calls=%async_computation.3 | async-start | bytes 4194304 | tf_op jit(solution)/shard_map/all_to_all | solution.py:197
  113.5 32.0 %collective-permute-start.10 = (bf16[64,1024]{1,0:T(8,128)(2,1)S(1)}, bf16[64,1024]{1,0:T(8,128)(2,1)S(1)}, u32[]{:S(2)}, u32[]{:S(2)}) collective-permute-start(bf16[64,1024]{1,0:T(8,128)(2,1)S(1)} %get-tuple-element.19), channel_id=1, source_target_pairs={{0,4},{1,5},{2,6},{3,7},{4,0},{5,1},{6,2},{7,3},{8,12},{9,13},{10,... | collective-permute-start | bytes 393224 | tf_op jit(solution)/shard_map/ppermute | solution.py:18
  114.1 33.6 %collective-permute-start.16 = (bf16[64,1024]{1,0:T(8,128)(2,1)S(1)}, bf16[64,1024]{1,0:T(8,128)(2,1)S(1)}, u32[]{:S(2)}, u32[]{:S(2)}) collective-permute-start(bf16[64,1024]{1,0:T(8,128)(2,1)S(1)} %get-tuple-element.20), channel_id=1, source_target_pairs={{0,7},{1,0},{2,1},{3,2},{4,3},{5,4},{6,5},{7,6},{8,15},{9,8},{10,9... | collective-permute-start | bytes 393224 | tf_op jit(solution)/shard_map/ppermute | solution.py:18
  142.0 9.5 %collective-permute-start.15 = (bf16[64,1024]{1,0:T(8,128)(2,1)S(1)}, bf16[64,1024]{1,0:T(8,128)(2,1)S(1)}, u32[]{:S(2)}, u32[]{:S(2)}) collective-permute-start(bf16[64,1024]{1,0:T(8,128)(2,1)S(1)} %get-tuple-element.21), channel_id=1, source_target_pairs={{0,1},{1,2},{2,3},{3,4},{4,5},{5,6},{6,7},{7,0},{8,9},{9,10},{10,1... | collective-permute-start | bytes 393224 | tf_op jit(solution)/shard_map/ppermute | solution.py:18
  142.6 10.4 %collective-permute-start.14 = (bf16[64,1024]{1,0:T(8,128)(2,1)S(1)}, bf16[64,1024]{1,0:T(8,128)(2,1)S(1)}, u32[]{:S(2)}, u32[]{:S(2)}) collective-permute-start(bf16[64,1024]{1,0:T(8,128)(2,1)S(1)} %get-tuple-element.22), channel_id=1, source_target_pairs={{0,6},{1,7},{2,0},{3,1},{4,2},{5,3},{6,4},{7,5},{8,14},{9,15},{10,... | collective-permute-start | bytes 393224 | tf_op jit(solution)/shard_map/ppermute | solution.py:18
  143.7 10.8 %collective-permute-start.13 = (bf16[64,1024]{1,0:T(8,128)(2,1)S(1)}, bf16[64,1024]{1,0:T(8,128)(2,1)S(1)}, u32[]{:S(2)}, u32[]{:S(2)}) collective-permute-start(bf16[64,1024]{1,0:T(8,128)(2,1)S(1)} %get-tuple-element.23), channel_id=1, source_target_pairs={{0,2},{1,3},{2,4},{3,5},{4,6},{5,7},{6,0},{7,1},{8,10},{9,11},{10,... | collective-permute-start | bytes 393224 | tf_op jit(solution)/shard_map/ppermute | solution.py:18
  145.5 13.8 %collective-permute-start.12 = (bf16[64,1024]{1,0:T(8,128)(2,1)S(1)}, bf16[64,1024]{1,0:T(8,128)(2,1)S(1)}, u32[]{:S(2)}, u32[]{:S(2)}) collective-permute-start(bf16[64,1024]{1,0:T(8,128)(2,1)S(1)} %get-tuple-element.24), channel_id=1, source_target_pairs={{0,5},{1,6},{2,7},{3,0},{4,1},{5,2},{6,3},{7,4},{8,13},{9,14},{10,... | collective-permute-start | bytes 393224 | tf_op jit(solution)/shard_map/ppermute | solution.py:18
  147.7 13.4 %collective-permute-start.11 = (bf16[64,1024]{1,0:T(8,128)(2,1)S(1)}, bf16[64,1024]{1,0:T(8,128)(2,1)S(1)}, u32[]{:S(2)}, u32[]{:S(2)}) collective-permute-start(bf16[64,1024]{1,0:T(8,128)(2,1)S(1)} %get-tuple-element.25), channel_id=1, source_target_pairs={{0,3},{1,4},{2,5},{3,6},{4,7},{5,0},{6,1},{7,2},{8,11},{9,12},{10,... | collective-permute-start | bytes 393224 | tf_op jit(solution)/shard_map/ppermute | solution.py:18

commit v2 on v1

v2 whole, which is shorter than its diff:
```python
import jax
import jax.numpy as jnp
from jax import lax
from jax.experimental import pallas as pl
from jax.experimental.pallas import tpu as pltpu
from jax.sharding import Mesh, PartitionSpec as P

logit_scale = 100.0
floor_value = -1e30
mib = 1024 * 1024
lanes = 128
block = 256

axes = ("y", "core", "x", "z")
plane = ("y", "x")
pair_line = ("core", "z")


def swap_core(values):
    return lax.ppermute(values, "core", [(0, 1), (1, 0)])


def shift_z(values, step):
    size = lax.axis_size("z")
    return lax.ppermute(values, "z", [(i, (i + step) % size) for i in range(size)])


def z_steps(size):
    steps = [size // 2]
    for step in range(size // 2 - 1, 0, -1):
        steps += [step, size - step]
    return steps


def spread(values, axis, count):
    return lax.all_to_all(jnp.broadcast_to(values[None], (count,) + values.shape), axis, 0, 0)


def contract(a, b, dim_a, dim_b):
    return lax.dot_general(a, b, (((dim_a,), (dim_b,)), ((), ())), preferred_element_type=jnp.float32)


def as_column(row):
    return jnp.broadcast_to(row, (lanes, row.shape[1])).T[:, 0:1]


def as_row(column):
    return jnp.broadcast_to(column, (column.shape[0], lanes)).T[0:1, :]


def fold(row):
    return jnp.concatenate([row[:, i : i + lanes] for i in range(0, row.shape[1], lanes)], axis=0)


def unfold(tile):
    return jnp.concatenate([tile[i : i + 1, :] for i in range(tile.shape[0])], axis=1)


def by_core(tile, core):
    half = tile.shape[0] // 2
    return jnp.where(core == 0, tile, jnp.concatenate([tile[half:], tile[:half]], axis=0))


def stats_kernel(core, rows_ref, near_ref, far_ref, ri, rg, ci, cg, kept_ref, row_ref, col_ref, peak, total):
    step = pl.program_id(0)
    half = near_ref.shape[0]
    for side, ref in enumerate((near_ref, far_ref)):
        span = slice(side * half, (side + 1) * half)
        scores = logit_scale * contract(rows_ref[...], ref[...], 1, 1)
        valid = jnp.logical_or(rg[...] != cg[:, span], ri[...] == ci[:, span])
        kept_ref[:, span] = jnp.where(valid, scores, floor_value)
    kept = kept_ref[...]

    row_peak = jnp.max(kept, axis=1, keepdims=True)
    row_total = jnp.sum(jnp.exp(kept - row_peak), axis=1, keepdims=True)
    row_lse = as_row(row_peak + jnp.log(row_total))
    for i in range(block // lanes):
        piece = row_lse[:, i * lanes : (i + 1) * lanes]
        row_ref[:, pl.ds(step * (block // lanes) + i, 1), :] = jnp.broadcast_to(
            piece[None], (row_ref.shape[0], 1, lanes)
        )

    @pl.when(step == 0)
    def _():
        peak[...] = jnp.full_like(peak, floor_value)
        total[...] = jnp.zeros_like(total)

    old = peak[...]
    top = jnp.maximum(old, jnp.max(kept, axis=0, keepdims=True))
    summed = total[...] * jnp.exp(old - top) + jnp.sum(jnp.exp(kept - top), axis=0, keepdims=True)
    peak[...] = top
    total[...] = summed

    @pl.when(step == pl.num_programs(0) - 1)
    def _():
        col_lse = by_core(fold(top + jnp.log(summed)), core[0])
        col_ref[...] = jnp.broadcast_to(col_lse[None], col_ref.shape)


def whole(shape):
    return pl.BlockSpec(shape, lambda i: (0,) * len(shape))


def by_rows(width):
    return pl.BlockSpec((block, width), lambda i: (i, 0))


def block_stats(core, rows, near, far, ri, rg, ci, cg, n_row, n_col):
    n_rows, width = rows.shape
    n_cols = 2 * near.shape[0]
    return pl.pallas_call(
        stats_kernel,
        grid=(n_rows // block,),
        in_specs=[
            pl.BlockSpec(memory_space=pltpu.SMEM),
            by_rows(width),
            whole(near.shape),
            whole(far.shape),
            by_rows(1),
            by_rows(1),
            whole((1, n_cols)),
            whole((1, n_cols)),
        ],
        out_specs=[
            by_rows(n_cols),
            whole((n_row, n_rows // lanes, lanes)),
            whole((n_col, n_cols // lanes, lanes)),
        ],
        out_shape=[
            jax.ShapeDtypeStruct((n_rows, n_cols), jnp.float32),
            jax.ShapeDtypeStruct((n_row, n_rows // lanes, lanes), jnp.float32),
            jax.ShapeDtypeStruct((n_col, n_cols // lanes, lanes), jnp.float32),
        ],
        scratch_shapes=[pltpu.VMEM((1, n_cols), jnp.float32), pltpu.VMEM((1, n_cols), jnp.float32)],
        compiler_params=pltpu.CompilerParams(vmem_limit_bytes=20 * mib),
        cost_estimate=pl.CostEstimate(
            flops=2 * n_rows * n_cols * width, bytes_accessed=8 * mib, transcendentals=2 * n_rows * n_cols
        ),
        name="stats",
    )(core, rows, near, far, ri, rg, ci, cg)


def merge(parts):
    top = jnp.max(parts, axis=0)
    return top + jnp.log(jnp.sum(jnp.exp(parts - top[None]), axis=0))


def grad_kernel(core, kept_ref, near_ref, far_ref, row_parts, col_parts, ri, ci, grad_ref, image_ref):
    step = pl.program_id(0)
    half = near_ref.shape[0]
    per = block // lanes
    row_lse = as_column(unfold(merge(row_parts[:, pl.ds(step * per, per), :])))
    col_lse = unfold(by_core(merge(col_parts[...]), core[0]))
    kept = kept_ref[...]
    weight = jnp.exp(kept - row_lse) + jnp.exp(kept - col_lse)
    grad = 0.5 * weight - jnp.where(ri[...] == ci[...], 1.0, 0.0)
    grad = grad.astype(jnp.bfloat16)
    grad_ref[...] = grad
    part = contract(grad[:, :half], near_ref[...], 1, 0) + contract(grad[:, half:], far_ref[...], 1, 0)
    image_ref[...] = part.astype(jnp.bfloat16)


def block_grad(core, kept, near, far, row_parts, col_parts, ri, ci):
    n_rows, n_cols = kept.shape
    width = near.shape[1]
    return pl.pallas_call(
        grad_kernel,
        grid=(n_rows // block,),
        in_specs=[
            pl.BlockSpec(memory_space=pltpu.SMEM),
            by_rows(n_cols),
            whole(near.shape),
            whole(far.shape),
            whole(row_parts.shape),
            whole(col_parts.shape),
            by_rows(1),
            whole((1, n_cols)),
        ],
        out_specs=[by_rows(n_cols), by_rows(width)],
        out_shape=[
            jax.ShapeDtypeStruct((n_rows, n_cols), jnp.bfloat16),
            jax.ShapeDtypeStruct((n_rows, width), jnp.bfloat16),
        ],
        compiler_params=pltpu.CompilerParams(vmem_limit_bytes=20 * mib),
        cost_estimate=pl.CostEstimate(
            flops=2 * n_rows * n_cols * width, bytes_accessed=10 * mib, transcendentals=2 * n_rows * n_cols
        ),
        name="grad",
    )(core, kept, near, far, row_parts, col_parts, ri, ci)


def far_kernel(grad_ref, rows_ref, out_ref):
    out_ref[...] = contract(grad_ref[...], rows_ref[...], 0, 0)


def far_terms(grad, rows):
    n_rows, width = rows.shape
    n_cols = grad.shape[1] // 2
    skip = n_cols // block
    return pl.pallas_call(
        far_kernel,
        grid=(n_cols // block,),
        in_specs=[pl.BlockSpec((n_rows, block), lambda i: (0, i + skip)), whole(rows.shape)],
        out_specs=by_rows(width),
        out_shape=jax.ShapeDtypeStruct((n_cols, width), jnp.float32),
        compiler_params=pltpu.CompilerParams(vmem_limit_bytes=20 * mib),
        cost_estimate=pl.CostEstimate(
            flops=2 * n_rows * n_cols * width, bytes_accessed=5 * mib, transcendentals=0
        ),
        name="far_terms",
    )(grad, rows)


def text_kernel(z, grad_ref, rows_ref, other_ref, own_ref, *outs):
    sent, total = outs[:-1], outs[-1]
    span = own_ref.shape[0]
    n_z = len(sent) + 1
    step = pl.program_id(0)
    total[pl.ds(step * block, block), :] = contract(grad_ref[...], rows_ref[...], 0, 0) + other_ref[...]

    @pl.when(step == pl.num_programs(0) - 1)
    def _():
        for k in range(n_z):
            at = pl.multiple_of(lax.rem(z[0] + k, n_z) * span, span)
            value = total[pl.ds(at, span), :]
            if k == 0:
                own_ref[...] = value
            else:
                sent[k - 1][...] = value.astype(jnp.bfloat16)


def text_terms(z, grad, rows, other, n_z):
    n_rows, width = rows.shape
    n_cols = grad.shape[1] // 2
    span = n_cols // n_z
    return pl.pallas_call(
        text_kernel,
        grid=(n_cols // block,),
        in_specs=[
            pl.BlockSpec(memory_space=pltpu.SMEM),
            pl.BlockSpec((n_rows, block), lambda i: (0, i)),
            whole(rows.shape),
            by_rows(width),
        ],
        out_specs=[whole((span, width))] * n_z,
        out_shape=[jax.ShapeDtypeStruct((span, width), jnp.float32)]
        + [jax.ShapeDtypeStruct((span, width), jnp.bfloat16)] * (n_z - 1),
        scratch_shapes=[pltpu.VMEM((n_cols, width), jnp.float32)],
        compiler_params=pltpu.CompilerParams(vmem_limit_bytes=20 * mib),
        cost_estimate=pl.CostEstimate(
            flops=2 * n_rows * n_cols * width, bytes_accessed=6 * mib, transcendentals=0
        ),
        name="text_terms",
    )(z, grad, rows, other)


def sum_kernel(image_parts, own_ref, *refs):
    text_parts, (image_ref, text_ref) = refs[:-2], refs[-2:]
    image_ref[...] = logit_scale * jnp.sum(image_parts[...].astype(jnp.float32), axis=0)
    total = own_ref[...]
    for ref in text_parts:
        total = total + ref[...].astype(jnp.float32)
    text_ref[...] = logit_scale * total


def final_sums(image_parts, own, text_parts):
    n_plane, span, width = image_parts.shape
    tall = 16
    rows = pl.BlockSpec((tall, width), lambda i: (i, 0))
    return pl.pallas_call(
        sum_kernel,
        grid=(span // tall,),
        in_specs=[pl.BlockSpec((n_plane, tall, width), lambda i: (0, i, 0))] + [rows] * (1 + len(text_parts)),
        out_specs=[rows, rows],
        out_shape=[jax.ShapeDtypeStruct((span, width), jnp.float32)] * 2,
        compiler_params=pltpu.CompilerParams(vmem_limit_bytes=20 * mib),
        cost_estimate=pl.CostEstimate(flops=span * width * 24, bytes_accessed=4 * mib, transcendentals=0),
        name="sums",
    )(image_parts, own, *text_parts)


def join_kernel(z, *refs):
    shards, out_ref = refs[:-1], refs[-1]
    span = shards[0].shape[0]
    for k, ref in enumerate(shards):
        at = pl.multiple_of(lax.rem(z[0] + k, len(shards)) * span, span)
        out_ref[pl.ds(at, span), :] = ref[...]


def join(z, shards):
    span, width = shards[0].shape
    memory = pl.BlockSpec(memory_space=pltpu.VMEM)
    return pl.pallas_call(
        join_kernel,
        in_specs=[pl.BlockSpec(memory_space=pltpu.SMEM)] + [memory] * len(shards),
        out_specs=memory,
        out_shape=jax.ShapeDtypeStruct((len(shards) * span, width), shards[0].dtype),
        compiler_params=pltpu.CompilerParams(vmem_limit_bytes=8 * mib),
        cost_estimate=pl.CostEstimate(flops=0, bytes_accessed=2 * mib, transcendentals=0),
        name="join",
    )(z, *shards)


def per_device(image_emb, text_emb, caption_group):
    span, width = image_emb.shape
    n_y, n_core, n_x, n_z = (lax.axis_size(a) for a in axes)
    y, core, x, z = (lax.axis_index(a) for a in axes)
    n_plane = n_y * n_x
    place = jnp.arange(span, dtype=jnp.int32)
    z_scalar = z.reshape(1).astype(jnp.int32)
    core_scalar = core.reshape(1).astype(jnp.int32)

    rows = spread(image_emb, plane, n_plane).reshape(n_plane * span, width)
    shards = {0: text_emb}
    for k in z_steps(n_z):
        shards[k] = shift_z(text_emb, -k)
    near = join(z_scalar, [shards[k] for k in range(n_z)])
    far = swap_core(near)

    at_y = jnp.arange(n_y, dtype=jnp.int32)[:, None, None]
    at_x = jnp.arange(n_x, dtype=jnp.int32)[None, :, None]
    row_index = ((((at_y * n_core + core) * n_x + at_x) * n_z + z) * span + place).reshape(-1)
    at_core = jnp.stack([core, 1 - core])[:, None, None]
    at_z = jnp.arange(n_z, dtype=jnp.int32)[None, :, None]
    col_index = ((((x * n_z + at_z) * n_y + y) * n_core + at_core) * span + place).reshape(-1)
    blocks = caption_group.reshape(-1, span)
    row_group = jnp.take(blocks, row_index[::span] // span, axis=0).reshape(-1)
    col_group = jnp.take(blocks, col_index[::span] // span, axis=0).reshape(-1)
    ri, rg = row_index[:, None], row_group[:, None]
    ci, cg = col_index[None, :], col_group[None, :]

    kept, row_part, col_part = block_stats(
        core_scalar, rows, near, far, ri, rg, ci, cg, n_plane, n_z * n_core
    )
    row_parts = lax.all_to_all(row_part, plane, 0, 0)
    col_parts = lax.all_to_all(col_part, pair_line, 0, 0)

    grad, image_part = block_grad(core_scalar, kept, near, far, row_parts, col_parts, ri, ci)
    image_parts = lax.all_to_all(image_part.reshape(n_plane, span, width), plane, 0, 0)
    other = swap_core(far_terms(grad, rows))
    own, *sent = text_terms(z_scalar, grad, rows, other, n_z)
    text_parts = {k: shift_z(sent[k - 1], k) for k in z_steps(n_z)}
    image_grad, text_grad = final_sums(image_parts, own, [text_parts[k] for k in range(1, n_z)])
    return (image_grad, text_grad)


def solution(mesh):
    fine = Mesh(mesh.devices.reshape(4, 2, 4, 8), axes)
    return jax.shard_map(
        per_device,
        mesh=fine,
        in_specs=(P(axes, None), P(("x", "z", "y", "core"), None), P()),
        out_specs=(P(axes, None), P(("x", "z", "y", "core"), None)),
        check_vma=False,
    )
```

time: 165 us -> 139 us (0.84)
  waiting for transfers between devices: 61 us -> 27.7 us
  blocking collectives: 0 us -> 21.8 us
  Pallas kernels: 11.9 us -> 22.2 us
  other arithmetic: 9.34 us -> 0.57 us
  starting transfers between devices: 51.1 us -> 44.3 us
  local copies, waits for them, and re-layouts: 25 us -> 20.7 us
  matrix products: 3.75 us -> 0 us
    all_to_all x4 -> x2, waiting for transfers between devices: 44.6 us -> 21.7 us  [the longest x1 13 us: per_device(): lax.all_to_all(image_part.reshape(n_plane, span, width), plane, 0, 0)]
    all_to_all x0 -> x2, blocking collectives: none -> 21.8 us  [the longest x1 11.3 us: per_device(): row_parts = lax.all_to_all(row_part, plane, 0, 0)]
    ppermute x17 -> x16, waiting for transfers between devices: 16.4 us -> 6.05 us  [the longest x14 6.04 us: shift_z(): lax.ppermute(values, 'z', [(i, (i + step) % size) for i in range(size)])]
    pallas_call x0 -> x4, Pallas kernels: none -> 9.93 us  [the longest x1 3.62 us: text_terms(): pl.pallas_call(text_kernel, grid=(n_cols // block,), in_specs=[pl.BlockSp...]
    all_to_all x4 -> x2, starting transfers between devices: 22 us -> 13.2 us  [the longest x1 7.52 us: spread(): lax.all_to_all(jnp.broadcast_to(values[None], (count,) + values.shape), a...]
    convert_element_type x1 -> x0, other arithmetic: 4.32 us -> none  [per_device(): text_sent = text_part.astype(jnp.bfloat16)]
    dot_general x1 -> x0, matrix products: 3.75 us -> none  [per_device(): image_part = jnp.dot(grad, cols, preferred_element_type=jnp.float32)]
    concatenate x2 -> x0, local copies, waits for them, and re-layouts: 3.09 us -> none  [the longest x1 2.38 us: per_device(): cols = jnp.concatenate([near, far], axis=0)]
  transfers between devices with their start and end apart: 21 -> 18, of which waited for: 11 -> 8; matrix products, arithmetic and copies ran while one was open for 16% -> 7% of each run, Pallas kernels for 0% -> 3%
where the time goes in v2:
time: 139 us; the launch traced here: 138 us
  starting transfers between devices  44.3 us (32%)
  waiting for transfers between devices  27.7 us (20%)
  Pallas kernels  22.2 us (16%)
  blocking collectives  21.8 us (16%)
  local copies, waits for them, and re-layouts  20.7 us (15%)
    ppermute x14, starting transfers between devices, shift_z(): lax.ppermute(values, 'z', [(i, (i + step) % size) for i in range(size)])  31 us
    all_to_all x1, waiting for transfers between devices, per_device(): lax.all_to_all(image_part.reshape(n_plane, span, width), plane, 0, 0)  13 us
    unnamed x36, local copies, waits for them, and re-layouts  11.5 us
    all_to_all x1, blocking collectives, per_device(): row_parts = lax.all_to_all(row_part, plane, 0, 0)  11.3 us
    all_to_all x1, blocking collectives, per_device(): col_parts = lax.all_to_all(col_part, pair_line, 0, 0)  10.5 us
    all_to_all x1, waiting for transfers between devices, spread(): lax.all_to_all(jnp.broadcast_to(values[None], (count,) + values.shape), a...  8.72 us
    all_to_all x1, starting transfers between devices, spread(): lax.all_to_all(jnp.broadcast_to(values[None], (count,) + values.shape), a...  7.52 us
    pallas_call x1, Pallas kernels, block_stats(): pl.pallas_call(stats_kernel, grid=(n_rows // block,), in_specs=[pl.BlockS...  6.63 us
  transfers between devices with their start and end apart: 18, of which 8 were waited for; matrix products, arithmetic and copies ran while one was open for 7% of the time, Pallas kernels for 3%

profile of v2, /device:TPU:8, one launch (start us, length us, event | category | flops | bytes accessed | tf_op | source)
XLA Modules:
  0.0 138.2 jit_solution(365252724372374291)
XLA Ops:
  0.6 3.3 %collective-permute-start.5 = (bf16[64,1024]{1,0:T(8,128)(2,1)}, bf16[64,1024]{1,0:T(8,128)(2,1)S(1)}, u32[]{:S(2)}, u32[]{:S(2)}) collective-permute-start(bf16[64,1024]{1,0:T(8,128)(2,1)} %refs_0_.1), channel_id=1, source_target_pairs={{0,2},{1,3},{2,4},{3,5},{4,6},{5,7},{6,0},{7,1},{8,10},{9,11},{10,... | collective-permute-start | bytes 393224 | tf_op jit(solution)/shard_map/ppermute | solution.py:25
  4.0 4.9 %collective-permute-start.4 = (bf16[64,1024]{1,0:T(8,128)(2,1)}, bf16[64,1024]{1,0:T(8,128)(2,1)S(1)}, u32[]{:S(2)}, u32[]{:S(2)}) collective-permute-start(bf16[64,1024]{1,0:T(8,128)(2,1)} %refs_0_.1), channel_id=1, source_target_pairs={{0,3},{1,4},{2,5},{3,6},{4,7},{5,0},{6,1},{7,2},{8,11},{9,12},{10,... | collective-permute-start | bytes 393224 | tf_op jit(solution)/shard_map/ppermute | solution.py:25
  9.9 4.5 %collective-permute-start.2 = (bf16[64,1024]{1,0:T(8,128)(2,1)}, bf16[64,1024]{1,0:T(8,128)(2,1)S(1)}, u32[]{:S(2)}, u32[]{:S(2)}) collective-permute-start(bf16[64,1024]{1,0:T(8,128)(2,1)} %refs_0_.1), channel_id=1, source_target_pairs={{0,5},{1,6},{2,7},{3,0},{4,1},{5,2},{6,3},{7,4},{8,13},{9,14},{10,... | collective-permute-start | bytes 393224 | tf_op jit(solution)/shard_map/ppermute | solution.py:25
  14.4 2.7 %collective-permute-start.1 = (bf16[64,1024]{1,0:T(8,128)(2,1)}, bf16[64,1024]{1,0:T(8,128)(2,1)S(1)}, u32[]{:S(2)}, u32[]{:S(2)}) collective-permute-start(bf16[64,1024]{1,0:T(8,128)(2,1)} %refs_0_.1), channel_id=1, source_target_pairs={{0,6},{1,7},{2,0},{3,1},{4,2},{5,3},{6,4},{7,5},{8,14},{9,15},{10,... | collective-permute-start | bytes 393224 | tf_op jit(solution)/shard_map/ppermute | solution.py:25
  17.1 2.5 %broadcast_in_dim.8 = bf16[16,64,1024]{2,1,0:T(8,128)(2,1)} broadcast(bf16[64,1024]{1,0:T(8,128)(2,1)} %param.5), dimensions={1,2} | broadcast | bytes 2228224 | tf_op jit(solution)/shard_map/broadcast_in_dim | solution.py:36
  19.6 7.5 %all-to-all-start = ((bf16[16,64,1024]{2,1,0:T(8,128)(2,1)}), bf16[16,64,1024]{2,1,0:T(8,128)(2,1)S(1)}, u32[]{:S(2)}, u32[]{:S(2)}) async-start(bf16[16,64,1024]{2,1,0:T(8,128)(2,1)} %broadcast_in_dim.8), calls=%async_computation | async-start | bytes 4194304 | tf_op jit(solution)/shard_map/all_to_all | solution.py:36
  27.7 2.0 %collective-permute-start.6 = (bf16[64,1024]{1,0:T(8,128)(2,1)S(1)}, bf16[64,1024]{1,0:T(8,128)(2,1)S(1)}, u32[]{:S(2)}, u32[]{:S(2)}) collective-permute-start(bf16[64,1024]{1,0:T(8,128)(2,1)S(1)} %copy-done.6), channel_id=1, source_target_pairs={{0,1},{1,2},{2,3},{3,4},{4,5},{5,6},{6,7},{7,0},{8,9},{9,10},{10,1... | collective-permute-start | bytes 393224 | tf_op jit(solution)/shard_map/ppermute | solution.py:25
  29.8 1.3 add.166.ri
  40.8 1.5 %gather_fusion.1 = s32[16,64]{1,0:T(8,128)S(1)} fusion(s32[256,64]{1,0:T(8,128)} %reshape.165, s32[1024]{0:T(1024)S(1)} %pad_clamp_fusion), kind=kCustom, calls=%fused_computation.1.clone | custom fusion | bytes 8256 | tf_op jit(solution)/shard_map/jit(_take)/gather | solution.py:328
  42.3 1.5 %gather_fusion = s32[16,64]{1,0:T(8,128)S(1)} fusion(s32[256,64]{1,0:T(8,128)} %reshape.165, s32[1024]{0:T(1024)S(1)} %pad_clamp_fusion.1), kind=kCustom, calls=%fused_computation.clone | custom fusion | bytes 8256 | tf_op jit(solution)/shard_map/jit(_take)/gather | solution.py:327
  44.0 1.3 broadcast_in_dim_reshape.10.rg
  45.3 8.7 %all-to-all-done = bf16[16,64,1024]{2,1,0:T(8,128)(2,1)S(1)} async-done(((bf16[16,64,1024]{2,1,0:T(8,128)(2,1)}), bf16[16,64,1024]{2,1,0:T(8,128)(2,1)S(1)}, u32[]{:S(2)}, u32[]{:S(2)}) %all-to-all-start) | async-done | bytes 2097184 | tf_op jit(solution)/shard_map/all_to_all | solution.py:36
  54.0 1.0 copy-done.3
  55.1 1.0 copy-done.5
  56.1 6.6 %stats.1 = (f32[1024,1024]{1,0:T(8,128)S(1)}, f32[16,8,128]{2,1,0:T(8,128)S(1)}, f32[16,8,128]{2,1,0:T(8,128)S(1)}) custom-call(s32[1]{0:T(128)} %bitcast.core, bf16[1024,1024]{1,0:T(8,128)(2,1)S(1)} %bitcast.5, bf16[512,1024]{1,0:T(8,128)(2,1)S(1)} %join.1.near_ref, bf16[512,1024]{1,0:T(8,128)(2,1)} %collective-permute-done.7.far_ref, ...), custom_call_target="tpu_custom_call" | custom-call | flops 2147483648 | bytes 8388608 | tf_op jit(solution)/shard_map/stats/pallas_call | solution.py:111
  62.7 11.3 %all_to_all.20.row_parts = f32[16,8,128]{2,1,0:T(8,128)S(1)} all-to-all(f32[16,8,128]{2,1,0:T(8,128)S(1)} %get-tuple-element.17), channel_id=1, replica_groups=mesh['y'=4,'core'=2,'x'=4,'z'=8] {'y','x'}, dimensions={0} | all-to-all | bytes 131072 | tf_op jit(solution)/shard_map/all_to_all | solution.py:335
  74.1 10.5 %all_to_all.21.col_parts = f32[16,8,128]{2,1,0:T(8,128)S(1)} all-to-all(f32[16,8,128]{2,1,0:T(8,128)S(1)} %get-tuple-element.18), channel_id=1, replica_groups=mesh['y'=4,'core'=2,'x'=4,'z'=8] {'core','z'}, dimensions={0} | all-to-all | bytes 131072 | tf_op jit(solution)/shard_map/all_to_all | solution.py:336
  84.5 5.7 %grad.1 = (bf16[1024,1024]{1,0:T(8,128)(2,1)S(1)}, bf16[1024,1024]{1,0:T(8,128)(2,1)S(1)}) custom-call(s32[1]{0:T(128)} %bitcast.core, f32[1024,1024]{1,0:T(8,128)S(1)} %get-tuple-element.16.kept_ref, bf16[512,1024]{1,0:T(8,128)(2,1)S(1)} %join.1.near_ref, bf16[512,1024]{1,0:T(8,128)(2,1)} %collective-permute-done.7.far_ref, ...), custom_call_target="tpu_custom_call" | custom-call | flops 2147483648 | bytes 10485760 | tf_op jit(solution)/shard_map/grad/pallas_call | solution.py:166
  90.2 2.6 %far_terms.1 = f32[512,1024]{1,0:T(8,128)} custom-call(bf16[1024,1024]{1,0:T(8,128)(2,1)S(1)} %get-tuple-element.20.grad_ref, bf16[1024,1024]{1,0:T(8,128)(2,1)S(1)} %bitcast.6), custom_call_target="tpu_custom_call" | custom-call | flops 1073741824 | bytes 5242880 | tf_op jit(solution)/shard_map/far_terms/pallas_call | solution.py:200
  92.9 5.7 %all-to-all-start.3 = ((bf16[16,64,1024]{2,1,0:T(8,128)(2,1)}), bf16[16,64,1024]{2,1,0:T(8,128)(2,1)}, u32[]{:S(2)}, u32[]{:S(2)}) async-start(bf16[16,64,1024]{2,1,0:T(8,128)(2,1)} %bitcast.8), calls=%async_computation.3 | async-start | bytes 4194304 | tf_op jit(solution)/shard_map/all_to_all | solution.py:339
  98.6 1.6 %copy-done.1 = bf16[1024,1024]{1,0:T(8,128)(2,1)S(1)} copy-done((bf16[1024,1024]{1,0:T(8,128)(2,1)S(1)}, bf16[1024,1024]{1,0:T(8,128)(2,1)}, u32[]{:S(2)}) %copy-start.1) | copy-done | bytes 2097176
  100.2 3.6 %text_terms.1 = (f32[64,1024]{1,0:T(8,128)S(1)}, bf16[64,1024]{1,0:T(8,128)(2,1)S(1)}, bf16[64,1024]{1,0:T(8,128)(2,1)S(1)}, bf16[64,1024]{1,0:T(8,128)(2,1)}, b...) custom-call(s32[1]{0:T(128)} %bitcast.2.z, ...), custom_call_target="tpu_custom_call" | custom-call | flops 1073741824 | bytes 6291456 | tf_op jit(solution)/shard_map/text_terms/pallas_call | solution.py:236
  105.4 2.3 %collective-permute-start.11 = (bf16[64,1024]{1,0:T(8,128)(2,1)}, bf16[64,1024]{1,0:T(8,128)(2,1)S(1)}, u32[]{:S(2)}, u32[]{:S(2)}) collective-permute-start(bf16[64,1024]{1,0:T(8,128)(2,1)} %get-tuple-element.24), channel_id=1, source_target_pairs={{0,3},{1,4},{2,5},{3,6},{4,7},{5,0},{6,1},{7,2},{8,11},{9,12},{10,... | collective-permute-start | bytes 393224 | tf_op jit(solution)/shard_map/ppermute | solution.py:25
  107.8 3.5 %collective-permute-start.12 = (bf16[64,1024]{1,0:T(8,128)(2,1)}, bf16[64,1024]{1,0:T(8,128)(2,1)S(1)}, u32[]{:S(2)}, u32[]{:S(2)}) collective-permute-start(bf16[64,1024]{1,0:T(8,128)(2,1)} %get-tuple-element.25), channel_id=1, source_target_pairs={{0,4},{1,5},{2,6},{3,7},{4,0},{5,1},{6,2},{7,3},{8,12},{9,13},{10,... | collective-permute-start | bytes 393224 | tf_op jit(solution)/shard_map/ppermute | solution.py:25
  111.3 2.2 %collective-permute-start.13 = (bf16[64,1024]{1,0:T(8,128)(2,1)}, bf16[64,1024]{1,0:T(8,128)(2,1)S(1)}, u32[]{:S(2)}, u32[]{:S(2)}) collective-permute-start(bf16[64,1024]{1,0:T(8,128)(2,1)} %get-tuple-element.26), channel_id=1, source_target_pairs={{0,5},{1,6},{2,7},{3,0},{4,1},{5,2},{6,3},{7,4},{8,13},{9,14},{10,... | collective-permute-start | bytes 393224 | tf_op jit(solution)/shard_map/ppermute | solution.py:25
  113.8 1.7 %collective-permute-start.14 = (bf16[64,1024]{1,0:T(8,128)(2,1)S(1)}, bf16[64,1024]{1,0:T(8,128)(2,1)S(1)}, u32[]{:S(2)}, u32[]{:S(2)}) collective-permute-start(bf16[64,1024]{1,0:T(8,128)(2,1)S(1)} %get-tuple-element.27), channel_id=1, source_target_pairs={{0,6},{1,7},{2,0},{3,1},{4,2},{5,3},{6,4},{7,5},{8,14},{9,15},{10,... | collective-permute-start | bytes 393224 | tf_op jit(solution)/shard_map/ppermute | solution.py:25
  115.5 2.3 %collective-permute-done.10.refs_1_ = bf16[64,1024]{1,0:T(8,128)(2,1)S(1)} collective-permute-done((bf16[64,1024]{1,0:T(8,128)(2,1)S(1)}, bf16[64,1024]{1,0:T(8,128)(2,1)S(1)}, u32[]{:S(2)}, u32[]{:S(2)}) %collective-permute-start.10) | collective-permute-done | bytes 131104 | tf_op jit(solution)/shard_map/ppermute | solution.py:25
  117.8 1.1 collective-permute-start.15
  118.9 13.0 %all-to-all-done.3.image_parts = bf16[16,64,1024]{2,1,0:T(8,128)(2,1)} async-done(((bf16[16,64,1024]{2,1,0:T(8,128)(2,1)}), bf16[16,64,1024]{2,1,0:T(8,128)(2,1)}, u32[]{:S(2)}, u32[]{:S(2)}) %all-to-all-start.3) | async-done | bytes 2097184 | tf_op jit(solution)/shard_map/all_to_all | solution.py:339
  131.9 1.7 %collective-permute-done.14.refs_5_ = bf16[64,1024]{1,0:T(8,128)(2,1)S(1)} collective-permute-done((bf16[64,1024]{1,0:T(8,128)(2,1)S(1)}, bf16[64,1024]{1,0:T(8,128)(2,1)S(1)}, u32[]{:S(2)}, u32[]{:S(2)}) %collective-permute-start.14) | collective-permute-done | bytes 131104 | tf_op jit(solution)/shard_map/ppermute | solution.py:25
  133.5 1.0 collective-permute-done.15.refs_6_
  134.6 3.6 %sums.1 = (f32[64,1024]{1,0:T(8,128)}, f32[64,1024]{1,0:T(8,128)}) custom-call(bf16[16,64,1024]{2,1,0:T(8,128)(2,1)} %all-to-all-done.3.image_parts, f32[64,1024]{1,0:T(8,128)S(1)} %get-tuple-element.21.own_ref, bf16[64,1024]{1,0:T(8,128)(2,1)S(1)} %collective-permute-done.9.refs_0_, bf16[64,1024]{1,0:T(8,128)(2,1)S(1)} %collective-permute-done.10.refs_1_, ...), custom_call_target="tpu_custom_call" | custom-call | flops 1572864 | bytes 4194304 | tf_op jit(solution)/shard_map/sums/pallas_call | solution.py:270
  (73 shorter events, 13.5 us)
Async XLA Ops:
  0.6 27.0 %collective-permute-start.5 = (bf16[64,1024]{1,0:T(8,128)(2,1)}, bf16[64,1024]{1,0:T(8,128)(2,1)S(1)}, u32[]{:S(2)}, u32[]{:S(2)}) collective-permute-start(bf16[64,1024]{1,0:T(8,128)(2,1)} %refs_0_.1), channel_id=1, source_target_pairs={{0,2},{1,3},{2,4},{3,5},{4,6},{5,7},{6,0},{7,1},{8,10},{9,11},{10,... | collective-permute-start | bytes 393224 | tf_op jit(solution)/shard_map/ppermute | solution.py:25
  4.0 23.7 %collective-permute-start.4 = (bf16[64,1024]{1,0:T(8,128)(2,1)}, bf16[64,1024]{1,0:T(8,128)(2,1)S(1)}, u32[]{:S(2)}, u32[]{:S(2)}) collective-permute-start(bf16[64,1024]{1,0:T(8,128)(2,1)} %refs_0_.1), channel_id=1, source_target_pairs={{0,3},{1,4},{2,5},{3,6},{4,7},{5,0},{6,1},{7,2},{8,11},{9,12},{10,... | collective-permute-start | bytes 393224 | tf_op jit(solution)/shard_map/ppermute | solution.py:25
  8.9 23.1 %collective-permute-start.3 = (bf16[64,1024]{1,0:T(8,128)(2,1)}, bf16[64,1024]{1,0:T(8,128)(2,1)S(1)}, u32[]{:S(2)}, u32[]{:S(2)}) collective-permute-start(bf16[64,1024]{1,0:T(8,128)(2,1)} %refs_0_.1), channel_id=1, source_target_pairs={{0,4},{1,5},{2,6},{3,7},{4,0},{5,1},{6,2},{7,3},{8,12},{9,13},{10,... | collective-permute-start | bytes 393224 | tf_op jit(solution)/shard_map/ppermute | solution.py:25
  9.9 22.8 %collective-permute-start.2 = (bf16[64,1024]{1,0:T(8,128)(2,1)}, bf16[64,1024]{1,0:T(8,128)(2,1)S(1)}, u32[]{:S(2)}, u32[]{:S(2)}) collective-permute-start(bf16[64,1024]{1,0:T(8,128)(2,1)} %refs_0_.1), channel_id=1, source_target_pairs={{0,5},{1,6},{2,7},{3,0},{4,1},{5,2},{6,3},{7,4},{8,13},{9,14},{10,... | collective-permute-start | bytes 393224 | tf_op jit(solution)/shard_map/ppermute | solution.py:25
  14.4 19.2 %collective-permute-start.1 = (bf16[64,1024]{1,0:T(8,128)(2,1)}, bf16[64,1024]{1,0:T(8,128)(2,1)S(1)}, u32[]{:S(2)}, u32[]{:S(2)}) collective-permute-start(bf16[64,1024]{1,0:T(8,128)(2,1)} %refs_0_.1), channel_id=1, source_target_pairs={{0,6},{1,7},{2,0},{3,1},{4,2},{5,3},{6,4},{7,5},{8,14},{9,15},{10,... | collective-permute-start | bytes 393224 | tf_op jit(solution)/shard_map/ppermute | solution.py:25
  19.6 8.0 %copy-start.6 = (bf16[64,1024]{1,0:T(8,128)(2,1)S(1)}, bf16[64,1024]{1,0:T(8,128)(2,1)}, u32[]{:S(2)}) copy-start(bf16[64,1024]{1,0:T(8,128)(2,1)} %refs_0_.1) | copy-start | bytes 393220
  19.6 11.7 %copy-start.17 = (s32[16384]{0:T(1024)S(1)}, s32[16384]{0:T(1024)}, u32[]{:S(2)}) copy-start(s32[16384]{0:T(1024)} %param.7) | copy-start | bytes 196612
  19.6 34.4 %all-to-all-start = ((bf16[16,64,1024]{2,1,0:T(8,128)(2,1)}), bf16[16,64,1024]{2,1,0:T(8,128)(2,1)S(1)}, u32[]{:S(2)}, u32[]{:S(2)}) async-start(bf16[16,64,1024]{2,1,0:T(8,128)(2,1)} %broadcast_in_dim.8), calls=%async_computation | async-start | bytes 4194304 | tf_op jit(solution)/shard_map/all_to_all | solution.py:36
  27.6 7.1 %collective-permute-start = (bf16[64,1024]{1,0:T(8,128)(2,1)S(1)}, bf16[64,1024]{1,0:T(8,128)(2,1)S(1)}, u32[]{:S(2)}, u32[]{:S(2)}) collective-permute-start(bf16[64,1024]{1,0:T(8,128)(2,1)S(1)} %copy-done.6), channel_id=1, source_target_pairs={{0,7},{1,0},{2,1},{3,2},{4,3},{5,4},{6,5},{7,6},{8,15},{9,8},{10,9... | collective-permute-start | bytes 393224 | tf_op jit(solution)/shard_map/ppermute | solution.py:25
  27.7 7.7 %collective-permute-start.6 = (bf16[64,1024]{1,0:T(8,128)(2,1)S(1)}, bf16[64,1024]{1,0:T(8,128)(2,1)S(1)}, u32[]{:S(2)}, u32[]{:S(2)}) collective-permute-start(bf16[64,1024]{1,0:T(8,128)(2,1)S(1)} %copy-done.6), channel_id=1, source_target_pairs={{0,1},{1,2},{2,3},{3,4},{4,5},{5,6},{6,7},{7,0},{8,9},{9,10},{10,1... | collective-permute-start | bytes 393224 | tf_op jit(solution)/shard_map/ppermute | solution.py:25
  35.4 0.7 copy-start.15
  36.1 0.9 copy-start.8
  37.0 0.9 copy-start.10
  37.9 0.9 copy-start.12
  38.8 0.9 copy-start.14
  39.7 0.9 copy-start.16
  40.7 4.6 %collective-permute-start.7 = (bf16[512,1024]{1,0:T(8,128)(2,1)S(1)}, bf16[512,1024]{1,0:T(8,128)(2,1)}, u32[]{:S(2)}, u32[]{:S(2)}) collective-permute-start(bf16[512,1024]{1,0:T(8,128)(2,1)S(1)} %join.1.near_ref), channel_id=1, source_target_pairs={{0,32},{32,0},{1,33},{33,1},{2,34},{34,2},{3,35},{35,3},{4,36},{36... | collective-permute-start | bytes 3145736 | tf_op jit(solution)/shard_map/ppermute | solution.py:20
  54.0 1.0 copy-start.3
  55.1 1.0 copy-start.5
  56.1 28.4 %copy-start.4 = (s32[1024,1]{1,0:T(8,128)S(1)}, s32[1024,1]{1,0:T(8,128)}, u32[]{:S(2)}) copy-start(s32[1024,1]{1,0:T(8,128)} %add.166.ri) | copy-start | bytes 12292
  90.2 2.7 %copy-start = (bf16[1024,1024]{1,0:T(8,128)(2,1)}, bf16[1024,1024]{1,0:T(8,128)(2,1)S(1)}, u32[]{:S(2)}) copy-start(bf16[1024,1024]{1,0:T(8,128)(2,1)S(1)} %get-tuple-element.20.grad_ref) | copy-start | bytes 6291460
  90.2 2.7 %copy-start.2 = (bf16[1024,1024]{1,0:T(8,128)(2,1)}, bf16[1024,1024]{1,0:T(8,128)(2,1)S(1)}, u32[]{:S(2)}) copy-start(bf16[1024,1024]{1,0:T(8,128)(2,1)S(1)} %get-tuple-element.19) | copy-start | bytes 6291460
  92.9 5.7 %collective-permute-start.8 = (f32[512,1024]{1,0:T(8,128)}, f32[512,1024]{1,0:T(8,128)}, u32[]{:S(2)}, u32[]{:S(2)}) collective-permute-start(f32[512,1024]{1,0:T(8,128)} %far_terms.1), channel_id=1, source_target_pairs={{0,32},{32,0},{1,33},{33,1},{2,34},{34,2},{3,35},{35,3},{4,36},{36... | collective-permute-start | bytes 6291464 | tf_op jit(solution)/shard_map/ppermute | solution.py:20
  92.9 39.0 %all-to-all-start.3 = ((bf16[16,64,1024]{2,1,0:T(8,128)(2,1)}), bf16[16,64,1024]{2,1,0:T(8,128)(2,1)}, u32[]{:S(2)}, u32[]{:S(2)}) async-start(bf16[16,64,1024]{2,1,0:T(8,128)(2,1)} %bitcast.8), calls=%async_computation.3 | async-start | bytes 4194304 | tf_op jit(solution)/shard_map/all_to_all | solution.py:339
  98.6 1.6 %copy-start.1 = (bf16[1024,1024]{1,0:T(8,128)(2,1)S(1)}, bf16[1024,1024]{1,0:T(8,128)(2,1)}, u32[]{:S(2)}) copy-start(bf16[1024,1024]{1,0:T(8,128)(2,1)} %copy-done) | copy-start | bytes 6291460
  103.8 10.0 %collective-permute-start.9 = (bf16[64,1024]{1,0:T(8,128)(2,1)S(1)}, bf16[64,1024]{1,0:T(8,128)(2,1)S(1)}, u32[]{:S(2)}, u32[]{:S(2)}) collective-permute-start(bf16[64,1024]{1,0:T(8,128)(2,1)S(1)} %get-tuple-element.22), channel_id=1, source_target_pairs={{0,1},{1,2},{2,3},{3,4},{4,5},{5,6},{6,7},{7,0},{8,9},{9,10},{10,1... | collective-permute-start | bytes 393224 | tf_op jit(solution)/shard_map/ppermute | solution.py:25
  104.8 13.0 %collective-permute-start.10 = (bf16[64,1024]{1,0:T(8,128)(2,1)S(1)}, bf16[64,1024]{1,0:T(8,128)(2,1)S(1)}, u32[]{:S(2)}, u32[]{:S(2)}) collective-permute-start(bf16[64,1024]{1,0:T(8,128)(2,1)S(1)} %get-tuple-element.23), channel_id=1, source_target_pairs={{0,2},{1,3},{2,4},{3,5},{4,6},{5,7},{6,0},{7,1},{8,10},{9,11},{10,... | collective-permute-start | bytes 393224 | tf_op jit(solution)/shard_map/ppermute | solution.py:25
  105.4 26.4 %collective-permute-start.11 = (bf16[64,1024]{1,0:T(8,128)(2,1)}, bf16[64,1024]{1,0:T(8,128)(2,1)S(1)}, u32[]{:S(2)}, u32[]{:S(2)}) collective-permute-start(bf16[64,1024]{1,0:T(8,128)(2,1)} %get-tuple-element.24), channel_id=1, source_target_pairs={{0,3},{1,4},{2,5},{3,6},{4,7},{5,0},{6,1},{7,2},{8,11},{9,12},{10,... | collective-permute-start | bytes 393224 | tf_op jit(solution)/shard_map/ppermute | solution.py:25
  107.8 24.1 %collective-permute-start.12 = (bf16[64,1024]{1,0:T(8,128)(2,1)}, bf16[64,1024]{1,0:T(8,128)(2,1)S(1)}, u32[]{:S(2)}, u32[]{:S(2)}) collective-permute-start(bf16[64,1024]{1,0:T(8,128)(2,1)} %get-tuple-element.25), channel_id=1, source_target_pairs={{0,4},{1,5},{2,6},{3,7},{4,0},{5,1},{6,2},{7,3},{8,12},{9,13},{10,... | collective-permute-start | bytes 393224 | tf_op jit(solution)/shard_map/ppermute | solution.py:25
  111.3 20.5 %collective-permute-start.13 = (bf16[64,1024]{1,0:T(8,128)(2,1)}, bf16[64,1024]{1,0:T(8,128)(2,1)S(1)}, u32[]{:S(2)}, u32[]{:S(2)}) collective-permute-start(bf16[64,1024]{1,0:T(8,128)(2,1)} %get-tuple-element.26), channel_id=1, source_target_pairs={{0,5},{1,6},{2,7},{3,0},{4,1},{5,2},{6,3},{7,4},{8,13},{9,14},{10,... | collective-permute-start | bytes 393224 | tf_op jit(solution)/shard_map/ppermute | solution.py:25
  113.8 19.7 %collective-permute-start.14 = (bf16[64,1024]{1,0:T(8,128)(2,1)S(1)}, bf16[64,1024]{1,0:T(8,128)(2,1)S(1)}, u32[]{:S(2)}, u32[]{:S(2)}) collective-permute-start(bf16[64,1024]{1,0:T(8,128)(2,1)S(1)} %get-tuple-element.27), channel_id=1, source_target_pairs={{0,6},{1,7},{2,0},{3,1},{4,2},{5,3},{6,4},{7,5},{8,14},{9,15},{10,... | collective-permute-start | bytes 393224 | tf_op jit(solution)/shard_map/ppermute | solution.py:25
  117.8 16.8 %collective-permute-start.15 = (bf16[64,1024]{1,0:T(8,128)(2,1)S(1)}, bf16[64,1024]{1,0:T(8,128)(2,1)S(1)}, u32[]{:S(2)}, u32[]{:S(2)}) collective-permute-start(bf16[64,1024]{1,0:T(8,128)(2,1)S(1)} %get-tuple-element.28), channel_id=1, source_target_pairs={{0,7},{1,0},{2,1},{3,2},{4,3},{5,4},{6,5},{7,6},{8,15},{9,8},{10,9... | collective-permute-start | bytes 393224 | tf_op jit(solution)/shard_map/ppermute | solution.py:25
  (4 other events, 2.6 us)

commit v3 on v0

v3 whole, which is shorter than its diff:
```python
import math

import jax
import jax.numpy as jnp
from jax import lax
from jax.experimental import pallas as pl
from jax.experimental.pallas import tpu as pltpu
from jax.sharding import Mesh, PartitionSpec as P

logit_scale = 100.0
scale_base2 = logit_scale / math.log(2.0)
floor_value = -1e30
mib = 1024 * 1024
lanes = 128
block = 256

axes = ("y", "core", "x", "z")
plane = ("y", "x")
in_vmem = pl.BlockSpec(memory_space=pltpu.VMEM)
in_hbm = pl.BlockSpec(memory_space=pltpu.HBM)


def swap_core(values):
    return lax.ppermute(values, "core", [(0, 1), (1, 0)])


def shift(values, axis, step):
    size = lax.axis_size(axis)
    return lax.ppermute(values, axis, [(i, (i + step) % size) for i in range(size)])


def shift_z(values, step):
    return shift(values, "z", step)


def z_steps(size):
    steps = [size // 2]
    for step in range(size // 2 - 1, 0, -1):
        steps += [step, size - step]
    return steps


def contract(a, b, dim_a, dim_b):
    return lax.dot_general(a, b, (((dim_a,), (dim_b,)), ((), ())), preferred_element_type=jnp.float32)


def as_column(row):
    return jnp.broadcast_to(row, (lanes, row.shape[1])).T[:, 0:1]


def as_row(column):
    return jnp.broadcast_to(column, (column.shape[0], lanes)).T[0:1, :]


def fold(row):
    return jnp.concatenate([row[:, i : i + lanes] for i in range(0, row.shape[1], lanes)], axis=0)


def unfold(tile):
    return jnp.concatenate([tile[i : i + 1, :] for i in range(tile.shape[0])], axis=1)


def by_core(tile, core):
    half = tile.shape[0] // 2
    return jnp.where(core == 0, tile, jnp.concatenate([tile[half:], tile[:half]], axis=0))


def estimate(flops, megabytes, exps=0):
    return pl.CostEstimate(flops=flops, bytes_accessed=megabytes * mib, transcendentals=exps)


def params(megabytes):
    return pltpu.CompilerParams(vmem_limit_bytes=megabytes * mib)


def here_in_mesh():
    return [lax.axis_index(name) for name in axes]


def row_ids(place, start, count, span):
    y, core, x, z = place
    at = start + lax.broadcasted_iota(jnp.int32, (count, 1), 0)
    member = at // span
    n_x, n_z, n_core = 4, 8, 2
    return (((member // n_x * n_core + core) * n_x + member % n_x) * n_z + z) * span + at % span


def col_ids(place, count, span):
    y, core, x, z = place
    n_y, n_z, n_core = 4, 8, 2
    at = lax.broadcasted_iota(jnp.int32, (1, count), 1)
    part = at // span
    side = jnp.where(part < n_z, core, 1 - core)
    return (((x * n_z + part % n_z) * n_y + y) * n_core + side) * span + at % span


def halves(a, b, which):
    low = lax.broadcasted_iota(jnp.int32, a.shape, 1) < lanes // 2
    turned_a = jnp.where(which == 0, a, pltpu.roll(a, lanes // 2, 1))
    turned_b = jnp.where(which == 0, pltpu.roll(b, lanes // 2, 1), b)
    return jnp.where(low, turned_a, turned_b)


def group_rows(place, group_ref):
    y, core, x, z = place
    n_x, n_z, n_plane = 4, 8, 16

    def ids(at):
        return group_ref[pl.ds(at, 1), :].astype(jnp.float32)

    rows = []
    for j in range(n_plane // 2):
        a, b = [ids(((m // n_x) * 2 + core) * 16 + (m % n_x) * 4 + z // 2) for m in (2 * j, 2 * j + 1)]
        rows.append(halves(a, b, lax.rem(z, 2)))
    cols = []
    for side in (core, 1 - core):
        for j in range(n_z // 2):
            a, b = [ids((x * n_z + m) * 4 + y) for m in (2 * j, 2 * j + 1)]
            cols.append(halves(a, b, side))
    return rows, cols


def repeat_kernel(in_ref, out_ref, held, sems):
    load = pltpu.make_async_copy(in_ref, held, sems.at[0])
    load.start()
    load.wait()
    copies = [pltpu.make_async_copy(held, out_ref.at[i], sems.at[1 + i]) for i in range(out_ref.shape[0])]
    for copy in copies:
        copy.start()
    for copy in copies:
        copy.wait()


def repeat(values, count):
    return pl.pallas_call(
        repeat_kernel,
        in_specs=[in_hbm],
        out_specs=in_hbm,
        out_shape=jax.ShapeDtypeStruct((count,) + values.shape, values.dtype),
        scratch_shapes=[pltpu.VMEM(values.shape, values.dtype), pltpu.SemaphoreType.DMA((1 + count,))],
        compiler_params=params(60),
        cost_estimate=estimate(0, 2),
        name="repeat",
    )(values)


def stats_kernel(rows, group_ref, *refs):
    shards, (kept_ref, cols_ref, row_ref, col_ref, kept_all, cols, groups, sems) = refs[:-8], refs[-8:]
    where = here_in_mesh()
    n_rows, n_cols = kept_ref.shape
    half = n_cols // 2
    n_blocks = n_rows // block
    n_z = len(shards) // 2
    span = half // n_z

    stores = [
        pltpu.make_async_copy(
            kept_all.at[pl.ds(i * block, block), :], kept_ref.at[pl.ds(i * block, block), :], sems.at[i]
        )
        for i in range(n_blocks)
    ]
    cols_store = pltpu.make_async_copy(cols, cols_ref, sems.at[n_blocks])
    group_load = pltpu.make_async_copy(group_ref, groups, sems.at[n_blocks + 1])
    group_load.start()
    for side in range(2):
        for k in range(n_z):
            at = pl.multiple_of(side * half + lax.rem(where[3] + k, n_z) * span, span)
            cols[pl.ds(at, span), :] = shards[side * n_z + k][...]
    cols_store.start()
    kept_all[:block, :] = scale_base2 * contract(rows[:block, :], cols[...], 1, 1)
    group_load.wait()
    row_groups, col_groups = group_rows(where, groups)
    ci = col_ids(where, n_cols, span)
    cg = jnp.concatenate(col_groups, axis=1)

    def fill(i):
        here = slice(i * block, (i + 1) * block)
        ri = row_ids(where, i * block, block, span)
        per = block // lanes
        rg = as_column(jnp.concatenate(row_groups[i * per : (i + 1) * per], axis=1))
        scores = scale_base2 * contract(rows[here, :], cols[...], 1, 1) if i else kept_all[here, :]
        valid = jnp.logical_or(rg != cg, ri == ci)
        kept_all[here, :] = jnp.where(valid, scores, floor_value)
        stores[i].start()

    peak = jnp.full((1, n_cols), floor_value, jnp.float32)
    total = jnp.zeros((1, n_cols), jnp.float32)
    fill(0)
    for i in range(n_blocks):
        if i + 1 < n_blocks:
            fill(i + 1)
        kept = kept_all[i * block : (i + 1) * block, :]
        row_peak = jnp.max(kept, axis=1, keepdims=True)
        row_total = jnp.sum(jnp.exp2(kept - row_peak), axis=1, keepdims=True)
        row_lse = fold(as_row(row_peak + jnp.log2(row_total)))
        for j in range(block // lanes):
            row_ref[:, i * block // lanes + j : i * block // lanes + j + 1, :] = jnp.broadcast_to(
                row_lse[None, j : j + 1, :], (row_ref.shape[0], 1, lanes)
            )
        top = jnp.maximum(peak, jnp.max(kept, axis=0, keepdims=True))
        total = total * jnp.exp2(peak - top) + jnp.sum(jnp.exp2(kept - top), axis=0, keepdims=True)
        peak = top
    col_lse = by_core(fold(peak + jnp.log2(total)), where[1])
    col_ref[...] = jnp.broadcast_to(col_lse[None], col_ref.shape)
    for copy in (cols_store, *stores):
        copy.wait()


def block_stats(rows, groups, shards, n_row, n_col):
    n_rows, width = rows.shape
    n_cols = len(shards) * shards[0].shape[0]
    return pl.pallas_call(
        stats_kernel,
        in_specs=[in_vmem, in_hbm] + [in_vmem] * len(shards),
        out_specs=[in_hbm, in_hbm, in_vmem, in_vmem],
        out_shape=[
            jax.ShapeDtypeStruct((n_rows, n_cols), jnp.float32),
            jax.ShapeDtypeStruct((n_cols, width), jnp.bfloat16),
            jax.ShapeDtypeStruct((n_row, n_rows // lanes, lanes), jnp.float32),
            jax.ShapeDtypeStruct((n_col, n_cols // lanes, lanes), jnp.float32),
        ],
        scratch_shapes=[
            pltpu.VMEM((n_rows, n_cols), jnp.float32),
            pltpu.VMEM((n_cols, width), jnp.bfloat16),
            pltpu.VMEM(groups.shape, groups.dtype),
            pltpu.SemaphoreType.DMA((n_rows // block + 2,)),
        ],
        compiler_params=params(55),
        cost_estimate=estimate(2 * n_rows * n_cols * width, 8, 2 * n_rows * n_cols),
        name="stats",
    )(rows, groups, *shards)


def merge(parts):
    top = parts[0]
    for part in parts[1:]:
        top = jnp.maximum(top, part)
    total = jnp.exp2(parts[0] - top)
    for part in parts[1:]:
        total = total + jnp.exp2(part - top)
    return top + jnp.log2(total)


def grad_kernel(kept_ref, cols_ref, row_parts, col_parts, col_others, image_ref, grad_ref, kept_all, cols, grads, image, sems):
    where = here_in_mesh()
    n_rows, n_cols = kept_ref.shape
    n_blocks = n_rows // block
    span = 64

    def piece(i):
        return pl.ds(i * block, block)

    kept_loads = [
        pltpu.make_async_copy(kept_ref.at[piece(i), :], kept_all.at[piece(i), :], sems.at[i]) for i in range(n_blocks)
    ]
    cols_load = pltpu.make_async_copy(cols_ref, cols, sems.at[n_blocks])
    image_stores = [
        pltpu.make_async_copy(image.at[piece(i), :], image_ref.at[piece(i), :], sems.at[n_blocks + 1 + i])
        for i in range(n_blocks)
    ]
    grad_stores = [
        pltpu.make_async_copy(grads.at[piece(i), :], grad_ref.at[piece(i), :], sems.at[2 * n_blocks + 1 + i])
        for i in range(n_blocks)
    ]
    for copy in (kept_loads[0], cols_load, *kept_loads[1:]):
        copy.start()
    ci = col_ids(where, n_cols, span)
    row_lse = merge([row_parts[i] for i in range(row_parts.shape[0])])
    col_lse = unfold(by_core(merge([ref[i] for ref in (col_parts, col_others) for i in range(ref.shape[0])]), where[1]))

    def fill(i):
        here = slice(i * block, (i + 1) * block)
        ri = row_ids(where, i * block, block, span)
        lse = as_column(unfold(row_lse[i * block // lanes : (i + 1) * block // lanes, :]))
        kept = kept_all[here, :]
        weight = jnp.exp2(kept - lse) + jnp.exp2(kept - col_lse)
        grad = 0.5 * weight - jnp.where(ri == ci, 1.0, 0.0)
        grads[here, :] = grad.astype(jnp.bfloat16)

    kept_loads[0].wait()
    fill(0)
    cols_load.wait()
    for i in range(n_blocks):
        if i + 1 < n_blocks:
            kept_loads[i + 1].wait()
            fill(i + 1)
        here = slice(i * block, (i + 1) * block)
        image[here, :] = contract(grads[here, :], cols[...], 1, 0).astype(jnp.bfloat16)
        image_stores[i].start()
        grad_stores[i].start()
    for copy in (*image_stores, *grad_stores):
        copy.wait()


def block_grad(kept, cols, row_parts, col_parts, col_others):
    n_rows, n_cols = kept.shape
    width = cols.shape[1]
    return pl.pallas_call(
        grad_kernel,
        in_specs=[in_hbm] * 2 + [in_vmem] * 3,
        out_specs=[in_hbm] * 2,
        out_shape=[
            jax.ShapeDtypeStruct((n_rows, width), jnp.bfloat16),
            jax.ShapeDtypeStruct((n_rows, n_cols), jnp.bfloat16),
        ],
        scratch_shapes=[
            pltpu.VMEM((n_rows, n_cols), jnp.float32),
            pltpu.VMEM((n_cols, width), jnp.bfloat16),
            pltpu.VMEM((n_rows, n_cols), jnp.bfloat16),
            pltpu.VMEM((n_rows, width), jnp.bfloat16),
            pltpu.SemaphoreType.DMA((3 * (n_rows // block) + 1,)),
        ],
        compiler_params=params(60),
        cost_estimate=estimate(2 * n_rows * n_cols * width, 12, 2 * n_rows * n_cols),
        name="grad",
    )(kept, cols, row_parts, col_parts, col_others)


def text_kernel(grad_ref, rows_ref, other_ref, other_rows_ref, own_ref, *refs):
    n_z = len(refs) - 3
    sent, (grads, rows, total, sems) = refs[: n_z - 1], refs[n_z - 1 :]
    n_cols = total.shape[0]
    span = n_cols // n_z
    depth = rows_ref.shape[0] // 2
    parts = [(i, j) for i in range(2) for j in range(2)]
    loads = {}
    for i, j in parts:
        here = pl.ds(j * depth, depth)
        pair = ((grad_ref, rows_ref), (other_ref, other_rows_ref))[i]
        loads[i, j] = [
            pltpu.make_async_copy(pair[0].at[here, pl.ds(i * n_cols, n_cols)], grads.at[i, here, :], sems.at[4 * i + 2 * j]),
            pltpu.make_async_copy(pair[1].at[here, :], rows.at[i, here, :], sems.at[4 * i + 2 * j + 1]),
        ]
        for copy in loads[i, j]:
            copy.start()
    for i, j in parts:
        for copy in loads[i, j]:
            copy.wait()
        deep = slice(j * depth, (j + 1) * depth)
        for at in range(0, n_cols, block):
            here = slice(at, at + block)
            part = contract(grads[i, deep, here], rows[i, deep, :], 0, 0)
            if i + j == 0:
                total[here, :] = part
            else:
                total[here, :] += part
    for k in range(n_z):
        at = pl.multiple_of(lax.rem(lax.axis_index("z") + k, n_z) * span, span)
        value = total[pl.ds(at, span), :]
        if k == 0:
            own_ref[...] = value
        else:
            sent[k - 1][...] = value.astype(jnp.bfloat16)


def text_terms(grad, rows, other, other_rows, n_z):
    n_rows, n_cols = grad.shape[0], grad.shape[1] // 2
    width = rows.shape[1]
    span = n_cols // n_z
    return pl.pallas_call(
        text_kernel,
        in_specs=[in_hbm] * 4,
        out_specs=[in_vmem] * n_z,
        out_shape=[jax.ShapeDtypeStruct((span, width), jnp.float32)]
        + [jax.ShapeDtypeStruct((span, width), jnp.bfloat16)] * (n_z - 1),
        scratch_shapes=[
            pltpu.VMEM((2, n_rows, n_cols), jnp.bfloat16),
            pltpu.VMEM((2, n_rows, width), jnp.bfloat16),
            pltpu.VMEM((n_cols, width), jnp.float32),
            pltpu.SemaphoreType.DMA((8,)),
        ],
        compiler_params=params(58),
        cost_estimate=estimate(4 * n_rows * n_cols * width, 8),
        name="text_terms",
    )(grad, rows, other, other_rows)


def sum_kernel(image_parts, own_ref, *refs):
    text_parts, (image_ref, text_ref, own, sem) = refs[:-4], refs[-4:]
    load = pltpu.make_async_copy(own_ref, own, sem)
    load.start()
    total = image_parts[0].astype(jnp.float32)
    for i in range(1, image_parts.shape[0]):
        total = total + image_parts[i].astype(jnp.float32)
    image_ref[...] = logit_scale * total
    total = text_parts[0][...].astype(jnp.float32)
    for ref in text_parts[1:]:
        total = total + ref[...].astype(jnp.float32)
    load.wait()
    total = total + own[...]
    text_ref[...] = logit_scale * total


def final_sums(image_parts, own, text_parts):
    n_plane, span, width = image_parts.shape
    return pl.pallas_call(
        sum_kernel,
        in_specs=[in_vmem, in_hbm] + [in_vmem] * len(text_parts),
        out_specs=[in_vmem] * 2,
        out_shape=[jax.ShapeDtypeStruct((span, width), jnp.float32)] * 2,
        scratch_shapes=[pltpu.VMEM((span, width), jnp.float32), pltpu.SemaphoreType.DMA],
        compiler_params=params(8),
        cost_estimate=estimate(span * width * 24, 4),
        name="sums",
    )(image_parts, own, *text_parts)


def per_device(image_emb, text_emb, caption_group):
    span, width = image_emb.shape
    n_y, n_core, n_x, n_z = (lax.axis_size(a) for a in axes)
    n_plane = n_y * n_x
    groups = caption_group.reshape(-1, lanes)

    rows = lax.all_to_all(repeat(image_emb, n_plane), plane, 0, 0)
    rows = rows.reshape(n_plane * span, width)
    shards = {0: text_emb}
    for k in range(1, n_z // 2):
        shards[n_z - k] = shift_z(shards[(n_z - k + 1) % n_z], 1)
        shards[k] = shift_z(shards[k - 1], -1)
    shards[n_z // 2] = shift_z(shards[n_z // 2 - 1], -1)
    near = [shards[k] for k in range(n_z)]
    far = [swap_core(shard) for shard in near]

    kept, cols, row_part, col_part = block_stats(rows, groups, near + far, n_plane, n_z)
    row_parts = lax.all_to_all(row_part, plane, 0, 0)
    col_parts = lax.all_to_all(col_part, "z", 0, 0)
    col_others = swap_core(col_parts)
    other_rows = swap_core(rows)

    image_part, grad = block_grad(kept, cols, row_parts, col_parts, col_others)
    image_parts = lax.all_to_all(image_part.reshape(n_plane, span, width), plane, 0, 0)
    own, *sent = text_terms(grad, rows, swap_core(grad), other_rows, n_z)
    text_parts = [shift_z(sent[k - 1], k) for k in z_steps(n_z)]
    return tuple(final_sums(image_parts, own, text_parts))


def solution(mesh):
    fine = Mesh(mesh.devices.reshape(4, 2, 4, 8), axes)
    return jax.shard_map(
        per_device,
        mesh=fine,
        in_specs=(P(axes, None), P(("x", "z", "y", "core"), None), P()),
        out_specs=(P(axes, None), P(("x", "z", "y", "core"), None)),
        check_vma=False,
    )
```

time: 592 us -> 129 us (0.22)
  waiting for transfers between devices: 357 us -> 33.1 us
  blocking collectives: 167 us -> 16.5 us
  starting transfers between devices: 0.16 us -> 47.8 us
  matrix products: 32.7 us -> 0 us
  Pallas kernels: 0 us -> 24 us
  between operations: 13.9 us -> 1.09 us
  local copies, waits for them, and re-layouts: 16.6 us -> 4.02 us
    reduce_scatter x2 -> x0, waiting for transfers between devices: 257 us -> none  [the longest x1 235 us: scatter_wide(): lax.psum_scatter(term(jnp.int32(0), span * lax.axis_size('wide')), 'wide'...]
    all_gather x2 -> x0, waiting for transfers between devices: 99.1 us -> none  [the longest x1 85.9 us: gather_wide(): return lax.all_gather(values, 'wide', axis=0, tiled=True)]
    pmax x2 -> x0, blocking collectives: 83.6 us -> none  [the longest x1 73.6 us: merge_wide(): top = lax.pmax(peak, 'wide')]
    psum x2 -> x0, blocking collectives: 83.2 us -> none  [the longest x1 70.8 us: merge_wide(): total = lax.psum(total * jnp.exp(peak - top), 'wide')]
    dot_general x10 -> x0, matrix products: 32.7 us -> none  [the longest x8 21.1 us: masked_logits(): lax.dot_general(rows_emb, cols_emb, (((1,), (1,)), ((), ())), preferred_e...]
    ppermute x0 -> x25, starting transfers between devices: none -> 30.4 us  [the longest x14 28.7 us: shift(): lax.ppermute(values, axis, [(i, (i + step) % size) for i in range(size)])]
    pallas_call x0 -> x5, Pallas kernels: none -> 24 us  [the longest x1 7.86 us: block_stats(): pl.pallas_call(stats_kernel, in_specs=[in_vmem, in_hbm] + [in_vmem] * len...]
    ppermute x0 -> x25, waiting for transfers between devices: none -> 20.4 us  [the longest x14 20.1 us: shift(): lax.ppermute(values, axis, [(i, (i + step) % size) for i in range(size)])]
  transfers between devices with their start and end apart: 4 -> 28, of which waited for: 4 -> 11; matrix products, arithmetic and copies ran while one was open for 3% -> 0% of each run, Pallas kernels for 0% -> 10%
where the time goes in v3:
time: 129 us; the launch traced here: 127 us
  starting transfers between devices  47.8 us (37%)
  waiting for transfers between devices  33.1 us (26%)
  Pallas kernels  24 us (19%)
  blocking collectives  16.5 us (13%)
  local copies, waits for them, and re-layouts  4.02 us (3%)
    ppermute x14, starting transfers between devices, shift(): lax.ppermute(values, axis, [(i, (i + step) % size) for i in range(size)])  28.7 us
    ppermute x14, waiting for transfers between devices, shift(): lax.ppermute(values, axis, [(i, (i + step) % size) for i in range(size)])  20.1 us
    all_to_all x1, blocking collectives, per_device(): col_parts = lax.all_to_all(col_part, 'z', 0, 0)  16.5 us
    pallas_call x1, Pallas kernels, block_stats(): pl.pallas_call(stats_kernel, in_specs=[in_vmem, in_hbm] + [in_vmem] * len...  7.86 us
    all_to_all x1, starting transfers between devices, per_device(): rows = lax.all_to_all(repeat(image_emb, n_plane), plane, 0, 0)  7.54 us
    pallas_call x1, Pallas kernels, block_grad(): pl.pallas_call(grad_kernel, in_specs=[in_hbm] * 2 + [in_vmem] * 3, out_sp...  7.51 us
    all_to_all x1, waiting for transfers between devices, per_device(): row_parts = lax.all_to_all(row_part, plane, 0, 0)  5.75 us
    all_to_all x1, waiting for transfers between devices, per_device(): lax.all_to_all(image_part.reshape(n_plane, span, width), plane, 0, 0)  5.06 us
  transfers between devices with their start and end apart: 28, of which 11 were waited for; matrix products, arithmetic and copies ran while one was open for 0% of the time, Pallas kernels for 10%

profile of v3, /device:TPU:8, one launch (start us, length us, event | category | flops | bytes accessed | tf_op | source)
XLA Modules:
  0.0 126.6 jit_solution(8437992578150194460)
XLA Ops:
  0.6 2.4 %repeat.1 = bf16[16,64,1024]{2,1,0:T(8,128)(2,1)} custom-call(bf16[64,1024]{1,0:T(8,128)(2,1)} %in_ref.1), custom_call_target="tpu_custom_call" | custom-call | bytes 2097152 | tf_op jit(solution)/shard_map/repeat/pallas_call | solution.py:135
  3.0 7.5 %all-to-all-start = ((bf16[16,64,1024]{2,1,0:T(8,128)(2,1)}), bf16[16,64,1024]{2,1,0:T(8,128)(2,1)S(1)}, u32[]{:S(2)}, u32[]{:S(2)}) async-start(bf16[16,64,1024]{2,1,0:T(8,128)(2,1)} %repeat.1), calls=%async_computation | async-start | bytes 4194304 | tf_op jit(solution)/shard_map/all_to_all | solution.py:414
  10.6 5.9 %collective-permute-start = (bf16[64,1024]{1,0:T(8,128)(2,1)S(1)}, bf16[64,1024]{1,0:T(8,128)(2,1)S(1)}, u32[]{:S(2)}, u32[]{:S(2)}) collective-permute-start(bf16[64,1024]{1,0:T(8,128)(2,1)S(1)} %copy-done.4), channel_id=1, source_target_pairs={{0,7},{1,0},{2,1},{3,2},{4,3},{5,4},{6,5},{7,6},{8,15},{9,8},{10,9... | collective-permute-start | bytes 393224 | tf_op jit(solution)/shard_map/ppermute | solution.py:29
  16.5 2.5 %collective-permute-done.refs_1_ = bf16[64,1024]{1,0:T(8,128)(2,1)S(1)} collective-permute-done((bf16[64,1024]{1,0:T(8,128)(2,1)S(1)}, bf16[64,1024]{1,0:T(8,128)(2,1)S(1)}, u32[]{:S(2)}, u32[]{:S(2)}) %collective-permute-start) | collective-permute-done | bytes 131104 | tf_op jit(solution)/shard_map/ppermute | solution.py:29
  19.0 3.7 %collective-permute-start.1 = (bf16[64,1024]{1,0:T(8,128)(2,1)S(1)}, bf16[64,1024]{1,0:T(8,128)(2,1)S(1)}, u32[]{:S(2)}, u32[]{:S(2)}) collective-permute-start(bf16[64,1024]{1,0:T(8,128)(2,1)S(1)} %collective-permute-done.refs_1_), channel_id=1, source_target_pairs={{0,7},{1,0},{2,1},{3,2},{4,3},{5,4},{6,5},{7,6},{8,15},{9,8},{10,9... | collective-permute-start | bytes 393224 | tf_op jit(solution)/shard_map/ppermute | solution.py:29
  22.7 2.5 %collective-permute-done.1.refs_2_ = bf16[64,1024]{1,0:T(8,128)(2,1)S(1)} collective-permute-done((bf16[64,1024]{1,0:T(8,128)(2,1)S(1)}, bf16[64,1024]{1,0:T(8,128)(2,1)S(1)}, u32[]{:S(2)}, u32[]{:S(2)}) %collective-permute-start.1) | collective-permute-done | bytes 131104 | tf_op jit(solution)/shard_map/ppermute | solution.py:29
  25.2 3.7 %collective-permute-start.2 = (bf16[64,1024]{1,0:T(8,128)(2,1)S(1)}, bf16[64,1024]{1,0:T(8,128)(2,1)S(1)}, u32[]{:S(2)}, u32[]{:S(2)}) collective-permute-start(bf16[64,1024]{1,0:T(8,128)(2,1)S(1)} %collective-permute-done.1.refs_2_), channel_id=1, source_target_pairs={{0,7},{1,0},{2,1},{3,2},{4,3},{5,4},{6,5},{7,6},{8,15},{9,8},{10,9... | collective-permute-start | bytes 393224 | tf_op jit(solution)/shard_map/ppermute | solution.py:29
  29.5 1.9 %collective-permute-done.2.refs_3_ = bf16[64,1024]{1,0:T(8,128)(2,1)S(1)} collective-permute-done((bf16[64,1024]{1,0:T(8,128)(2,1)S(1)}, bf16[64,1024]{1,0:T(8,128)(2,1)S(1)}, u32[]{:S(2)}, u32[]{:S(2)}) %collective-permute-start.2) | collective-permute-done | bytes 131104 | tf_op jit(solution)/shard_map/ppermute | solution.py:29
  31.4 3.7 %collective-permute-start.3 = (bf16[64,1024]{1,0:T(8,128)(2,1)S(1)}, bf16[64,1024]{1,0:T(8,128)(2,1)S(1)}, u32[]{:S(2)}, u32[]{:S(2)}) collective-permute-start(bf16[64,1024]{1,0:T(8,128)(2,1)S(1)} %collective-permute-done.2.refs_3_), channel_id=1, source_target_pairs={{0,7},{1,0},{2,1},{3,2},{4,3},{5,4},{6,5},{7,6},{8,15},{9,8},{10,9... | collective-permute-start | bytes 393224 | tf_op jit(solution)/shard_map/ppermute | solution.py:29
  35.7 0.8 collective-permute-done.6.refs_5_
  36.5 1.0 collective-permute-done.3.refs_4_
  38.4 0.7 copy-done.18
  39.1 1.9 %all-to-all-done = bf16[16,64,1024]{2,1,0:T(8,128)(2,1)S(1)} async-done(((bf16[16,64,1024]{2,1,0:T(8,128)(2,1)}), bf16[16,64,1024]{2,1,0:T(8,128)(2,1)S(1)}, u32[]{:S(2)}, u32[]{:S(2)}) %all-to-all-start) | async-done | bytes 2097184 | tf_op jit(solution)/shard_map/all_to_all | solution.py:414
  41.0 1.3 copy-done.1
  42.3 7.9 %stats.1 = (f32[1024,1024]{1,0:T(8,128)}, bf16[1024,1024]{1,0:T(8,128)(2,1)}, f32[16,8,128]{2,1,0:T(8,128)}, f32[8,8,128]{2,1,0:T(8,128)}) custom-call(bf16[1024,1024]{1,0:T(8,128)(2,1)} %bitcast.3, s32[128,128]{1,0:T(8,128)} %bitcast.7, bf16[64,1024]{1,0:T(8,128)(2,1)} %refs_0_.1, bf16[64,1024]{1,0:T(8,128)(2,1)} %copy-done.5, bf16[64,1024]{1,0:T(8,128)(2,1)} %copy-done.7, ...), custom_call_target="tpu_custom_call" | custom-call | flops 2147483648 | bytes 8388608 | tf_op jit(solution)/shard_map/stats/pallas_call | solution.py:212
  50.2 16.5 %all_to_all.20.col_parts = f32[8,8,128]{2,1,0:T(8,128)S(1)} all-to-all(f32[8,8,128]{2,1,0:T(8,128)} %get-tuple-element.19), channel_id=1, replica_groups=mesh['y'=4,'core'=2,'x'=4,'z'=8] {'z'}, dimensions={0} | all-to-all | bytes 65536 | tf_op jit(solution)/shard_map/all_to_all | solution.py:426
  66.7 4.8 %all-to-all-start.1 = ((f32[16,8,128]{2,1,0:T(8,128)}), f32[16,8,128]{2,1,0:T(8,128)S(1)}, u32[]{:S(2)}, u32[]{:S(2)}) async-start(f32[16,8,128]{2,1,0:T(8,128)} %get-tuple-element.18), calls=%async_computation.1 | async-start | bytes 131072 | tf_op jit(solution)/shard_map/all_to_all | solution.py:425
  72.0 5.8 %all-to-all-done.1.row_parts = f32[16,8,128]{2,1,0:T(8,128)S(1)} async-done(((f32[16,8,128]{2,1,0:T(8,128)}), f32[16,8,128]{2,1,0:T(8,128)S(1)}, u32[]{:S(2)}, u32[]{:S(2)}) %all-to-all-start.1) | async-done | bytes 65568 | tf_op jit(solution)/shard_map/all_to_all | solution.py:425
  78.4 7.5 %grad.1 = (bf16[1024,1024]{1,0:T(8,128)(2,1)}, bf16[1024,1024]{1,0:T(8,128)(2,1)}) custom-call(f32[1024,1024]{1,0:T(8,128)} %get-tuple-element.16.kept_ref, bf16[1024,1024]{1,0:T(8,128)(2,1)} %get-tuple-element.17.cols_ref, f32[16,8,128]{2,1,0:T(8,128)} %copy-done.2, f32[8,8,128]{2,1,0:T(8,128)} %copy-done.3, f32[8,8,128]{2,1,0:T(8,128)} %copy-done.19), custom_call_target="tpu_custom_call" | custom-call | flops 2147483648 | bytes 12582912 | tf_op jit(solution)/shard_map/grad/pallas_call | solution.py:298
  86.0 5.0 %all-to-all-start.3 = ((bf16[16,64,1024]{2,1,0:T(8,128)(2,1)}), bf16[16,64,1024]{2,1,0:T(8,128)(2,1)S(1)}, u32[]{:S(2)}, u32[]{:S(2)}) async-start(bf16[16,64,1024]{2,1,0:T(8,128)(2,1)} %bitcast.6), calls=%async_computation.3 | async-start | bytes 4194304 | tf_op jit(solution)/shard_map/all_to_all | solution.py:431
  91.1 5.0 %text_terms.1 = (f32[64,1024]{1,0:T(8,128)}, bf16[64,1024]{1,0:T(8,128)(2,1)}, bf16[64,1024]{1,0:T(8,128)(2,1)}, bf16[64,1024]{1,0:T(8,128)(2,1)}, bf16[64,1024]...) custom-call(bf16[1024,1024]{1,0:T(8,128)(2,1)} %get-tuple-element.21.grad_ref, ...), custom_call_target="tpu_custom_call" | custom-call | flops 2147483648 | bytes 8388608 | tf_op jit(solution)/shard_map/text_terms/pallas_call | solution.py:360
  96.1 0.8 collective-permute-start.18
  97.0 3.1 %collective-permute-start.19 = (bf16[64,1024]{1,0:T(8,128)(2,1)}, bf16[64,1024]{1,0:T(8,128)(2,1)S(1)}, u32[]{:S(2)}, u32[]{:S(2)}) collective-permute-start(bf16[64,1024]{1,0:T(8,128)(2,1)} %get-tuple-element.24), channel_id=1, source_target_pairs={{0,3},{1,4},{2,5},{3,6},{4,7},{5,0},{6,1},{7,2},{8,11},{9,12},{10,... | collective-permute-start | bytes 393224 | tf_op jit(solution)/shard_map/ppermute | solution.py:29
  100.1 1.9 %collective-permute-start.20 = (bf16[64,1024]{1,0:T(8,128)(2,1)}, bf16[64,1024]{1,0:T(8,128)(2,1)S(1)}, u32[]{:S(2)}, u32[]{:S(2)}) collective-permute-start(bf16[64,1024]{1,0:T(8,128)(2,1)} %get-tuple-element.25), channel_id=1, source_target_pairs={{0,5},{1,6},{2,7},{3,0},{4,1},{5,2},{6,3},{7,4},{8,13},{9,14},{10,... | collective-permute-start | bytes 393224 | tf_op jit(solution)/shard_map/ppermute | solution.py:29
  102.0 2.4 %collective-permute-start.21 = (bf16[64,1024]{1,0:T(8,128)(2,1)}, bf16[64,1024]{1,0:T(8,128)(2,1)S(1)}, u32[]{:S(2)}, u32[]{:S(2)}) collective-permute-start(bf16[64,1024]{1,0:T(8,128)(2,1)} %get-tuple-element.26), channel_id=1, source_target_pairs={{0,2},{1,3},{2,4},{3,5},{4,6},{5,7},{6,0},{7,1},{8,10},{9,11},{10,... | collective-permute-start | bytes 393224 | tf_op jit(solution)/shard_map/ppermute | solution.py:29
  104.4 1.8 %collective-permute-start.22 = (bf16[64,1024]{1,0:T(8,128)(2,1)}, bf16[64,1024]{1,0:T(8,128)(2,1)S(1)}, u32[]{:S(2)}, u32[]{:S(2)}) collective-permute-start(bf16[64,1024]{1,0:T(8,128)(2,1)} %get-tuple-element.27), channel_id=1, source_target_pairs={{0,6},{1,7},{2,0},{3,1},{4,2},{5,3},{6,4},{7,5},{8,14},{9,15},{10,... | collective-permute-start | bytes 393224 | tf_op jit(solution)/shard_map/ppermute | solution.py:29
  106.1 7.3 %collective-permute-done.18.refs_0_ = bf16[64,1024]{1,0:T(8,128)(2,1)S(1)} collective-permute-done((bf16[64,1024]{1,0:T(8,128)(2,1)}, bf16[64,1024]{1,0:T(8,128)(2,1)S(1)}, u32[]{:S(2)}, u32[]{:S(2)}) %collective-permute-start.18) | collective-permute-done | bytes 131104 | tf_op jit(solution)/shard_map/ppermute | solution.py:29
  113.5 3.9 %collective-permute-done.19.refs_1_ = bf16[64,1024]{1,0:T(8,128)(2,1)S(1)} collective-permute-done((bf16[64,1024]{1,0:T(8,128)(2,1)}, bf16[64,1024]{1,0:T(8,128)(2,1)S(1)}, u32[]{:S(2)}, u32[]{:S(2)}) %collective-permute-start.19) | collective-permute-done | bytes 131104 | tf_op jit(solution)/shard_map/ppermute | solution.py:29
  117.4 1.7 %collective-permute-start.24 = (bf16[64,1024]{1,0:T(8,128)(2,1)}, bf16[64,1024]{1,0:T(8,128)(2,1)S(1)}, u32[]{:S(2)}, u32[]{:S(2)}) collective-permute-start(bf16[64,1024]{1,0:T(8,128)(2,1)} %get-tuple-element.29), channel_id=1, source_target_pairs={{0,7},{1,0},{2,1},{3,2},{4,3},{5,4},{6,5},{7,6},{8,15},{9,8},{10,9... | collective-permute-start | bytes 393224 | tf_op jit(solution)/shard_map/ppermute | solution.py:29
  119.1 5.1 %all-to-all-done.3.image_parts = bf16[16,64,1024]{2,1,0:T(8,128)(2,1)S(1)} async-done(((bf16[16,64,1024]{2,1,0:T(8,128)(2,1)}), bf16[16,64,1024]{2,1,0:T(8,128)(2,1)S(1)}, u32[]{:S(2)}, u32[]{:S(2)}) %all-to-all-start.3) | async-done | bytes 2097184 | tf_op jit(solution)/shard_map/all_to_all | solution.py:431
  124.2 0.9 copy-done
  125.2 1.2 sums.1
  (70 shorter events, 3.3 us)
Async XLA Ops:
  3.0 37.9 %all-to-all-start = ((bf16[16,64,1024]{2,1,0:T(8,128)(2,1)}), bf16[16,64,1024]{2,1,0:T(8,128)(2,1)S(1)}, u32[]{:S(2)}, u32[]{:S(2)}) async-start(bf16[16,64,1024]{2,1,0:T(8,128)(2,1)} %repeat.1), calls=%async_computation | async-start | bytes 4194304 | tf_op jit(solution)/shard_map/all_to_all | solution.py:414
  10.6 8.5 %collective-permute-start = (bf16[64,1024]{1,0:T(8,128)(2,1)S(1)}, bf16[64,1024]{1,0:T(8,128)(2,1)S(1)}, u32[]{:S(2)}, u32[]{:S(2)}) collective-permute-start(bf16[64,1024]{1,0:T(8,128)(2,1)S(1)} %copy-done.4), channel_id=1, source_target_pairs={{0,7},{1,0},{2,1},{3,2},{4,3},{5,4},{6,5},{7,6},{8,15},{9,8},{10,9... | collective-permute-start | bytes 393224 | tf_op jit(solution)/shard_map/ppermute | solution.py:29
  16.5 6.2 %collective-permute-start.4 = (bf16[64,1024]{1,0:T(8,128)(2,1)S(1)}, bf16[64,1024]{1,0:T(8,128)(2,1)S(1)}, u32[]{:S(2)}, u32[]{:S(2)}) collective-permute-start(bf16[64,1024]{1,0:T(8,128)(2,1)S(1)} %copy-done.4), channel_id=1, source_target_pairs={{0,1},{1,2},{2,3},{3,4},{4,5},{5,6},{6,7},{7,0},{8,9},{9,10},{10,1... | collective-permute-start | bytes 393224 | tf_op jit(solution)/shard_map/ppermute | solution.py:29
  19.0 21.9 %copy-start.5 = (bf16[64,1024]{1,0:T(8,128)(2,1)}, bf16[64,1024]{1,0:T(8,128)(2,1)S(1)}, u32[]{:S(2)}) copy-start(bf16[64,1024]{1,0:T(8,128)(2,1)S(1)} %collective-permute-done.refs_1_) | copy-start | bytes 393220
  19.0 6.2 %collective-permute-start.1 = (bf16[64,1024]{1,0:T(8,128)(2,1)S(1)}, bf16[64,1024]{1,0:T(8,128)(2,1)S(1)}, u32[]{:S(2)}, u32[]{:S(2)}) collective-permute-start(bf16[64,1024]{1,0:T(8,128)(2,1)S(1)} %collective-permute-done.refs_1_), channel_id=1, source_target_pairs={{0,7},{1,0},{2,1},{3,2},{4,3},{5,4},{6,5},{7,6},{8,15},{9,8},{10,9... | collective-permute-start | bytes 393224 | tf_op jit(solution)/shard_map/ppermute | solution.py:29
  22.7 18.3 %copy-start.6 = (bf16[64,1024]{1,0:T(8,128)(2,1)}, bf16[64,1024]{1,0:T(8,128)(2,1)S(1)}, u32[]{:S(2)}) copy-start(bf16[64,1024]{1,0:T(8,128)(2,1)S(1)} %collective-permute-done.4.refs_7_) | copy-start | bytes 393220
  22.7 6.7 %collective-permute-start.5 = (bf16[64,1024]{1,0:T(8,128)(2,1)S(1)}, bf16[64,1024]{1,0:T(8,128)(2,1)S(1)}, u32[]{:S(2)}, u32[]{:S(2)}) collective-permute-start(bf16[64,1024]{1,0:T(8,128)(2,1)S(1)} %collective-permute-done.4.refs_7_), channel_id=1, source_target_pairs={{0,1},{1,2},{2,3},{3,4},{4,5},{5,6},{6,7},{7,0},{8,9},{9,10},{10,1... | collective-permute-start | bytes 393224 | tf_op jit(solution)/shard_map/ppermute | solution.py:29
  25.2 15.7 %copy-start.7 = (bf16[64,1024]{1,0:T(8,128)(2,1)}, bf16[64,1024]{1,0:T(8,128)(2,1)S(1)}, u32[]{:S(2)}) copy-start(bf16[64,1024]{1,0:T(8,128)(2,1)S(1)} %collective-permute-done.1.refs_2_) | copy-start | bytes 393220
  25.2 6.2 %collective-permute-start.2 = (bf16[64,1024]{1,0:T(8,128)(2,1)S(1)}, bf16[64,1024]{1,0:T(8,128)(2,1)S(1)}, u32[]{:S(2)}, u32[]{:S(2)}) collective-permute-start(bf16[64,1024]{1,0:T(8,128)(2,1)S(1)} %collective-permute-done.1.refs_2_), channel_id=1, source_target_pairs={{0,7},{1,0},{2,1},{3,2},{4,3},{5,4},{6,5},{7,6},{8,15},{9,8},{10,9... | collective-permute-start | bytes 393224 | tf_op jit(solution)/shard_map/ppermute | solution.py:29
  28.9 6.2 %collective-permute-start.7 = (bf16[64,1024]{1,0:T(8,128)(2,1)S(1)}, bf16[64,1024]{1,0:T(8,128)(2,1)S(1)}, u32[]{:S(2)}, u32[]{:S(2)}) collective-permute-start(bf16[64,1024]{1,0:T(8,128)(2,1)S(1)} %copy-done.4), channel_id=1, source_target_pairs={{0,32},{32,0},{1,33},{33,1},{2,34},{34,2},{3,35},{35,3},{4,36},{36... | collective-permute-start | bytes 393224 | tf_op jit(solution)/shard_map/ppermute | solution.py:24
  28.9 6.2 %collective-permute-start.14 = (bf16[64,1024]{1,0:T(8,128)(2,1)S(1)}, bf16[64,1024]{1,0:T(8,128)(2,1)S(1)}, u32[]{:S(2)}, u32[]{:S(2)}) collective-permute-start(bf16[64,1024]{1,0:T(8,128)(2,1)S(1)} %collective-permute-done.4.refs_7_), channel_id=1, source_target_pairs={{0,32},{32,0},{1,33},{33,1},{2,34},{34,2},{3,35},{35,3},{4,36},{36... | collective-permute-start | bytes 393224 | tf_op jit(solution)/shard_map/ppermute | solution.py:24
  29.4 6.2 %collective-permute-start.8 = (bf16[64,1024]{1,0:T(8,128)(2,1)S(1)}, bf16[64,1024]{1,0:T(8,128)(2,1)S(1)}, u32[]{:S(2)}, u32[]{:S(2)}) collective-permute-start(bf16[64,1024]{1,0:T(8,128)(2,1)S(1)} %collective-permute-done.refs_1_), channel_id=1, source_target_pairs={{0,32},{32,0},{1,33},{33,1},{2,34},{34,2},{3,35},{35,3},{4,36},{36... | collective-permute-start | bytes 393224 | tf_op jit(solution)/shard_map/ppermute | solution.py:24
  29.4 11.6 %copy-start.8 = (bf16[64,1024]{1,0:T(8,128)(2,1)}, bf16[64,1024]{1,0:T(8,128)(2,1)S(1)}, u32[]{:S(2)}) copy-start(bf16[64,1024]{1,0:T(8,128)(2,1)S(1)} %collective-permute-done.5.refs_6_) | copy-start | bytes 393220
  29.4 7.1 %collective-permute-start.6 = (bf16[64,1024]{1,0:T(8,128)(2,1)S(1)}, bf16[64,1024]{1,0:T(8,128)(2,1)S(1)}, u32[]{:S(2)}, u32[]{:S(2)}) collective-permute-start(bf16[64,1024]{1,0:T(8,128)(2,1)S(1)} %collective-permute-done.5.refs_6_), channel_id=1, source_target_pairs={{0,1},{1,2},{2,3},{3,4},{4,5},{5,6},{6,7},{7,0},{8,9},{9,10},{10,1... | collective-permute-start | bytes 393224 | tf_op jit(solution)/shard_map/ppermute | solution.py:29
  31.4 6.2 %collective-permute-start.3 = (bf16[64,1024]{1,0:T(8,128)(2,1)S(1)}, bf16[64,1024]{1,0:T(8,128)(2,1)S(1)}, u32[]{:S(2)}, u32[]{:S(2)}) collective-permute-start(bf16[64,1024]{1,0:T(8,128)(2,1)S(1)} %collective-permute-done.2.refs_3_), channel_id=1, source_target_pairs={{0,7},{1,0},{2,1},{3,2},{4,3},{5,4},{6,5},{7,6},{8,15},{9,8},{10,9... | collective-permute-start | bytes 393224 | tf_op jit(solution)/shard_map/ppermute | solution.py:29
  35.1 2.5 %collective-permute-start.13 = (bf16[64,1024]{1,0:T(8,128)(2,1)S(1)}, bf16[64,1024]{1,0:T(8,128)(2,1)S(1)}, u32[]{:S(2)}, u32[]{:S(2)}) collective-permute-start(bf16[64,1024]{1,0:T(8,128)(2,1)S(1)} %collective-permute-done.5.refs_6_), channel_id=1, source_target_pairs={{0,32},{32,0},{1,33},{33,1},{2,34},{34,2},{3,35},{35,3},{4,36},{36... | collective-permute-start | bytes 393224 | tf_op jit(solution)/shard_map/ppermute | solution.py:24
  35.1 2.5 %collective-permute-start.9 = (bf16[64,1024]{1,0:T(8,128)(2,1)S(1)}, bf16[64,1024]{1,0:T(8,128)(2,1)S(1)}, u32[]{:S(2)}, u32[]{:S(2)}) collective-permute-start(bf16[64,1024]{1,0:T(8,128)(2,1)S(1)} %collective-permute-done.1.refs_2_), channel_id=1, source_target_pairs={{0,32},{32,0},{1,33},{33,1},{2,34},{34,2},{3,35},{35,3},{4,36},{36... | collective-permute-start | bytes 393224 | tf_op jit(solution)/shard_map/ppermute | solution.py:24
  35.6 2.0 %collective-permute-start.10 = (bf16[64,1024]{1,0:T(8,128)(2,1)S(1)}, bf16[64,1024]{1,0:T(8,128)(2,1)S(1)}, u32[]{:S(2)}, u32[]{:S(2)}) collective-permute-start(bf16[64,1024]{1,0:T(8,128)(2,1)S(1)} %collective-permute-done.2.refs_3_), channel_id=1, source_target_pairs={{0,32},{32,0},{1,33},{33,1},{2,34},{34,2},{3,35},{35,3},{4,36},{36... | collective-permute-start | bytes 393224 | tf_op jit(solution)/shard_map/ppermute | solution.py:24
  36.5 1.3 %collective-permute-start.12 = (bf16[64,1024]{1,0:T(8,128)(2,1)S(1)}, bf16[64,1024]{1,0:T(8,128)(2,1)S(1)}, u32[]{:S(2)}, u32[]{:S(2)}) collective-permute-start(bf16[64,1024]{1,0:T(8,128)(2,1)S(1)} %collective-permute-done.6.refs_5_), channel_id=1, source_target_pairs={{0,32},{32,0},{1,33},{33,1},{2,34},{34,2},{3,35},{35,3},{4,36},{36... | collective-permute-start | bytes 393224 | tf_op jit(solution)/shard_map/ppermute | solution.py:24
  37.6 1.5 %collective-permute-start.11 = (bf16[64,1024]{1,0:T(8,128)(2,1)S(1)}, bf16[64,1024]{1,0:T(8,128)(2,1)}, u32[]{:S(2)}, u32[]{:S(2)}) collective-permute-start(bf16[64,1024]{1,0:T(8,128)(2,1)S(1)} %collective-permute-done.3.refs_4_), channel_id=1, source_target_pairs={{0,32},{32,0},{1,33},{33,1},{2,34},{34,2},{3,35},{35,3},{4,36},{36... | collective-permute-start | bytes 393224 | tf_op jit(solution)/shard_map/ppermute | solution.py:24
  66.7 11.1 %all-to-all-start.1 = ((f32[16,8,128]{2,1,0:T(8,128)}), f32[16,8,128]{2,1,0:T(8,128)S(1)}, u32[]{:S(2)}, u32[]{:S(2)}) async-start(f32[16,8,128]{2,1,0:T(8,128)} %get-tuple-element.18), calls=%async_computation.1 | async-start | bytes 131072 | tf_op jit(solution)/shard_map/all_to_all | solution.py:425
  71.5 6.3 %collective-permute-start.15 = (f32[8,8,128]{2,1,0:T(8,128)S(1)}, f32[8,8,128]{2,1,0:T(8,128)S(1)}, u32[]{:S(2)}, u32[]{:S(2)}) collective-permute-start(f32[8,8,128]{2,1,0:T(8,128)S(1)} %all_to_all.20.col_parts), channel_id=1, source_target_pairs={{0,32},{32,0},{1,33},{33,1},{2,34},{34,2},{3,35},{35,3},{4,36},{36... | collective-permute-start | bytes 98312 | tf_op jit(solution)/shard_map/ppermute | solution.py:24
  71.5 19.6 %collective-permute-start.17 = (bf16[1024,1024]{1,0:T(8,128)(2,1)}, bf16[1024,1024]{1,0:T(8,128)(2,1)}, u32[]{:S(2)}, u32[]{:S(2)}) collective-permute-start(bf16[1024,1024]{1,0:T(8,128)(2,1)} %bitcast.4), channel_id=1, source_target_pairs={{0,32},{32,0},{1,33},{33,1},{2,34},{34,2},{3,35},{35,3},{4,36},{36... | collective-permute-start | bytes 6291464 | tf_op jit(solution)/shard_map/ppermute | solution.py:24
  85.9 5.2 %collective-permute-start.16 = (bf16[1024,1024]{1,0:T(8,128)(2,1)}, bf16[1024,1024]{1,0:T(8,128)(2,1)}, u32[]{:S(2)}, u32[]{:S(2)}) collective-permute-start(bf16[1024,1024]{1,0:T(8,128)(2,1)} %get-tuple-element.21.grad_ref), channel_id=1, source_target_pairs={{0,32},{32,0},{1,33},{33,1},{2,34},{34,2},{3,35},{35,3},{4,36},{36... | collective-permute-start | bytes 6291464 | tf_op jit(solution)/shard_map/ppermute | solution.py:24
  86.0 38.1 %all-to-all-start.3 = ((bf16[16,64,1024]{2,1,0:T(8,128)(2,1)}), bf16[16,64,1024]{2,1,0:T(8,128)(2,1)S(1)}, u32[]{:S(2)}, u32[]{:S(2)}) async-start(bf16[16,64,1024]{2,1,0:T(8,128)(2,1)} %bitcast.6), calls=%async_computation.3 | async-start | bytes 4194304 | tf_op jit(solution)/shard_map/all_to_all | solution.py:431
  96.1 17.3 %collective-permute-start.18 = (bf16[64,1024]{1,0:T(8,128)(2,1)}, bf16[64,1024]{1,0:T(8,128)(2,1)S(1)}, u32[]{:S(2)}, u32[]{:S(2)}) collective-permute-start(bf16[64,1024]{1,0:T(8,128)(2,1)} %get-tuple-element.23), channel_id=1, source_target_pairs={{0,4},{1,5},{2,6},{3,7},{4,0},{5,1},{6,2},{7,3},{8,12},{9,13},{10,... | collective-permute-start | bytes 393224 | tf_op jit(solution)/shard_map/ppermute | solution.py:29
  97.0 20.4 %collective-permute-start.19 = (bf16[64,1024]{1,0:T(8,128)(2,1)}, bf16[64,1024]{1,0:T(8,128)(2,1)S(1)}, u32[]{:S(2)}, u32[]{:S(2)}) collective-permute-start(bf16[64,1024]{1,0:T(8,128)(2,1)} %get-tuple-element.24), channel_id=1, source_target_pairs={{0,3},{1,4},{2,5},{3,6},{4,7},{5,0},{6,1},{7,2},{8,11},{9,12},{10,... | collective-permute-start | bytes 393224 | tf_op jit(solution)/shard_map/ppermute | solution.py:29
  100.1 24.1 %collective-permute-start.20 = (bf16[64,1024]{1,0:T(8,128)(2,1)}, bf16[64,1024]{1,0:T(8,128)(2,1)S(1)}, u32[]{:S(2)}, u32[]{:S(2)}) collective-permute-start(bf16[64,1024]{1,0:T(8,128)(2,1)} %get-tuple-element.25), channel_id=1, source_target_pairs={{0,5},{1,6},{2,7},{3,0},{4,1},{5,2},{6,3},{7,4},{8,13},{9,14},{10,... | collective-permute-start | bytes 393224 | tf_op jit(solution)/shard_map/ppermute | solution.py:29
  102.0 22.2 %collective-permute-start.21 = (bf16[64,1024]{1,0:T(8,128)(2,1)}, bf16[64,1024]{1,0:T(8,128)(2,1)S(1)}, u32[]{:S(2)}, u32[]{:S(2)}) collective-permute-start(bf16[64,1024]{1,0:T(8,128)(2,1)} %get-tuple-element.26), channel_id=1, source_target_pairs={{0,2},{1,3},{2,4},{3,5},{4,6},{5,7},{6,0},{7,1},{8,10},{9,11},{10,... | collective-permute-start | bytes 393224 | tf_op jit(solution)/shard_map/ppermute | solution.py:29
  104.4 19.8 %collective-permute-start.22 = (bf16[64,1024]{1,0:T(8,128)(2,1)}, bf16[64,1024]{1,0:T(8,128)(2,1)S(1)}, u32[]{:S(2)}, u32[]{:S(2)}) collective-permute-start(bf16[64,1024]{1,0:T(8,128)(2,1)} %get-tuple-element.27), channel_id=1, source_target_pairs={{0,6},{1,7},{2,0},{3,1},{4,2},{5,3},{6,4},{7,5},{8,14},{9,15},{10,... | collective-permute-start | bytes 393224 | tf_op jit(solution)/shard_map/ppermute | solution.py:29
  113.5 10.7 %collective-permute-start.23 = (bf16[64,1024]{1,0:T(8,128)(2,1)}, bf16[64,1024]{1,0:T(8,128)(2,1)S(1)}, u32[]{:S(2)}, u32[]{:S(2)}) collective-permute-start(bf16[64,1024]{1,0:T(8,128)(2,1)} %get-tuple-element.28), channel_id=1, source_target_pairs={{0,1},{1,2},{2,3},{3,4},{4,5},{5,6},{6,7},{7,0},{8,9},{9,10},{10,1... | collective-permute-start | bytes 393224 | tf_op jit(solution)/shard_map/ppermute | solution.py:29
  117.4 6.8 %collective-permute-start.24 = (bf16[64,1024]{1,0:T(8,128)(2,1)}, bf16[64,1024]{1,0:T(8,128)(2,1)S(1)}, u32[]{:S(2)}, u32[]{:S(2)}) collective-permute-start(bf16[64,1024]{1,0:T(8,128)(2,1)} %get-tuple-element.29), channel_id=1, source_target_pairs={{0,7},{1,0},{2,1},{3,2},{4,3},{5,4},{6,5},{7,6},{8,15},{9,8},{10,9... | collective-permute-start | bytes 393224 | tf_op jit(solution)/shard_map/ppermute | solution.py:29
  (16 other events, 62.5 us)

commit v4 on v3

--- a/solution.py
+++ b/solution.py
@@ -70,7 +70,7 @@
 
 
 def params(megabytes):
-    return pltpu.CompilerParams(vmem_limit_bytes=megabytes * mib)
+    return pltpu.CompilerParams(vmem_limit_bytes=int(megabytes * mib))
 
 
 def here_in_mesh():
@@ -145,28 +145,30 @@
 
 
 def stats_kernel(rows, group_ref, *refs):
-    shards, (kept_ref, cols_ref, row_ref, col_ref, kept_all, cols, groups, sems) = refs[:-8], refs[-8:]
+    shards, (near_ref, far_ref, cols_ref, rows_ref, row_ref, col_ref, kept_all, cols, groups, sems) = refs[:-10], refs[-10:]
     where = here_in_mesh()
-    n_rows, n_cols = kept_ref.shape
+    n_rows, n_cols = kept_all.shape
     half = n_cols // 2
     n_blocks = n_rows // block
     n_z = len(shards) // 2
     span = half // n_z
 
-    stores = [
-        pltpu.make_async_copy(
-            kept_all.at[pl.ds(i * block, block), :], kept_ref.at[pl.ds(i * block, block), :], sems.at[i]
-        )
-        for i in range(n_blocks)
-    ]
-    cols_store = pltpu.make_async_copy(cols, cols_ref, sems.at[n_blocks])
-    group_load = pltpu.make_async_copy(group_ref, groups, sems.at[n_blocks + 1])
+    stores = []
+    for i in range(n_blocks):
+        for side, ref in enumerate((near_ref, far_ref)):
+            here = pl.ds(i * block, block)
+            there = pl.ds(side * half, half)
+            stores.append(pltpu.make_async_copy(kept_all.at[here, there], ref.at[here, :], sems.at[2 * i + side]))
+    cols_store = pltpu.make_async_copy(cols, cols_ref, sems.at[2 * n_blocks])
+    group_load = pltpu.make_async_copy(group_ref, groups, sems.at[2 * n_blocks + 1])
     group_load.start()
+    rows_store = pltpu.make_async_copy(rows, rows_ref, sems.at[2 * n_blocks + 2])
     for side in range(2):
         for k in range(n_z):
             at = pl.multiple_of(side * half + lax.rem(where[3] + k, n_z) * span, span)
             cols[pl.ds(at, span), :] = shards[side * n_z + k][...]
     cols_store.start()
+    rows_store.start()
     kept_all[:block, :] = scale_base2 * contract(rows[:block, :], cols[...], 1, 1)
     group_load.wait()
     row_groups, col_groups = group_rows(where, groups)
@@ -181,7 +183,8 @@
         scores = scale_base2 * contract(rows[here, :], cols[...], 1, 1) if i else kept_all[here, :]
         valid = jnp.logical_or(rg != cg, ri == ci)
         kept_all[here, :] = jnp.where(valid, scores, floor_value)
-        stores[i].start()
+        stores[2 * i].start()
+        stores[2 * i + 1].start()
 
     peak = jnp.full((1, n_cols), floor_value, jnp.float32)
     total = jnp.zeros((1, n_cols), jnp.float32)
@@ -194,38 +197,38 @@
         row_total = jnp.sum(jnp.exp2(kept - row_peak), axis=1, keepdims=True)
         row_lse = fold(as_row(row_peak + jnp.log2(row_total)))
         for j in range(block // lanes):
-            row_ref[:, i * block // lanes + j : i * block // lanes + j + 1, :] = jnp.broadcast_to(
-                row_lse[None, j : j + 1, :], (row_ref.shape[0], 1, lanes)
-            )
+            row_ref[i * block // lanes + j : i * block // lanes + j + 1, :] = row_lse[j : j + 1, :]
         top = jnp.maximum(peak, jnp.max(kept, axis=0, keepdims=True))
         total = total * jnp.exp2(peak - top) + jnp.sum(jnp.exp2(kept - top), axis=0, keepdims=True)
         peak = top
     col_lse = by_core(fold(peak + jnp.log2(total)), where[1])
     col_ref[...] = jnp.broadcast_to(col_lse[None], col_ref.shape)
-    for copy in (cols_store, *stores):
+    for copy in (cols_store, rows_store, *stores):
         copy.wait()
 
 
-def block_stats(rows, groups, shards, n_row, n_col):
+def block_stats(rows, groups, shards, n_col):
     n_rows, width = rows.shape
     n_cols = len(shards) * shards[0].shape[0]
     return pl.pallas_call(
         stats_kernel,
         in_specs=[in_vmem, in_hbm] + [in_vmem] * len(shards),
-        out_specs=[in_hbm, in_hbm, in_vmem, in_vmem],
+        out_specs=[in_hbm, in_hbm, in_hbm, in_hbm, in_vmem, in_vmem],
         out_shape=[
-            jax.ShapeDtypeStruct((n_rows, n_cols), jnp.float32),
+            jax.ShapeDtypeStruct((n_rows, n_cols // 2), jnp.float32),
+            jax.ShapeDtypeStruct((n_rows, n_cols // 2), jnp.float32),
             jax.ShapeDtypeStruct((n_cols, width), jnp.bfloat16),
-            jax.ShapeDtypeStruct((n_row, n_rows // lanes, lanes), jnp.float32),
+            jax.ShapeDtypeStruct((n_rows, width), jnp.bfloat16),
+            jax.ShapeDtypeStruct((n_rows // lanes, lanes), jnp.float32),
             jax.ShapeDtypeStruct((n_col, n_cols // lanes, lanes), jnp.float32),
         ],
         scratch_shapes=[
             pltpu.VMEM((n_rows, n_cols), jnp.float32),
             pltpu.VMEM((n_cols, width), jnp.bfloat16),
             pltpu.VMEM(groups.shape, groups.dtype),
-            pltpu.SemaphoreType.DMA((n_rows // block + 2,)),
+            pltpu.SemaphoreType.DMA((2 * (n_rows // block) + 3,)),
         ],
-        compiler_params=params(55),
+        compiler_params=params(50),
         cost_estimate=estimate(2 * n_rows * n_cols * width, 8, 2 * n_rows * n_cols),
         name="stats",
     )(rows, groups, *shards)
@@ -241,138 +244,118 @@
     return top + jnp.log2(total)
 
 
-def grad_kernel(kept_ref, cols_ref, row_parts, col_parts, col_others, image_ref, grad_ref, kept_all, cols, grads, image, sems):
-    where = here_in_mesh()
-    n_rows, n_cols = kept_ref.shape
+def grad_kernel(near_ref, far_ref, other_ref, cols_ref, rows_ref, other_rows_ref, row_parts, col_parts, col_others, image_ref, own_ref, *refs):
+    sent, (kept, other, cols, rows, grads, other_grads, image, total, sems) = refs[:-9], refs[-9:]
+    y, core, x, z = here_in_mesh()
+    n_rows, n_cols = kept.shape
+    half = n_cols // 2
     n_blocks = n_rows // block
-    span = 64
+    n_z = len(sent) + 1
+    span = half // n_z
+    per = block // lanes
 
     def piece(i):
         return pl.ds(i * block, block)
 
-    kept_loads = [
-        pltpu.make_async_copy(kept_ref.at[piece(i), :], kept_all.at[piece(i), :], sems.at[i]) for i in range(n_blocks)
-    ]
-    cols_load = pltpu.make_async_copy(cols_ref, cols, sems.at[n_blocks])
+    loads = []
+    for i in range(n_blocks):
+        for side, ref in enumerate((near_ref, far_ref)):
+            there = kept.at[piece(i), pl.ds(side * half, half)]
+            loads.append(pltpu.make_async_copy(ref.at[piece(i), :], there, sems.at[2 * i + side]))
+    at = 2 * n_blocks
+    cols_load = pltpu.make_async_copy(cols_ref, cols, sems.at[at])
+    other_load = pltpu.make_async_copy(other_ref, other, sems.at[at + 1])
+    rows_load = pltpu.make_async_copy(rows_ref, rows.at[0], sems.at[at + 2])
+    other_rows_load = pltpu.make_async_copy(other_rows_ref, rows.at[1], sems.at[at + 3])
     image_stores = [
-        pltpu.make_async_copy(image.at[piece(i), :], image_ref.at[piece(i), :], sems.at[n_blocks + 1 + i])
+        pltpu.make_async_copy(image.at[piece(i), :], image_ref.at[piece(i), :], sems.at[at + 4 + i])
         for i in range(n_blocks)
     ]
-    grad_stores = [
-        pltpu.make_async_copy(grads.at[piece(i), :], grad_ref.at[piece(i), :], sems.at[2 * n_blocks + 1 + i])
-        for i in range(n_blocks)
-    ]
-    for copy in (kept_loads[0], cols_load, *kept_loads[1:]):
+    for copy in (*loads[:2], cols_load, *loads[2:], rows_load, other_load, other_rows_load):
         copy.start()
-    ci = col_ids(where, n_cols, span)
-    row_lse = merge([row_parts[i] for i in range(row_parts.shape[0])])
-    col_lse = unfold(by_core(merge([ref[i] for ref in (col_parts, col_others) for i in range(ref.shape[0])]), where[1]))
+    ci = col_ids((y, core, x, z), n_cols, span)
+    row_lse = merge([row_parts[i, 0] for i in range(row_parts.shape[0])])
+    other_lse = merge([row_parts[i, 1] for i in range(row_parts.shape[0])])
+    col_lse = merge([ref[i] for ref in (col_parts, col_others) for i in range(ref.shape[0])])
+    col_lse = unfold(by_core(col_lse, core))
+
+    def gradient(logits, i, side, lse_tile, ci, col_lse):
+        ri = row_ids((y, side, x, z), i * block, block, span)
+        lse = as_column(unfold(lse_tile[i * per : (i + 1) * per, :]))
+        weight = jnp.exp2(logits - lse) + jnp.exp2(logits - col_lse)
+        grad = 0.5 * weight - jnp.where(ri == ci, 1.0, 0.0)
+        return grad.astype(jnp.bfloat16)
 
     def fill(i):
         here = slice(i * block, (i + 1) * block)
-        ri = row_ids(where, i * block, block, span)
-        lse = as_column(unfold(row_lse[i * block // lanes : (i + 1) * block // lanes, :]))
-        kept = kept_all[here, :]
-        weight = jnp.exp2(kept - lse) + jnp.exp2(kept - col_lse)
-        grad = 0.5 * weight - jnp.where(ri == ci, 1.0, 0.0)
-        grads[here, :] = grad.astype(jnp.bfloat16)
-
-    kept_loads[0].wait()
+        grads[here, :] = gradient(kept[here, :], i, core, row_lse, ci, col_lse)
+
+    def fill_other(i):
+        here = slice(i * block, (i + 1) * block)
+        other_grads[here, :] = gradient(other[here, :], i, 1 - core, other_lse, ci[:, :half], col_lse[:, :half])
+
+    loads[0].wait()
+    loads[1].wait()
     fill(0)
     cols_load.wait()
     for i in range(n_blocks):
         if i + 1 < n_blocks:
-            kept_loads[i + 1].wait()
+            loads[2 * i + 2].wait()
+            loads[2 * i + 3].wait()
             fill(i + 1)
         here = slice(i * block, (i + 1) * block)
         image[here, :] = contract(grads[here, :], cols[...], 1, 0).astype(jnp.bfloat16)
         image_stores[i].start()
-        grad_stores[i].start()
-    for copy in (*image_stores, *grad_stores):
-        copy.wait()
-
-
-def block_grad(kept, cols, row_parts, col_parts, col_others):
-    n_rows, n_cols = kept.shape
-    width = cols.shape[1]
-    return pl.pallas_call(
-        grad_kernel,
-        in_specs=[in_hbm] * 2 + [in_vmem] * 3,
-        out_specs=[in_hbm] * 2,
-        out_shape=[
-            jax.ShapeDtypeStruct((n_rows, width), jnp.bfloat16),
-            jax.ShapeDtypeStruct((n_rows, n_cols), jnp.bfloat16),
-        ],
-        scratch_shapes=[
-            pltpu.VMEM((n_rows, n_cols), jnp.float32),
-            pltpu.VMEM((n_cols, width), jnp.bfloat16),
-            pltpu.VMEM((n_rows, n_cols), jnp.bfloat16),
-            pltpu.VMEM((n_rows, width), jnp.bfloat16),
-            pltpu.SemaphoreType.DMA((3 * (n_rows // block) + 1,)),
-        ],
-        compiler_params=params(60),
-        cost_estimate=estimate(2 * n_rows * n_cols * width, 12, 2 * n_rows * n_cols),
-        name="grad",
-    )(kept, cols, row_parts, col_parts, col_others)
-
-
-def text_kernel(grad_ref, rows_ref, other_ref, other_rows_ref, own_ref, *refs):
-    n_z = len(refs) - 3
-    sent, (grads, rows, total, sems) = refs[: n_z - 1], refs[n_z - 1 :]
-    n_cols = total.shape[0]
-    span = n_cols // n_z
-    depth = rows_ref.shape[0] // 2
-    parts = [(i, j) for i in range(2) for j in range(2)]
-    loads = {}
-    for i, j in parts:
-        here = pl.ds(j * depth, depth)
-        pair = ((grad_ref, rows_ref), (other_ref, other_rows_ref))[i]
-        loads[i, j] = [
-            pltpu.make_async_copy(pair[0].at[here, pl.ds(i * n_cols, n_cols)], grads.at[i, here, :], sems.at[4 * i + 2 * j]),
-            pltpu.make_async_copy(pair[1].at[here, :], rows.at[i, here, :], sems.at[4 * i + 2 * j + 1]),
-        ]
-        for copy in loads[i, j]:
-            copy.start()
-    for i, j in parts:
-        for copy in loads[i, j]:
-            copy.wait()
-        deep = slice(j * depth, (j + 1) * depth)
-        for at in range(0, n_cols, block):
-            here = slice(at, at + block)
-            part = contract(grads[i, deep, here], rows[i, deep, :], 0, 0)
-            if i + j == 0:
-                total[here, :] = part
-            else:
-                total[here, :] += part
+    rows_load.wait()
+    other_load.wait()
+    for i in range(n_blocks):
+        fill_other(i)
+    for i in range(0, half, block):
+        here = slice(i, i + block)
+        total[here, :] = contract(grads[:, here], rows[0], 0, 0)
+    other_rows_load.wait()
+    for i in range(0, half, block):
+        here = slice(i, i + block)
+        total[here, :] += contract(other_grads[:, here], rows[1], 0, 0)
     for k in range(n_z):
-        at = pl.multiple_of(lax.rem(lax.axis_index("z") + k, n_z) * span, span)
-        value = total[pl.ds(at, span), :]
+        value = total[pl.ds(pl.multiple_of(lax.rem(z + k, n_z) * span, span), span), :]
         if k == 0:
             own_ref[...] = value
         else:
             sent[k - 1][...] = value.astype(jnp.bfloat16)
-
-
-def text_terms(grad, rows, other, other_rows, n_z):
-    n_rows, n_cols = grad.shape[0], grad.shape[1] // 2
-    width = rows.shape[1]
-    span = n_cols // n_z
+    for copy in image_stores:
+        copy.wait()
+
+
+def block_grad(near, far, other, cols, rows, other_rows, parts, n_z):
+    n_rows, width = rows.shape
+    half = near.shape[1]
+    n_cols = 2 * half
+    shard = (half // n_z, width)
     return pl.pallas_call(
-        text_kernel,
-        in_specs=[in_hbm] * 4,
-        out_specs=[in_vmem] * n_z,
-        out_shape=[jax.ShapeDtypeStruct((span, width), jnp.float32)]
-        + [jax.ShapeDtypeStruct((span, width), jnp.bfloat16)] * (n_z - 1),
+        grad_kernel,
+        in_specs=[in_hbm] * 6 + [in_vmem] * len(parts),
+        out_specs=[in_hbm] + [in_vmem] * n_z,
+        out_shape=[
+            jax.ShapeDtypeStruct((n_rows, width), jnp.bfloat16),
+            jax.ShapeDtypeStruct(shard, jnp.float32),
+        ]
+        + [jax.ShapeDtypeStruct(shard, jnp.bfloat16)] * (n_z - 1),
         scratch_shapes=[
-            pltpu.VMEM((2, n_rows, n_cols), jnp.bfloat16),
+            pltpu.VMEM((n_rows, n_cols), jnp.float32),
+            pltpu.VMEM((n_rows, half), jnp.float32),
+            pltpu.VMEM((n_cols, width), jnp.bfloat16),
             pltpu.VMEM((2, n_rows, width), jnp.bfloat16),
-            pltpu.VMEM((n_cols, width), jnp.float32),
-            pltpu.SemaphoreType.DMA((8,)),
+            pltpu.VMEM((n_rows, n_cols), jnp.bfloat16),
+            pltpu.VMEM((n_rows, half), jnp.bfloat16),
+            pltpu.VMEM((n_rows, width), jnp.bfloat16),
+            pltpu.VMEM((half, width), jnp.float32),
+            pltpu.SemaphoreType.DMA((3 * (n_rows // block) + 4,)),
         ],
-        compiler_params=params(58),
-        cost_estimate=estimate(4 * n_rows * n_cols * width, 8),
-        name="text_terms",
-    )(grad, rows, other, other_rows)
+        compiler_params=params(53.5),
+        cost_estimate=estimate(4 * n_rows * n_cols * width, 14, 3 * n_rows * n_cols),
+        name="grad",
+    )(near, far, other, cols, rows, other_rows, *parts)
 
 
 def sum_kernel(image_parts, own_ref, *refs):
@@ -421,15 +404,16 @@
     near = [shards[k] for k in range(n_z)]
     far = [swap_core(shard) for shard in near]
 
-    kept, cols, row_part, col_part = block_stats(rows, groups, near + far, n_plane, n_z)
-    row_parts = lax.all_to_all(row_part, plane, 0, 0)
+    near_kept, far_kept, cols, rows, row_part, col_part = block_stats(rows, groups, near + far, n_z)
+    pair = jnp.stack([row_part, swap_core(row_part)])
     col_parts = lax.all_to_all(col_part, "z", 0, 0)
-    col_others = swap_core(col_parts)
+    row_parts = lax.all_to_all(jnp.broadcast_to(pair[None], (n_plane,) + pair.shape), plane, 0, 0)
+    other_kept = swap_core(far_kept)
     other_rows = swap_core(rows)
-
-    image_part, grad = block_grad(kept, cols, row_parts, col_parts, col_others)
+    parts = [row_parts, col_parts, swap_core(col_parts)]
+
+    image_part, own, *sent = block_grad(near_kept, far_kept, other_kept, cols, rows, other_rows, parts, n_z)
     image_parts = lax.all_to_all(image_part.reshape(n_plane, span, width), plane, 0, 0)
-    own, *sent = text_terms(grad, rows, swap_core(grad), other_rows, n_z)
     text_parts = [shift_z(sent[k - 1], k) for k in z_steps(n_z)]
     return tuple(final_sums(image_parts, own, text_parts))
 

time: 129 us -> 123 us (0.953)
  blocking collectives: 16.5 us -> 0 us
  starting transfers between devices: 47.8 us -> 59 us
  waiting for transfers between devices: 33.1 us -> 38.2 us
  Pallas kernels: 24 us -> 21.3 us
  local copies, waits for them, and re-layouts: 4.02 us -> 1.33 us
    all_to_all x1 -> x0, blocking collectives: 16.5 us -> none  [per_device(): col_parts = lax.all_to_all(col_part, 'z', 0, 0)]
    all_to_all x1 -> x2, starting transfers between devices: 4.83 us -> 13.3 us  [the longest x1 8.46 us: per_device(): col_parts = lax.all_to_all(col_part, 'z', 0, 0)]
    all_to_all x1 -> x2, waiting for transfers between devices: 5.75 us -> 13.2 us  [the longest x1 8.01 us: per_device(): col_parts = lax.all_to_all(col_part, 'z', 0, 0)]
    all_to_all x1, waiting for transfers between devices: 5.06 us -> 0.58 us  [per_device(): lax.all_to_all(image_part.reshape(n_plane, span, width), plane, 0, 0)]
    unnamed x40 -> x10, local copies, waits for them, and re-layouts: 4.02 us -> 0.67 us
    ppermute x11 -> x12, waiting for transfers between devices: 0.31 us -> 2.55 us  [swap_core(): return lax.ppermute(values, 'core', [(0, 1), (1, 0)])]
    ppermute x14, starting transfers between devices: 28.7 us -> 30.9 us  [shift(): lax.ppermute(values, axis, [(i, (i + step) % size) for i in range(size)])]
    pallas_call x2 -> x1, Pallas kernels: 12.6 us -> 10.4 us  [block_grad(): pl.pallas_call(grad_kernel, in_specs=[in_hbm] * 6 + [in_vmem] * len(parts...]
  transfers between devices with their start and end apart: 28 -> 30, of which waited for: 11 -> 18; matrix products, arithmetic and copies ran while one was open for 0% -> 1% of each run, Pallas kernels for 10% -> 0%
where the time goes in v4:
time: 123 us; the launch traced here: 121 us
  starting transfers between devices  59 us (48%)
  waiting for transfers between devices  38.2 us (31%)
  Pallas kernels  21.3 us (17%)
  local copies, waits for them, and re-layouts  1.33 us (1%)
    ppermute x14, starting transfers between devices, shift(): lax.ppermute(values, axis, [(i, (i + step) % size) for i in range(size)])  30.9 us
    ppermute x14, waiting for transfers between devices, shift(): lax.ppermute(values, axis, [(i, (i + step) % size) for i in range(size)])  19.8 us
    pallas_call x1, Pallas kernels, block_grad(): pl.pallas_call(grad_kernel, in_specs=[in_hbm] * 6 + [in_vmem] * len(parts...  10.4 us
    all_to_all x1, starting transfers between devices, per_device(): col_parts = lax.all_to_all(col_part, 'z', 0, 0)  8.46 us
    all_to_all x1, waiting for transfers between devices, per_device(): col_parts = lax.all_to_all(col_part, 'z', 0, 0)  8.01 us
    all_to_all x1, starting transfers between devices, per_device(): rows = lax.all_to_all(repeat(image_emb, n_plane), plane, 0, 0)  7.54 us
    pallas_call x1, Pallas kernels, block_stats(): pl.pallas_call(stats_kernel, in_specs=[in_vmem, in_hbm] + [in_vmem] * len...  7.3 us
    all_to_all x1, starting transfers between devices, per_device(): lax.all_to_all(image_part.reshape(n_plane, span, width), plane, 0, 0)  5.38 us
  transfers between devices with their start and end apart: 30, of which 18 were waited for; matrix products, arithmetic and copies ran while one was open for 1% of the time, Pallas kernels for 0%

profile of v4, /device:TPU:8, one launch (start us, length us, event | category | flops | bytes accessed | tf_op | source)
XLA Modules:
  0.0 120.8 jit_solution(11075922271257640978)
XLA Ops:
  0.6 2.4 %repeat.1 = bf16[16,64,1024]{2,1,0:T(8,128)(2,1)} custom-call(bf16[64,1024]{1,0:T(8,128)(2,1)} %in_ref.1), custom_call_target="tpu_custom_call" | custom-call | bytes 2097152 | tf_op jit(solution)/shard_map/repeat/pallas_call | solution.py:135
  3.1 7.5 %all-to-all-start = ((bf16[16,64,1024]{2,1,0:T(8,128)(2,1)}), bf16[16,64,1024]{2,1,0:T(8,128)(2,1)}, u32[]{:S(2)}, u32[]{:S(2)}) async-start(bf16[16,64,1024]{2,1,0:T(8,128)(2,1)} %repeat.1), calls=%async_computation | async-start | bytes 4194304 | tf_op jit(solution)/shard_map/all_to_all | solution.py:397
  10.6 5.9 %collective-permute-start = (bf16[64,1024]{1,0:T(8,128)(2,1)S(1)}, bf16[64,1024]{1,0:T(8,128)(2,1)S(1)}, u32[]{:S(2)}, u32[]{:S(2)}) collective-permute-start(bf16[64,1024]{1,0:T(8,128)(2,1)S(1)} %copy-done.1), channel_id=1, source_target_pairs={{0,7},{1,0},{2,1},{3,2},{4,3},{5,4},{6,5},{7,6},{8,15},{9,8},{10,9... | collective-permute-start | bytes 393224 | tf_op jit(solution)/shard_map/ppermute | solution.py:29
  16.6 2.5 %collective-permute-done.refs_1_ = bf16[64,1024]{1,0:T(8,128)(2,1)S(1)} collective-permute-done((bf16[64,1024]{1,0:T(8,128)(2,1)S(1)}, bf16[64,1024]{1,0:T(8,128)(2,1)S(1)}, u32[]{:S(2)}, u32[]{:S(2)}) %collective-permute-start) | collective-permute-done | bytes 131104 | tf_op jit(solution)/shard_map/ppermute | solution.py:29
  19.1 3.7 %collective-permute-start.1 = (bf16[64,1024]{1,0:T(8,128)(2,1)S(1)}, bf16[64,1024]{1,0:T(8,128)(2,1)S(1)}, u32[]{:S(2)}, u32[]{:S(2)}) collective-permute-start(bf16[64,1024]{1,0:T(8,128)(2,1)S(1)} %collective-permute-done.refs_1_), channel_id=1, source_target_pairs={{0,7},{1,0},{2,1},{3,2},{4,3},{5,4},{6,5},{7,6},{8,15},{9,8},{10,9... | collective-permute-start | bytes 393224 | tf_op jit(solution)/shard_map/ppermute | solution.py:29
  22.7 2.5 %collective-permute-done.1.refs_2_ = bf16[64,1024]{1,0:T(8,128)(2,1)S(1)} collective-permute-done((bf16[64,1024]{1,0:T(8,128)(2,1)S(1)}, bf16[64,1024]{1,0:T(8,128)(2,1)S(1)}, u32[]{:S(2)}, u32[]{:S(2)}) %collective-permute-start.1) | collective-permute-done | bytes 131104 | tf_op jit(solution)/shard_map/ppermute | solution.py:29
  25.2 3.7 %collective-permute-start.2 = (bf16[64,1024]{1,0:T(8,128)(2,1)S(1)}, bf16[64,1024]{1,0:T(8,128)(2,1)S(1)}, u32[]{:S(2)}, u32[]{:S(2)}) collective-permute-start(bf16[64,1024]{1,0:T(8,128)(2,1)S(1)} %collective-permute-done.1.refs_2_), channel_id=1, source_target_pairs={{0,7},{1,0},{2,1},{3,2},{4,3},{5,4},{6,5},{7,6},{8,15},{9,8},{10,9... | collective-permute-start | bytes 393224 | tf_op jit(solution)/shard_map/ppermute | solution.py:29
  29.4 2.0 %collective-permute-done.2.refs_3_ = bf16[64,1024]{1,0:T(8,128)(2,1)S(1)} collective-permute-done((bf16[64,1024]{1,0:T(8,128)(2,1)S(1)}, bf16[64,1024]{1,0:T(8,128)(2,1)S(1)}, u32[]{:S(2)}, u32[]{:S(2)}) %collective-permute-start.2) | collective-permute-done | bytes 131104 | tf_op jit(solution)/shard_map/ppermute | solution.py:29
  31.4 3.7 %collective-permute-start.3 = (bf16[64,1024]{1,0:T(8,128)(2,1)S(1)}, bf16[64,1024]{1,0:T(8,128)(2,1)S(1)}, u32[]{:S(2)}, u32[]{:S(2)}) collective-permute-start(bf16[64,1024]{1,0:T(8,128)(2,1)S(1)} %collective-permute-done.2.refs_3_), channel_id=1, source_target_pairs={{0,7},{1,0},{2,1},{3,2},{4,3},{5,4},{6,5},{7,6},{8,15},{9,8},{10,9... | collective-permute-start | bytes 393224 | tf_op jit(solution)/shard_map/ppermute | solution.py:29
  35.7 0.8 collective-permute-done.6.refs_5_
  36.5 1.1 collective-permute-done.3.refs_4_
  37.9 1.1 collective-permute-done.11.refs_12_
  39.0 2.1 %all-to-all-done = bf16[16,64,1024]{2,1,0:T(8,128)(2,1)} async-done(((bf16[16,64,1024]{2,1,0:T(8,128)(2,1)}), bf16[16,64,1024]{2,1,0:T(8,128)(2,1)}, u32[]{:S(2)}, u32[]{:S(2)}) %all-to-all-start) | async-done | bytes 2097184 | tf_op jit(solution)/shard_map/all_to_all | solution.py:397
  41.1 7.3 %stats.1 = (f32[1024,512]{1,0:T(8,128)}, f32[1024,512]{1,0:T(8,128)}, bf16[1024,1024]{1,0:T(8,128)(2,1)}, bf16[1024,1024]{1,0:T(8,128)(2,1)}, f32[8,128]{1,0:T(8,128)S(1)}, /*index=5*/f32[8,8,128]{2,1,0:T(8,128)}) custom-call(bf16[1024,1024]{1,0:T(8,128)(2,1)} %bitcast.rows, s32[128,128]{1,0:T(8,128)S(1)} %bitcast.6, bf16[64,1024]{1,0:T(8,128)(2,1)S(1)} %copy-done.1, ...), custom_call_target="tpu_custom_call" | custom-call | flops 2147483648 | bytes 8388608 | tf_op jit(solution)/shard_map/stats/pallas_call | solution.py:213
  49.1 8.5 %all-to-all-start.2 = ((f32[8,8,128]{2,1,0:T(8,128)}), f32[8,8,128]{2,1,0:T(8,128)S(1)}, u32[]{:S(2)}, u32[]{:S(2)}) async-start(f32[8,8,128]{2,1,0:T(8,128)} %get-tuple-element.22), calls=%async_computation.2 | async-start | bytes 65536 | tf_op jit(solution)/shard_map/all_to_all | solution.py:409
  57.6 8.0 %all-to-all-done.2.col_parts = f32[8,8,128]{2,1,0:T(8,128)S(1)} async-done(((f32[8,8,128]{2,1,0:T(8,128)}), f32[8,8,128]{2,1,0:T(8,128)S(1)}, u32[]{:S(2)}, u32[]{:S(2)}) %all-to-all-start.2) | async-done | bytes 32800 | tf_op jit(solution)/shard_map/all_to_all | solution.py:409
  65.6 0.7 broadcast_in_dim.2
  66.2 4.9 %all-to-all-start.1 = ((f32[16,2,8,128]{3,2,1,0:T(8,128)}), f32[16,2,8,128]{3,2,1,0:T(8,128)S(1)}, u32[]{:S(2)}, u32[]{:S(2)}) async-start(f32[16,2,8,128]{3,2,1,0:T(8,128)} %broadcast_in_dim.2), calls=%async_computation.1 | async-start | bytes 262144 | tf_op jit(solution)/shard_map/all_to_all | solution.py:410
  71.1 1.2 collective-permute-done.18.col_others
  72.3 5.2 %all-to-all-done.1.row_parts = f32[16,2,8,128]{3,2,1,0:T(8,128)S(1)} async-done(((f32[16,2,8,128]{3,2,1,0:T(8,128)}), f32[16,2,8,128]{3,2,1,0:T(8,128)S(1)}, u32[]{:S(2)}, u32[]{:S(2)}) %all-to-all-start.1) | async-done | bytes 131104 | tf_op jit(solution)/shard_map/all_to_all | solution.py:410
  78.1 10.4 %grad.1 = (bf16[1024,1024]{1,0:T(8,128)(2,1)}, f32[64,1024]{1,0:T(8,128)}, bf16[64,1024]{1,0:T(8,128)(2,1)S(1)}, bf16[64,1024]{1,0:T(8,128)(2,1)S(1)}, bf16[64,1...) custom-call(f32[1024,512]{1,0:T(8,128)} %get-tuple-element.17.near_r, ...), custom_call_target="tpu_custom_call" | custom-call | flops 4294967296 | bytes 14680064 | tf_op jit(solution)/shard_map/grad/pallas_call | solution.py:335
  88.5 5.4 %all-to-all-start.3 = ((bf16[16,64,1024]{2,1,0:T(8,128)(2,1)}), bf16[16,64,1024]{2,1,0:T(8,128)(2,1)S(1)}, u32[]{:S(2)}, u32[]{:S(2)}) async-start(bf16[16,64,1024]{2,1,0:T(8,128)(2,1)} %bitcast.7), calls=%async_computation.3 | async-start | bytes 4194304 | tf_op jit(solution)/shard_map/all_to_all | solution.py:416
  94.5 3.1 %collective-permute-start.20 = (bf16[64,1024]{1,0:T(8,128)(2,1)S(1)}, bf16[64,1024]{1,0:T(8,128)(2,1)S(1)}, u32[]{:S(2)}, u32[]{:S(2)}) collective-permute-start(bf16[64,1024]{1,0:T(8,128)(2,1)S(1)} %get-tuple-element.26), channel_id=1, source_target_pairs={{0,3},{1,4},{2,5},{3,6},{4,7},{5,0},{6,1},{7,2},{8,11},{9,12},{10,... | collective-permute-start | bytes 393224 | tf_op jit(solution)/shard_map/ppermute | solution.py:29
  97.7 1.9 %collective-permute-start.21 = (bf16[64,1024]{1,0:T(8,128)(2,1)}, bf16[64,1024]{1,0:T(8,128)(2,1)S(1)}, u32[]{:S(2)}, u32[]{:S(2)}) collective-permute-start(bf16[64,1024]{1,0:T(8,128)(2,1)} %get-tuple-element.27), channel_id=1, source_target_pairs={{0,5},{1,6},{2,7},{3,0},{4,1},{5,2},{6,3},{7,4},{8,13},{9,14},{10,... | collective-permute-start | bytes 393224 | tf_op jit(solution)/shard_map/ppermute | solution.py:29
  99.6 2.4 %collective-permute-start.22 = (bf16[64,1024]{1,0:T(8,128)(2,1)S(1)}, bf16[64,1024]{1,0:T(8,128)(2,1)S(1)}, u32[]{:S(2)}, u32[]{:S(2)}) collective-permute-start(bf16[64,1024]{1,0:T(8,128)(2,1)S(1)} %get-tuple-element.28), channel_id=1, source_target_pairs={{0,2},{1,3},{2,4},{3,5},{4,6},{5,7},{6,0},{7,1},{8,10},{9,11},{10,... | collective-permute-start | bytes 393224 | tf_op jit(solution)/shard_map/ppermute | solution.py:29
  102.0 1.8 %collective-permute-start.23 = (bf16[64,1024]{1,0:T(8,128)(2,1)}, bf16[64,1024]{1,0:T(8,128)(2,1)S(1)}, u32[]{:S(2)}, u32[]{:S(2)}) collective-permute-start(bf16[64,1024]{1,0:T(8,128)(2,1)} %get-tuple-element.29), channel_id=1, source_target_pairs={{0,6},{1,7},{2,0},{3,1},{4,2},{5,3},{6,4},{7,5},{8,14},{9,15},{10,... | collective-permute-start | bytes 393224 | tf_op jit(solution)/shard_map/ppermute | solution.py:29
  103.7 4.9 %collective-permute-done.19.refs_0_ = bf16[64,1024]{1,0:T(8,128)(2,1)S(1)} collective-permute-done((bf16[64,1024]{1,0:T(8,128)(2,1)S(1)}, bf16[64,1024]{1,0:T(8,128)(2,1)S(1)}, u32[]{:S(2)}, u32[]{:S(2)}) %collective-permute-start.19) | collective-permute-done | bytes 131104 | tf_op jit(solution)/shard_map/ppermute | solution.py:29
  108.7 3.1 %collective-permute-done.20.refs_1_ = bf16[64,1024]{1,0:T(8,128)(2,1)S(1)} collective-permute-done((bf16[64,1024]{1,0:T(8,128)(2,1)S(1)}, bf16[64,1024]{1,0:T(8,128)(2,1)S(1)}, u32[]{:S(2)}, u32[]{:S(2)}) %collective-permute-start.20) | collective-permute-done | bytes 131104 | tf_op jit(solution)/shard_map/ppermute | solution.py:29
  111.8 4.2 %collective-permute-start.25 = (bf16[64,1024]{1,0:T(8,128)(2,1)}, bf16[64,1024]{1,0:T(8,128)(2,1)S(1)}, u32[]{:S(2)}, u32[]{:S(2)}) collective-permute-start(bf16[64,1024]{1,0:T(8,128)(2,1)} %get-tuple-element.31), channel_id=1, source_target_pairs={{0,7},{1,0},{2,1},{3,2},{4,3},{5,4},{6,5},{7,6},{8,15},{9,8},{10,9... | collective-permute-start | bytes 393224 | tf_op jit(solution)/shard_map/ppermute | solution.py:29
  116.0 1.3 %collective-permute-done.22.refs_3_ = bf16[64,1024]{1,0:T(8,128)(2,1)S(1)} collective-permute-done((bf16[64,1024]{1,0:T(8,128)(2,1)S(1)}, bf16[64,1024]{1,0:T(8,128)(2,1)S(1)}, u32[]{:S(2)}, u32[]{:S(2)}) %collective-permute-start.22) | collective-permute-done | bytes 131104 | tf_op jit(solution)/shard_map/ppermute | solution.py:29
  117.9 0.7 collective-permute-done.24.refs_5_
  119.4 1.2 %sums.1 = (f32[64,1024]{1,0:T(8,128)}, f32[64,1024]{1,0:T(8,128)}) custom-call(bf16[16,64,1024]{2,1,0:T(8,128)(2,1)S(1)} %all-to-all-done.3.image_parts, f32[64,1024]{1,0:T(8,128)S(1)} %copy-done, bf16[64,1024]{1,0:T(8,128)(2,1)S(1)} %collective-permute-done.19.refs_0_, bf16[64,1024]{1,0:T(8,128)(2,1)S(1)} %collective-permute-done.20.refs_1_, ...), custom_call_target="tpu_custom_call" | custom-call | flops 1572864 | bytes 4194304 | tf_op jit(solution)/shard_map/sums/pallas_call | solution.py:379
  (44 shorter events, 4.8 us)
Async XLA Ops:
  3.1 38.0 %copy-start.2 = (s32[16384]{0:T(1024)S(1)}, s32[16384]{0:T(1024)}, u32[]{:S(2)}) copy-start(s32[16384]{0:T(1024)} %param.5) | copy-start | bytes 196612
  3.1 38.0 %all-to-all-start = ((bf16[16,64,1024]{2,1,0:T(8,128)(2,1)}), bf16[16,64,1024]{2,1,0:T(8,128)(2,1)}, u32[]{:S(2)}, u32[]{:S(2)}) async-start(bf16[16,64,1024]{2,1,0:T(8,128)(2,1)} %repeat.1), calls=%async_computation | async-start | bytes 4194304 | tf_op jit(solution)/shard_map/all_to_all | solution.py:397
  10.6 8.5 %collective-permute-start = (bf16[64,1024]{1,0:T(8,128)(2,1)S(1)}, bf16[64,1024]{1,0:T(8,128)(2,1)S(1)}, u32[]{:S(2)}, u32[]{:S(2)}) collective-permute-start(bf16[64,1024]{1,0:T(8,128)(2,1)S(1)} %copy-done.1), channel_id=1, source_target_pairs={{0,7},{1,0},{2,1},{3,2},{4,3},{5,4},{6,5},{7,6},{8,15},{9,8},{10,9... | collective-permute-start | bytes 393224 | tf_op jit(solution)/shard_map/ppermute | solution.py:29
  16.5 6.2 %collective-permute-start.4 = (bf16[64,1024]{1,0:T(8,128)(2,1)S(1)}, bf16[64,1024]{1,0:T(8,128)(2,1)S(1)}, u32[]{:S(2)}, u32[]{:S(2)}) collective-permute-start(bf16[64,1024]{1,0:T(8,128)(2,1)S(1)} %copy-done.1), channel_id=1, source_target_pairs={{0,1},{1,2},{2,3},{3,4},{4,5},{5,6},{6,7},{7,0},{8,9},{9,10},{10,1... | collective-permute-start | bytes 393224 | tf_op jit(solution)/shard_map/ppermute | solution.py:29
  19.1 6.2 %collective-permute-start.1 = (bf16[64,1024]{1,0:T(8,128)(2,1)S(1)}, bf16[64,1024]{1,0:T(8,128)(2,1)S(1)}, u32[]{:S(2)}, u32[]{:S(2)}) collective-permute-start(bf16[64,1024]{1,0:T(8,128)(2,1)S(1)} %collective-permute-done.refs_1_), channel_id=1, source_target_pairs={{0,7},{1,0},{2,1},{3,2},{4,3},{5,4},{6,5},{7,6},{8,15},{9,8},{10,9... | collective-permute-start | bytes 393224 | tf_op jit(solution)/shard_map/ppermute | solution.py:29
  22.7 6.7 %collective-permute-start.5 = (bf16[64,1024]{1,0:T(8,128)(2,1)S(1)}, bf16[64,1024]{1,0:T(8,128)(2,1)S(1)}, u32[]{:S(2)}, u32[]{:S(2)}) collective-permute-start(bf16[64,1024]{1,0:T(8,128)(2,1)S(1)} %collective-permute-done.4.refs_7_), channel_id=1, source_target_pairs={{0,1},{1,2},{2,3},{3,4},{4,5},{5,6},{6,7},{7,0},{8,9},{9,10},{10,1... | collective-permute-start | bytes 393224 | tf_op jit(solution)/shard_map/ppermute | solution.py:29
  25.2 6.2 %collective-permute-start.2 = (bf16[64,1024]{1,0:T(8,128)(2,1)S(1)}, bf16[64,1024]{1,0:T(8,128)(2,1)S(1)}, u32[]{:S(2)}, u32[]{:S(2)}) collective-permute-start(bf16[64,1024]{1,0:T(8,128)(2,1)S(1)} %collective-permute-done.1.refs_2_), channel_id=1, source_target_pairs={{0,7},{1,0},{2,1},{3,2},{4,3},{5,4},{6,5},{7,6},{8,15},{9,8},{10,9... | collective-permute-start | bytes 393224 | tf_op jit(solution)/shard_map/ppermute | solution.py:29
  28.9 6.2 %collective-permute-start.7 = (bf16[64,1024]{1,0:T(8,128)(2,1)S(1)}, bf16[64,1024]{1,0:T(8,128)(2,1)S(1)}, u32[]{:S(2)}, u32[]{:S(2)}) collective-permute-start(bf16[64,1024]{1,0:T(8,128)(2,1)S(1)} %copy-done.1), channel_id=1, source_target_pairs={{0,32},{32,0},{1,33},{33,1},{2,34},{34,2},{3,35},{35,3},{4,36},{36... | collective-permute-start | bytes 393224 | tf_op jit(solution)/shard_map/ppermute | solution.py:24
  28.9 6.2 %collective-permute-start.14 = (bf16[64,1024]{1,0:T(8,128)(2,1)S(1)}, bf16[64,1024]{1,0:T(8,128)(2,1)S(1)}, u32[]{:S(2)}, u32[]{:S(2)}) collective-permute-start(bf16[64,1024]{1,0:T(8,128)(2,1)S(1)} %collective-permute-done.4.refs_7_), channel_id=1, source_target_pairs={{0,32},{32,0},{1,33},{33,1},{2,34},{34,2},{3,35},{35,3},{4,36},{36... | collective-permute-start | bytes 393224 | tf_op jit(solution)/shard_map/ppermute | solution.py:24
  29.4 6.2 %collective-permute-start.8 = (bf16[64,1024]{1,0:T(8,128)(2,1)S(1)}, bf16[64,1024]{1,0:T(8,128)(2,1)S(1)}, u32[]{:S(2)}, u32[]{:S(2)}) collective-permute-start(bf16[64,1024]{1,0:T(8,128)(2,1)S(1)} %collective-permute-done.refs_1_), channel_id=1, source_target_pairs={{0,32},{32,0},{1,33},{33,1},{2,34},{34,2},{3,35},{35,3},{4,36},{36... | collective-permute-start | bytes 393224 | tf_op jit(solution)/shard_map/ppermute | solution.py:24
  29.4 7.1 %collective-permute-start.6 = (bf16[64,1024]{1,0:T(8,128)(2,1)S(1)}, bf16[64,1024]{1,0:T(8,128)(2,1)S(1)}, u32[]{:S(2)}, u32[]{:S(2)}) collective-permute-start(bf16[64,1024]{1,0:T(8,128)(2,1)S(1)} %collective-permute-done.5.refs_6_), channel_id=1, source_target_pairs={{0,1},{1,2},{2,3},{3,4},{4,5},{5,6},{6,7},{7,0},{8,9},{9,10},{10,1... | collective-permute-start | bytes 393224 | tf_op jit(solution)/shard_map/ppermute | solution.py:29
  31.4 6.2 %collective-permute-start.3 = (bf16[64,1024]{1,0:T(8,128)(2,1)S(1)}, bf16[64,1024]{1,0:T(8,128)(2,1)S(1)}, u32[]{:S(2)}, u32[]{:S(2)}) collective-permute-start(bf16[64,1024]{1,0:T(8,128)(2,1)S(1)} %collective-permute-done.2.refs_3_), channel_id=1, source_target_pairs={{0,7},{1,0},{2,1},{3,2},{4,3},{5,4},{6,5},{7,6},{8,15},{9,8},{10,9... | collective-permute-start | bytes 393224 | tf_op jit(solution)/shard_map/ppermute | solution.py:29
  35.1 2.5 %collective-permute-start.13 = (bf16[64,1024]{1,0:T(8,128)(2,1)S(1)}, bf16[64,1024]{1,0:T(8,128)(2,1)S(1)}, u32[]{:S(2)}, u32[]{:S(2)}) collective-permute-start(bf16[64,1024]{1,0:T(8,128)(2,1)S(1)} %collective-permute-done.5.refs_6_), channel_id=1, source_target_pairs={{0,32},{32,0},{1,33},{33,1},{2,34},{34,2},{3,35},{35,3},{4,36},{36... | collective-permute-start | bytes 393224 | tf_op jit(solution)/shard_map/ppermute | solution.py:24
  35.1 2.5 %collective-permute-start.9 = (bf16[64,1024]{1,0:T(8,128)(2,1)S(1)}, bf16[64,1024]{1,0:T(8,128)(2,1)S(1)}, u32[]{:S(2)}, u32[]{:S(2)}) collective-permute-start(bf16[64,1024]{1,0:T(8,128)(2,1)S(1)} %collective-permute-done.1.refs_2_), channel_id=1, source_target_pairs={{0,32},{32,0},{1,33},{33,1},{2,34},{34,2},{3,35},{35,3},{4,36},{36... | collective-permute-start | bytes 393224 | tf_op jit(solution)/shard_map/ppermute | solution.py:24
  35.6 2.3 %collective-permute-start.10 = (bf16[64,1024]{1,0:T(8,128)(2,1)S(1)}, bf16[64,1024]{1,0:T(8,128)(2,1)S(1)}, u32[]{:S(2)}, u32[]{:S(2)}) collective-permute-start(bf16[64,1024]{1,0:T(8,128)(2,1)S(1)} %collective-permute-done.2.refs_3_), channel_id=1, source_target_pairs={{0,32},{32,0},{1,33},{33,1},{2,34},{34,2},{3,35},{35,3},{4,36},{36... | collective-permute-start | bytes 393224 | tf_op jit(solution)/shard_map/ppermute | solution.py:24
  36.5 1.3 %collective-permute-start.12 = (bf16[64,1024]{1,0:T(8,128)(2,1)S(1)}, bf16[64,1024]{1,0:T(8,128)(2,1)S(1)}, u32[]{:S(2)}, u32[]{:S(2)}) collective-permute-start(bf16[64,1024]{1,0:T(8,128)(2,1)S(1)} %collective-permute-done.6.refs_5_), channel_id=1, source_target_pairs={{0,32},{32,0},{1,33},{33,1},{2,34},{34,2},{3,35},{35,3},{4,36},{36... | collective-permute-start | bytes 393224 | tf_op jit(solution)/shard_map/ppermute | solution.py:24
  37.6 1.3 %collective-permute-start.11 = (bf16[64,1024]{1,0:T(8,128)(2,1)S(1)}, bf16[64,1024]{1,0:T(8,128)(2,1)S(1)}, u32[]{:S(2)}, u32[]{:S(2)}) collective-permute-start(bf16[64,1024]{1,0:T(8,128)(2,1)S(1)} %collective-permute-done.3.refs_4_), channel_id=1, source_target_pairs={{0,32},{32,0},{1,33},{33,1},{2,34},{34,2},{3,35},{35,3},{4,36},{36... | collective-permute-start | bytes 393224 | tf_op jit(solution)/shard_map/ppermute | solution.py:24
  48.4 29.1 %collective-permute-start.15 = (f32[1024,512]{1,0:T(8,128)}, f32[1024,512]{1,0:T(8,128)}, u32[]{:S(2)}, u32[]{:S(2)}) collective-permute-start(f32[1024,512]{1,0:T(8,128)} %get-tuple-element.18.far_ref), channel_id=1, source_target_pairs={{0,32},{32,0},{1,33},{33,1},{2,34},{34,2},{3,35},{35,3},{4,36},{36... | collective-permute-start | bytes 6291464 | tf_op jit(solution)/shard_map/ppermute | solution.py:24
  48.5 29.0 %collective-permute-start.16 = (bf16[1024,1024]{1,0:T(8,128)(2,1)}, bf16[1024,1024]{1,0:T(8,128)(2,1)}, u32[]{:S(2)}, u32[]{:S(2)}) collective-permute-start(bf16[1024,1024]{1,0:T(8,128)(2,1)} %get-tuple-element.20.rows_ref), channel_id=1, source_target_pairs={{0,32},{32,0},{1,33},{33,1},{2,34},{34,2},{3,35},{35,3},{4,36},{36... | collective-permute-start | bytes 6291464 | tf_op jit(solution)/shard_map/ppermute | solution.py:24
  49.0 8.6 %collective-permute-start.17 = (f32[8,128]{1,0:T(8,128)S(1)}, f32[8,128]{1,0:T(8,128)S(1)}, u32[]{:S(2)}, u32[]{:S(2)}) collective-permute-start(f32[8,128]{1,0:T(8,128)S(1)} %get-tuple-element.21), channel_id=1, source_target_pairs={{0,32},{32,0},{1,33},{33,1},{2,34},{34,2},{3,35},{35,3},{4,36},{36... | collective-permute-start | bytes 12296 | tf_op jit(solution)/shard_map/ppermute | solution.py:24
  49.1 16.5 %all-to-all-start.2 = ((f32[8,8,128]{2,1,0:T(8,128)}), f32[8,8,128]{2,1,0:T(8,128)S(1)}, u32[]{:S(2)}, u32[]{:S(2)}) async-start(f32[8,8,128]{2,1,0:T(8,128)} %get-tuple-element.22), calls=%async_computation.2 | async-start | bytes 65536 | tf_op jit(solution)/shard_map/all_to_all | solution.py:409
  66.2 11.2 %all-to-all-start.1 = ((f32[16,2,8,128]{3,2,1,0:T(8,128)}), f32[16,2,8,128]{3,2,1,0:T(8,128)S(1)}, u32[]{:S(2)}, u32[]{:S(2)}) async-start(f32[16,2,8,128]{3,2,1,0:T(8,128)} %broadcast_in_dim.2), calls=%async_computation.1 | async-start | bytes 262144 | tf_op jit(solution)/shard_map/all_to_all | solution.py:410
  71.1 1.2 %collective-permute-start.18 = (f32[8,8,128]{2,1,0:T(8,128)S(1)}, f32[8,8,128]{2,1,0:T(8,128)S(1)}, u32[]{:S(2)}, u32[]{:S(2)}) collective-permute-start(f32[8,8,128]{2,1,0:T(8,128)S(1)} %all-to-all-done.2.col_parts), channel_id=1, source_target_pairs={{0,32},{32,0},{1,33},{33,1},{2,34},{34,2},{3,35},{35,3},{4,36},{36... | collective-permute-start | bytes 98312 | tf_op jit(solution)/shard_map/ppermute | solution.py:24
  88.5 30.9 %copy-start = (f32[64,1024]{1,0:T(8,128)S(1)}, f32[64,1024]{1,0:T(8,128)}, u32[]{:S(2)}) copy-start(f32[64,1024]{1,0:T(8,128)} %get-tuple-element.24.own_ref) | copy-start | bytes 786436
  88.5 30.8 %all-to-all-start.3 = ((bf16[16,64,1024]{2,1,0:T(8,128)(2,1)}), bf16[16,64,1024]{2,1,0:T(8,128)(2,1)S(1)}, u32[]{:S(2)}, u32[]{:S(2)}) async-start(bf16[16,64,1024]{2,1,0:T(8,128)(2,1)} %bitcast.7), calls=%async_computation.3 | async-start | bytes 4194304 | tf_op jit(solution)/shard_map/all_to_all | solution.py:416
  93.9 14.7 %collective-permute-start.19 = (bf16[64,1024]{1,0:T(8,128)(2,1)S(1)}, bf16[64,1024]{1,0:T(8,128)(2,1)S(1)}, u32[]{:S(2)}, u32[]{:S(2)}) collective-permute-start(bf16[64,1024]{1,0:T(8,128)(2,1)S(1)} %copy-done.4), channel_id=1, source_target_pairs={{0,4},{1,5},{2,6},{3,7},{4,0},{5,1},{6,2},{7,3},{8,12},{9,13},{10,... | collective-permute-start | bytes 393224 | tf_op jit(solution)/shard_map/ppermute | solution.py:29
  94.5 17.2 %collective-permute-start.20 = (bf16[64,1024]{1,0:T(8,128)(2,1)S(1)}, bf16[64,1024]{1,0:T(8,128)(2,1)S(1)}, u32[]{:S(2)}, u32[]{:S(2)}) collective-permute-start(bf16[64,1024]{1,0:T(8,128)(2,1)S(1)} %get-tuple-element.26), channel_id=1, source_target_pairs={{0,3},{1,4},{2,5},{3,6},{4,7},{5,0},{6,1},{7,2},{8,11},{9,12},{10,... | collective-permute-start | bytes 393224 | tf_op jit(solution)/shard_map/ppermute | solution.py:29
  97.7 18.3 %collective-permute-start.21 = (bf16[64,1024]{1,0:T(8,128)(2,1)}, bf16[64,1024]{1,0:T(8,128)(2,1)S(1)}, u32[]{:S(2)}, u32[]{:S(2)}) collective-permute-start(bf16[64,1024]{1,0:T(8,128)(2,1)} %get-tuple-element.27), channel_id=1, source_target_pairs={{0,5},{1,6},{2,7},{3,0},{4,1},{5,2},{6,3},{7,4},{8,13},{9,14},{10,... | collective-permute-start | bytes 393224 | tf_op jit(solution)/shard_map/ppermute | solution.py:29
  99.6 17.7 %collective-permute-start.22 = (bf16[64,1024]{1,0:T(8,128)(2,1)S(1)}, bf16[64,1024]{1,0:T(8,128)(2,1)S(1)}, u32[]{:S(2)}, u32[]{:S(2)}) collective-permute-start(bf16[64,1024]{1,0:T(8,128)(2,1)S(1)} %get-tuple-element.28), channel_id=1, source_target_pairs={{0,2},{1,3},{2,4},{3,5},{4,6},{5,7},{6,0},{7,1},{8,10},{9,11},{10,... | collective-permute-start | bytes 393224 | tf_op jit(solution)/shard_map/ppermute | solution.py:29
  102.0 15.9 %collective-permute-start.23 = (bf16[64,1024]{1,0:T(8,128)(2,1)}, bf16[64,1024]{1,0:T(8,128)(2,1)S(1)}, u32[]{:S(2)}, u32[]{:S(2)}) collective-permute-start(bf16[64,1024]{1,0:T(8,128)(2,1)} %get-tuple-element.29), channel_id=1, source_target_pairs={{0,6},{1,7},{2,0},{3,1},{4,2},{5,3},{6,4},{7,5},{8,14},{9,15},{10,... | collective-permute-start | bytes 393224 | tf_op jit(solution)/shard_map/ppermute | solution.py:29
  108.6 10.0 %collective-permute-start.24 = (bf16[64,1024]{1,0:T(8,128)(2,1)S(1)}, bf16[64,1024]{1,0:T(8,128)(2,1)S(1)}, u32[]{:S(2)}, u32[]{:S(2)}) collective-permute-start(bf16[64,1024]{1,0:T(8,128)(2,1)S(1)} %get-tuple-element.30), channel_id=1, source_target_pairs={{0,1},{1,2},{2,3},{3,4},{4,5},{5,6},{6,7},{7,0},{8,9},{9,10},{10,1... | collective-permute-start | bytes 393224 | tf_op jit(solution)/shard_map/ppermute | solution.py:29
  111.8 7.0 %collective-permute-start.25 = (bf16[64,1024]{1,0:T(8,128)(2,1)}, bf16[64,1024]{1,0:T(8,128)(2,1)S(1)}, u32[]{:S(2)}, u32[]{:S(2)}) collective-permute-start(bf16[64,1024]{1,0:T(8,128)(2,1)} %get-tuple-element.31), channel_id=1, source_target_pairs={{0,7},{1,0},{2,1},{3,2},{4,3},{5,4},{6,5},{7,6},{8,15},{9,8},{10,9... | collective-permute-start | bytes 393224 | tf_op jit(solution)/shard_map/ppermute | solution.py:29
  (3 other events, 13.6 us)

commit v5 on v4

--- a/solution.py
+++ b/solution.py
@@ -144,8 +144,8 @@
     )(values)
 
 
-def stats_kernel(rows, group_ref, *refs):
-    shards, (near_ref, far_ref, cols_ref, rows_ref, row_ref, col_ref, kept_all, cols, groups, sems) = refs[:-10], refs[-10:]
+def stats_kernel(rows_ref, group_ref, *refs):
+    shards, (near_ref, far_ref, cols_ref, row_ref, col_ref, kept_all, rows, cols, groups, sems) = refs[:-10], refs[-10:]
     where = here_in_mesh()
     n_rows, n_cols = kept_all.shape
     half = n_cols // 2
@@ -162,15 +162,21 @@
     cols_store = pltpu.make_async_copy(cols, cols_ref, sems.at[2 * n_blocks])
     group_load = pltpu.make_async_copy(group_ref, groups, sems.at[2 * n_blocks + 1])
     group_load.start()
-    rows_store = pltpu.make_async_copy(rows, rows_ref, sems.at[2 * n_blocks + 2])
+    row_loads = []
+    for i in range(n_blocks):
+        here = pl.ds(i * block, block)
+        row_loads.append(pltpu.make_async_copy(rows_ref.at[here, :], rows.at[here, :], sems.at[2 * n_blocks + 2 + i]))
+        row_loads[i].start()
     for side in range(2):
         for k in range(n_z):
             at = pl.multiple_of(side * half + lax.rem(where[3] + k, n_z) * span, span)
             cols[pl.ds(at, span), :] = shards[side * n_z + k][...]
     cols_store.start()
-    rows_store.start()
+    row_loads[0].wait()
     kept_all[:block, :] = scale_base2 * contract(rows[:block, :], cols[...], 1, 1)
     group_load.wait()
+    for copy in row_loads[1:]:
+        copy.wait()
     row_groups, col_groups = group_rows(where, groups)
     ci = col_ids(where, n_cols, span)
     cg = jnp.concatenate(col_groups, axis=1)
@@ -203,7 +209,7 @@
         peak = top
     col_lse = by_core(fold(peak + jnp.log2(total)), where[1])
     col_ref[...] = jnp.broadcast_to(col_lse[None], col_ref.shape)
-    for copy in (cols_store, rows_store, *stores):
+    for copy in (cols_store, *stores):
         copy.wait()
 
 
@@ -212,21 +218,21 @@
     n_cols = len(shards) * shards[0].shape[0]
     return pl.pallas_call(
         stats_kernel,
-        in_specs=[in_vmem, in_hbm] + [in_vmem] * len(shards),
-        out_specs=[in_hbm, in_hbm, in_hbm, in_hbm, in_vmem, in_vmem],
+        in_specs=[in_hbm] * 2 + [in_vmem] * len(shards),
+        out_specs=[in_hbm, in_hbm, in_hbm, in_vmem, in_vmem],
         out_shape=[
             jax.ShapeDtypeStruct((n_rows, n_cols // 2), jnp.float32),
             jax.ShapeDtypeStruct((n_rows, n_cols // 2), jnp.float32),
             jax.ShapeDtypeStruct((n_cols, width), jnp.bfloat16),
-            jax.ShapeDtypeStruct((n_rows, width), jnp.bfloat16),
             jax.ShapeDtypeStruct((n_rows // lanes, lanes), jnp.float32),
             jax.ShapeDtypeStruct((n_col, n_cols // lanes, lanes), jnp.float32),
         ],
         scratch_shapes=[
             pltpu.VMEM((n_rows, n_cols), jnp.float32),
+            pltpu.VMEM((n_rows, width), jnp.bfloat16),
             pltpu.VMEM((n_cols, width), jnp.bfloat16),
             pltpu.VMEM(groups.shape, groups.dtype),
-            pltpu.SemaphoreType.DMA((2 * (n_rows // block) + 3,)),
+            pltpu.SemaphoreType.DMA((3 * (n_rows // block) + 2,)),
         ],
         compiler_params=params(50),
         cost_estimate=estimate(2 * n_rows * n_cols * width, 8, 2 * n_rows * n_cols),
@@ -352,7 +358,7 @@
             pltpu.VMEM((half, width), jnp.float32),
             pltpu.SemaphoreType.DMA((3 * (n_rows // block) + 4,)),
         ],
-        compiler_params=params(53.5),
+        compiler_params=params(52),
         cost_estimate=estimate(4 * n_rows * n_cols * width, 14, 3 * n_rows * n_cols),
         name="grad",
     )(near, far, other, cols, rows, other_rows, *parts)
@@ -404,7 +410,7 @@
     near = [shards[k] for k in range(n_z)]
     far = [swap_core(shard) for shard in near]
 
-    near_kept, far_kept, cols, rows, row_part, col_part = block_stats(rows, groups, near + far, n_z)
+    near_kept, far_kept, cols, row_part, col_part = block_stats(rows, groups, near + far, n_z)
     pair = jnp.stack([row_part, swap_core(row_part)])
     col_parts = lax.all_to_all(col_part, "z", 0, 0)
     row_parts = lax.all_to_all(jnp.broadcast_to(pair[None], (n_plane,) + pair.shape), plane, 0, 0)

time: 123 us -> 121 us (0.984)
    all_to_all x1, waiting for transfers between devices: 2.12 us -> 3.46 us  [per_device(): rows = lax.all_to_all(repeat(image_emb, n_plane), plane, 0, 0)]
    ppermute x12, waiting for transfers between devices: 2.55 us -> 1.23 us  [swap_core(): return lax.ppermute(values, 'core', [(0, 1), (1, 0)])]
  transfers between devices with their start and end apart: 30 -> 30, of which waited for: 18 -> 16; matrix products, arithmetic and copies ran while one was open for 1% -> 1% of each run, Pallas kernels for 0% -> 6%
where the time goes in v5:
time: 121 us; the launch traced here: 119 us
  starting transfers between devices  58.7 us (49%)
  waiting for transfers between devices  38.3 us (32%)
  Pallas kernels  20.2 us (17%)
    ppermute x14, starting transfers between devices, shift(): lax.ppermute(values, axis, [(i, (i + step) % size) for i in range(size)])  30.8 us
    ppermute x14, waiting for transfers between devices, shift(): lax.ppermute(values, axis, [(i, (i + step) % size) for i in range(size)])  19.8 us
    pallas_call x1, Pallas kernels, block_grad(): pl.pallas_call(grad_kernel, in_specs=[in_hbm] * 6 + [in_vmem] * len(parts...  9.34 us
    all_to_all x1, starting transfers between devices, per_device(): col_parts = lax.all_to_all(col_part, 'z', 0, 0)  8.46 us
    all_to_all x1, waiting for transfers between devices, per_device(): col_parts = lax.all_to_all(col_part, 'z', 0, 0)  8.01 us
    all_to_all x1, starting transfers between devices, per_device(): rows = lax.all_to_all(repeat(image_emb, n_plane), plane, 0, 0)  7.54 us
    pallas_call x1, Pallas kernels, block_stats(): pl.pallas_call(stats_kernel, in_specs=[in_hbm] * 2 + [in_vmem] * len(shar...  7.29 us
    all_to_all x1, starting transfers between devices, per_device(): lax.all_to_all(image_part.reshape(n_plane, span, width), plane, 0, 0)  5.25 us
  transfers between devices with their start and end apart: 30, of which 16 were waited for; matrix products, arithmetic and copies ran while one was open for 1% of the time, Pallas kernels for 6%

profile of v5, /device:TPU:8, one launch (start us, length us, event | category | flops | bytes accessed | tf_op | source)
XLA Modules:
  0.0 118.8 jit_solution(3164887414878035505)
XLA Ops:
  0.6 2.4 %repeat.1 = bf16[16,64,1024]{2,1,0:T(8,128)(2,1)} custom-call(bf16[64,1024]{1,0:T(8,128)(2,1)} %in_ref.1), custom_call_target="tpu_custom_call" | custom-call | bytes 2097152 | tf_op jit(solution)/shard_map/repeat/pallas_call | solution.py:135
  3.1 7.5 %all-to-all-start = ((bf16[16,64,1024]{2,1,0:T(8,128)(2,1)}), bf16[16,64,1024]{2,1,0:T(8,128)(2,1)}, u32[]{:S(2)}, u32[]{:S(2)}) async-start(bf16[16,64,1024]{2,1,0:T(8,128)(2,1)} %repeat.1), calls=%async_computation | async-start | bytes 4194304 | tf_op jit(solution)/shard_map/all_to_all | solution.py:403
  10.6 5.9 %collective-permute-start = (bf16[64,1024]{1,0:T(8,128)(2,1)S(1)}, bf16[64,1024]{1,0:T(8,128)(2,1)S(1)}, u32[]{:S(2)}, u32[]{:S(2)}) collective-permute-start(bf16[64,1024]{1,0:T(8,128)(2,1)S(1)} %copy-done), channel_id=1, source_target_pairs={{0,7},{1,0},{2,1},{3,2},{4,3},{5,4},{6,5},{7,6},{8,15},{9,8},{10,9... | collective-permute-start | bytes 393224 | tf_op jit(solution)/shard_map/ppermute | solution.py:29
  16.5 2.5 %collective-permute-done.refs_1_ = bf16[64,1024]{1,0:T(8,128)(2,1)S(1)} collective-permute-done((bf16[64,1024]{1,0:T(8,128)(2,1)S(1)}, bf16[64,1024]{1,0:T(8,128)(2,1)S(1)}, u32[]{:S(2)}, u32[]{:S(2)}) %collective-permute-start) | collective-permute-done | bytes 131104 | tf_op jit(solution)/shard_map/ppermute | solution.py:29
  19.1 3.7 %collective-permute-start.1 = (bf16[64,1024]{1,0:T(8,128)(2,1)S(1)}, bf16[64,1024]{1,0:T(8,128)(2,1)S(1)}, u32[]{:S(2)}, u32[]{:S(2)}) collective-permute-start(bf16[64,1024]{1,0:T(8,128)(2,1)S(1)} %collective-permute-done.refs_1_), channel_id=1, source_target_pairs={{0,7},{1,0},{2,1},{3,2},{4,3},{5,4},{6,5},{7,6},{8,15},{9,8},{10,9... | collective-permute-start | bytes 393224 | tf_op jit(solution)/shard_map/ppermute | solution.py:29
  22.7 2.5 %collective-permute-done.1.refs_2_ = bf16[64,1024]{1,0:T(8,128)(2,1)S(1)} collective-permute-done((bf16[64,1024]{1,0:T(8,128)(2,1)S(1)}, bf16[64,1024]{1,0:T(8,128)(2,1)S(1)}, u32[]{:S(2)}, u32[]{:S(2)}) %collective-permute-start.1) | collective-permute-done | bytes 131104 | tf_op jit(solution)/shard_map/ppermute | solution.py:29
  25.2 3.7 %collective-permute-start.2 = (bf16[64,1024]{1,0:T(8,128)(2,1)S(1)}, bf16[64,1024]{1,0:T(8,128)(2,1)S(1)}, u32[]{:S(2)}, u32[]{:S(2)}) collective-permute-start(bf16[64,1024]{1,0:T(8,128)(2,1)S(1)} %collective-permute-done.1.refs_2_), channel_id=1, source_target_pairs={{0,7},{1,0},{2,1},{3,2},{4,3},{5,4},{6,5},{7,6},{8,15},{9,8},{10,9... | collective-permute-start | bytes 393224 | tf_op jit(solution)/shard_map/ppermute | solution.py:29
  29.4 2.0 %collective-permute-done.2.refs_3_ = bf16[64,1024]{1,0:T(8,128)(2,1)S(1)} collective-permute-done((bf16[64,1024]{1,0:T(8,128)(2,1)S(1)}, bf16[64,1024]{1,0:T(8,128)(2,1)S(1)}, u32[]{:S(2)}, u32[]{:S(2)}) %collective-permute-start.2) | collective-permute-done | bytes 131104 | tf_op jit(solution)/shard_map/ppermute | solution.py:29
  31.4 3.7 %collective-permute-start.3 = (bf16[64,1024]{1,0:T(8,128)(2,1)S(1)}, bf16[64,1024]{1,0:T(8,128)(2,1)S(1)}, u32[]{:S(2)}, u32[]{:S(2)}) collective-permute-start(bf16[64,1024]{1,0:T(8,128)(2,1)S(1)} %collective-permute-done.2.refs_3_), channel_id=1, source_target_pairs={{0,7},{1,0},{2,1},{3,2},{4,3},{5,4},{6,5},{7,6},{8,15},{9,8},{10,9... | collective-permute-start | bytes 393224 | tf_op jit(solution)/shard_map/ppermute | solution.py:29
  35.7 0.8 collective-permute-done.6.refs_5_
  36.5 1.1 collective-permute-done.3.refs_4_
  37.6 3.5 %all-to-all-done = bf16[16,64,1024]{2,1,0:T(8,128)(2,1)} async-done(((bf16[16,64,1024]{2,1,0:T(8,128)(2,1)}), bf16[16,64,1024]{2,1,0:T(8,128)(2,1)}, u32[]{:S(2)}, u32[]{:S(2)}) %all-to-all-start) | async-done | bytes 2097184 | tf_op jit(solution)/shard_map/all_to_all | solution.py:403
  41.1 7.3 %stats.1 = (f32[1024,512]{1,0:T(8,128)}, f32[1024,512]{1,0:T(8,128)}, bf16[1024,1024]{1,0:T(8,128)(2,1)}, f32[8,128]{1,0:T(8,128)S(1)}, f32[8,8,128]{2,1,0:T(8,128)}) custom-call(bf16[1024,1024]{1,0:T(8,128)(2,1)} %bitcast.rows_ref, s32[128,128]{1,0:T(8,128)S(1)} %bitcast.6, bf16[64,1024]{1,0:T(8,128)(2,1)S(1)} %copy-done, ...), custom_call_target="tpu_custom_call" | custom-call | flops 2147483648 | bytes 8388608 | tf_op jit(solution)/shard_map/stats/pallas_call | solution.py:219
  49.1 8.5 %all-to-all-start.2 = ((f32[8,8,128]{2,1,0:T(8,128)}), f32[8,8,128]{2,1,0:T(8,128)S(1)}, u32[]{:S(2)}, u32[]{:S(2)}) async-start(f32[8,8,128]{2,1,0:T(8,128)} %get-tuple-element.20), calls=%async_computation.2 | async-start | bytes 65536 | tf_op jit(solution)/shard_map/all_to_all | solution.py:415
  57.6 8.0 %all-to-all-done.2.col_parts = f32[8,8,128]{2,1,0:T(8,128)S(1)} async-done(((f32[8,8,128]{2,1,0:T(8,128)}), f32[8,8,128]{2,1,0:T(8,128)S(1)}, u32[]{:S(2)}, u32[]{:S(2)}) %all-to-all-start.2) | async-done | bytes 32800 | tf_op jit(solution)/shard_map/all_to_all | solution.py:415
  65.6 0.7 broadcast_in_dim.2
  66.2 4.9 %all-to-all-start.1 = ((f32[16,2,8,128]{3,2,1,0:T(8,128)}), f32[16,2,8,128]{3,2,1,0:T(8,128)S(1)}, u32[]{:S(2)}, u32[]{:S(2)}) async-start(f32[16,2,8,128]{3,2,1,0:T(8,128)} %broadcast_in_dim.2), calls=%async_computation.1 | async-start | bytes 262144 | tf_op jit(solution)/shard_map/all_to_all | solution.py:416
  71.1 1.2 %collective-permute-done.18.col_others = f32[8,8,128]{2,1,0:T(8,128)S(1)} collective-permute-done((f32[8,8,128]{2,1,0:T(8,128)S(1)}, f32[8,8,128]{2,1,0:T(8,128)S(1)}, u32[]{:S(2)}, u32[]{:S(2)}) %collective-permute-start.18) | collective-permute-done | bytes 32800 | tf_op jit(solution)/shard_map/ppermute | solution.py:24
  72.3 5.2 %all-to-all-done.1.row_parts = f32[16,2,8,128]{3,2,1,0:T(8,128)S(1)} async-done(((f32[16,2,8,128]{3,2,1,0:T(8,128)}), f32[16,2,8,128]{3,2,1,0:T(8,128)S(1)}, u32[]{:S(2)}, u32[]{:S(2)}) %all-to-all-start.1) | async-done | bytes 131104 | tf_op jit(solution)/shard_map/all_to_all | solution.py:416
  77.5 9.3 %grad.1 = (bf16[1024,1024]{1,0:T(8,128)(2,1)}, f32[64,1024]{1,0:T(8,128)S(1)}, bf16[64,1024]{1,0:T(8,128)(2,1)S(1)}, bf16[64,1024]{1,0:T(8,128)(2,1)}, bf16[64,1...) custom-call(f32[1024,512]{1,0:T(8,128)} %get-tuple-element.16.near_r, ...), custom_call_target="tpu_custom_call" | custom-call | flops 4294967296 | bytes 14680064 | tf_op jit(solution)/shard_map/grad/pallas_call | solution.py:341
  86.8 5.3 %all-to-all-start.3 = ((bf16[16,64,1024]{2,1,0:T(8,128)(2,1)}), bf16[16,64,1024]{2,1,0:T(8,128)(2,1)S(1)}, u32[]{:S(2)}, u32[]{:S(2)}) async-start(bf16[16,64,1024]{2,1,0:T(8,128)(2,1)} %bitcast.7), calls=%async_computation.3 | async-start | bytes 4194304 | tf_op jit(solution)/shard_map/all_to_all | solution.py:422
  92.6 3.1 %collective-permute-start.20 = (bf16[64,1024]{1,0:T(8,128)(2,1)S(1)}, bf16[64,1024]{1,0:T(8,128)(2,1)S(1)}, u32[]{:S(2)}, u32[]{:S(2)}) collective-permute-start(bf16[64,1024]{1,0:T(8,128)(2,1)S(1)} %get-tuple-element.24), channel_id=1, source_target_pairs={{0,3},{1,4},{2,5},{3,6},{4,7},{5,0},{6,1},{7,2},{8,11},{9,12},{10,... | collective-permute-start | bytes 393224 | tf_op jit(solution)/shard_map/ppermute | solution.py:29
  95.7 1.9 %collective-permute-start.21 = (bf16[64,1024]{1,0:T(8,128)(2,1)}, bf16[64,1024]{1,0:T(8,128)(2,1)S(1)}, u32[]{:S(2)}, u32[]{:S(2)}) collective-permute-start(bf16[64,1024]{1,0:T(8,128)(2,1)} %get-tuple-element.25), channel_id=1, source_target_pairs={{0,5},{1,6},{2,7},{3,0},{4,1},{5,2},{6,3},{7,4},{8,13},{9,14},{10,... | collective-permute-start | bytes 393224 | tf_op jit(solution)/shard_map/ppermute | solution.py:29
  97.6 2.4 %collective-permute-start.22 = (bf16[64,1024]{1,0:T(8,128)(2,1)}, bf16[64,1024]{1,0:T(8,128)(2,1)S(1)}, u32[]{:S(2)}, u32[]{:S(2)}) collective-permute-start(bf16[64,1024]{1,0:T(8,128)(2,1)} %get-tuple-element.26), channel_id=1, source_target_pairs={{0,2},{1,3},{2,4},{3,5},{4,6},{5,7},{6,0},{7,1},{8,10},{9,11},{10,... | collective-permute-start | bytes 393224 | tf_op jit(solution)/shard_map/ppermute | solution.py:29
  100.0 1.8 %collective-permute-start.23 = (bf16[64,1024]{1,0:T(8,128)(2,1)}, bf16[64,1024]{1,0:T(8,128)(2,1)S(1)}, u32[]{:S(2)}, u32[]{:S(2)}) collective-permute-start(bf16[64,1024]{1,0:T(8,128)(2,1)} %get-tuple-element.27), channel_id=1, source_target_pairs={{0,6},{1,7},{2,0},{3,1},{4,2},{5,3},{6,4},{7,5},{8,14},{9,15},{10,... | collective-permute-start | bytes 393224 | tf_op jit(solution)/shard_map/ppermute | solution.py:29
  101.8 4.9 %collective-permute-done.19.refs_0_ = bf16[64,1024]{1,0:T(8,128)(2,1)S(1)} collective-permute-done((bf16[64,1024]{1,0:T(8,128)(2,1)S(1)}, bf16[64,1024]{1,0:T(8,128)(2,1)S(1)}, u32[]{:S(2)}, u32[]{:S(2)}) %collective-permute-start.19) | collective-permute-done | bytes 131104 | tf_op jit(solution)/shard_map/ppermute | solution.py:29
  106.7 3.2 %collective-permute-done.20.refs_1_ = bf16[64,1024]{1,0:T(8,128)(2,1)S(1)} collective-permute-done((bf16[64,1024]{1,0:T(8,128)(2,1)S(1)}, bf16[64,1024]{1,0:T(8,128)(2,1)S(1)}, u32[]{:S(2)}, u32[]{:S(2)}) %collective-permute-start.20) | collective-permute-done | bytes 131104 | tf_op jit(solution)/shard_map/ppermute | solution.py:29
  109.8 4.2 %collective-permute-start.25 = (bf16[64,1024]{1,0:T(8,128)(2,1)S(1)}, bf16[64,1024]{1,0:T(8,128)(2,1)S(1)}, u32[]{:S(2)}, u32[]{:S(2)}) collective-permute-start(bf16[64,1024]{1,0:T(8,128)(2,1)S(1)} %get-tuple-element.29), channel_id=1, source_target_pairs={{0,7},{1,0},{2,1},{3,2},{4,3},{5,4},{6,5},{7,6},{8,15},{9,8},{10,9... | collective-permute-start | bytes 393224 | tf_op jit(solution)/shard_map/ppermute | solution.py:29
  114.0 1.3 %collective-permute-done.22.refs_3_ = bf16[64,1024]{1,0:T(8,128)(2,1)S(1)} collective-permute-done((bf16[64,1024]{1,0:T(8,128)(2,1)}, bf16[64,1024]{1,0:T(8,128)(2,1)S(1)}, u32[]{:S(2)}, u32[]{:S(2)}) %collective-permute-start.22) | collective-permute-done | bytes 131104 | tf_op jit(solution)/shard_map/ppermute | solution.py:29
  115.9 0.8 collective-permute-done.24.refs_5_
  116.8 0.6 all-to-all-done.3.image_parts
  117.4 1.2 %sums.1 = (f32[64,1024]{1,0:T(8,128)}, f32[64,1024]{1,0:T(8,128)}) custom-call(bf16[16,64,1024]{2,1,0:T(8,128)(2,1)S(1)} %all-to-all-done.3.image_parts, f32[64,1024]{1,0:T(8,128)S(1)} %get-tuple-element.22.own_ref, bf16[64,1024]{1,0:T(8,128)(2,1)S(1)} %collective-permute-done.19.refs_0_, bf16[64,1024]{1,0:T(8,128)(2,1)S(1)} %collective-permute-done.20.refs_1_, ...), custom_call_target="tpu_custom_call" | custom-call | flops 1572864 | bytes 4194304 | tf_op jit(solution)/shard_map/sums/pallas_call | solution.py:385
  (38 shorter events, 3.1 us)
Async XLA Ops:
  3.0 7.6 %copy-start = (bf16[64,1024]{1,0:T(8,128)(2,1)S(1)}, bf16[64,1024]{1,0:T(8,128)(2,1)}, u32[]{:S(2)}) copy-start(bf16[64,1024]{1,0:T(8,128)(2,1)} %refs_0_.1) | copy-start | bytes 393220
  3.0 38.0 %copy-start.1 = (s32[16384]{0:T(1024)S(1)}, s32[16384]{0:T(1024)}, u32[]{:S(2)}) copy-start(s32[16384]{0:T(1024)} %param.5) | copy-start | bytes 196612
  3.1 38.0 %all-to-all-start = ((bf16[16,64,1024]{2,1,0:T(8,128)(2,1)}), bf16[16,64,1024]{2,1,0:T(8,128)(2,1)}, u32[]{:S(2)}, u32[]{:S(2)}) async-start(bf16[16,64,1024]{2,1,0:T(8,128)(2,1)} %repeat.1), calls=%async_computation | async-start | bytes 4194304 | tf_op jit(solution)/shard_map/all_to_all | solution.py:403
  10.6 8.5 %collective-permute-start = (bf16[64,1024]{1,0:T(8,128)(2,1)S(1)}, bf16[64,1024]{1,0:T(8,128)(2,1)S(1)}, u32[]{:S(2)}, u32[]{:S(2)}) collective-permute-start(bf16[64,1024]{1,0:T(8,128)(2,1)S(1)} %copy-done), channel_id=1, source_target_pairs={{0,7},{1,0},{2,1},{3,2},{4,3},{5,4},{6,5},{7,6},{8,15},{9,8},{10,9... | collective-permute-start | bytes 393224 | tf_op jit(solution)/shard_map/ppermute | solution.py:29
  16.5 6.2 %collective-permute-start.4 = (bf16[64,1024]{1,0:T(8,128)(2,1)S(1)}, bf16[64,1024]{1,0:T(8,128)(2,1)S(1)}, u32[]{:S(2)}, u32[]{:S(2)}) collective-permute-start(bf16[64,1024]{1,0:T(8,128)(2,1)S(1)} %copy-done), channel_id=1, source_target_pairs={{0,1},{1,2},{2,3},{3,4},{4,5},{5,6},{6,7},{7,0},{8,9},{9,10},{10,1... | collective-permute-start | bytes 393224 | tf_op jit(solution)/shard_map/ppermute | solution.py:29
  19.1 6.2 %collective-permute-start.1 = (bf16[64,1024]{1,0:T(8,128)(2,1)S(1)}, bf16[64,1024]{1,0:T(8,128)(2,1)S(1)}, u32[]{:S(2)}, u32[]{:S(2)}) collective-permute-start(bf16[64,1024]{1,0:T(8,128)(2,1)S(1)} %collective-permute-done.refs_1_), channel_id=1, source_target_pairs={{0,7},{1,0},{2,1},{3,2},{4,3},{5,4},{6,5},{7,6},{8,15},{9,8},{10,9... | collective-permute-start | bytes 393224 | tf_op jit(solution)/shard_map/ppermute | solution.py:29
  22.7 6.7 %collective-permute-start.5 = (bf16[64,1024]{1,0:T(8,128)(2,1)S(1)}, bf16[64,1024]{1,0:T(8,128)(2,1)S(1)}, u32[]{:S(2)}, u32[]{:S(2)}) collective-permute-start(bf16[64,1024]{1,0:T(8,128)(2,1)S(1)} %collective-permute-done.4.refs_7_), channel_id=1, source_target_pairs={{0,1},{1,2},{2,3},{3,4},{4,5},{5,6},{6,7},{7,0},{8,9},{9,10},{10,1... | collective-permute-start | bytes 393224 | tf_op jit(solution)/shard_map/ppermute | solution.py:29
  25.2 6.2 %collective-permute-start.2 = (bf16[64,1024]{1,0:T(8,128)(2,1)S(1)}, bf16[64,1024]{1,0:T(8,128)(2,1)S(1)}, u32[]{:S(2)}, u32[]{:S(2)}) collective-permute-start(bf16[64,1024]{1,0:T(8,128)(2,1)S(1)} %collective-permute-done.1.refs_2_), channel_id=1, source_target_pairs={{0,7},{1,0},{2,1},{3,2},{4,3},{5,4},{6,5},{7,6},{8,15},{9,8},{10,9... | collective-permute-start | bytes 393224 | tf_op jit(solution)/shard_map/ppermute | solution.py:29
  28.9 6.2 %collective-permute-start.7 = (bf16[64,1024]{1,0:T(8,128)(2,1)S(1)}, bf16[64,1024]{1,0:T(8,128)(2,1)S(1)}, u32[]{:S(2)}, u32[]{:S(2)}) collective-permute-start(bf16[64,1024]{1,0:T(8,128)(2,1)S(1)} %copy-done), channel_id=1, source_target_pairs={{0,32},{32,0},{1,33},{33,1},{2,34},{34,2},{3,35},{35,3},{4,36},{36... | collective-permute-start | bytes 393224 | tf_op jit(solution)/shard_map/ppermute | solution.py:24
  28.9 6.2 %collective-permute-start.14 = (bf16[64,1024]{1,0:T(8,128)(2,1)S(1)}, bf16[64,1024]{1,0:T(8,128)(2,1)S(1)}, u32[]{:S(2)}, u32[]{:S(2)}) collective-permute-start(bf16[64,1024]{1,0:T(8,128)(2,1)S(1)} %collective-permute-done.4.refs_7_), channel_id=1, source_target_pairs={{0,32},{32,0},{1,33},{33,1},{2,34},{34,2},{3,35},{35,3},{4,36},{36... | collective-permute-start | bytes 393224 | tf_op jit(solution)/shard_map/ppermute | solution.py:24
  29.4 6.2 %collective-permute-start.8 = (bf16[64,1024]{1,0:T(8,128)(2,1)S(1)}, bf16[64,1024]{1,0:T(8,128)(2,1)S(1)}, u32[]{:S(2)}, u32[]{:S(2)}) collective-permute-start(bf16[64,1024]{1,0:T(8,128)(2,1)S(1)} %collective-permute-done.refs_1_), channel_id=1, source_target_pairs={{0,32},{32,0},{1,33},{33,1},{2,34},{34,2},{3,35},{35,3},{4,36},{36... | collective-permute-start | bytes 393224 | tf_op jit(solution)/shard_map/ppermute | solution.py:24
  29.4 7.1 %collective-permute-start.6 = (bf16[64,1024]{1,0:T(8,128)(2,1)S(1)}, bf16[64,1024]{1,0:T(8,128)(2,1)S(1)}, u32[]{:S(2)}, u32[]{:S(2)}) collective-permute-start(bf16[64,1024]{1,0:T(8,128)(2,1)S(1)} %collective-permute-done.5.refs_6_), channel_id=1, source_target_pairs={{0,1},{1,2},{2,3},{3,4},{4,5},{5,6},{6,7},{7,0},{8,9},{9,10},{10,1... | collective-permute-start | bytes 393224 | tf_op jit(solution)/shard_map/ppermute | solution.py:29
  31.4 6.2 %collective-permute-start.3 = (bf16[64,1024]{1,0:T(8,128)(2,1)S(1)}, bf16[64,1024]{1,0:T(8,128)(2,1)S(1)}, u32[]{:S(2)}, u32[]{:S(2)}) collective-permute-start(bf16[64,1024]{1,0:T(8,128)(2,1)S(1)} %collective-permute-done.2.refs_3_), channel_id=1, source_target_pairs={{0,7},{1,0},{2,1},{3,2},{4,3},{5,4},{6,5},{7,6},{8,15},{9,8},{10,9... | collective-permute-start | bytes 393224 | tf_op jit(solution)/shard_map/ppermute | solution.py:29
  35.1 2.5 %collective-permute-start.13 = (bf16[64,1024]{1,0:T(8,128)(2,1)S(1)}, bf16[64,1024]{1,0:T(8,128)(2,1)S(1)}, u32[]{:S(2)}, u32[]{:S(2)}) collective-permute-start(bf16[64,1024]{1,0:T(8,128)(2,1)S(1)} %collective-permute-done.5.refs_6_), channel_id=1, source_target_pairs={{0,32},{32,0},{1,33},{33,1},{2,34},{34,2},{3,35},{35,3},{4,36},{36... | collective-permute-start | bytes 393224 | tf_op jit(solution)/shard_map/ppermute | solution.py:24
  35.1 6.0 %collective-permute-start.9 = (bf16[64,1024]{1,0:T(8,128)(2,1)S(1)}, bf16[64,1024]{1,0:T(8,128)(2,1)S(1)}, u32[]{:S(2)}, u32[]{:S(2)}) collective-permute-start(bf16[64,1024]{1,0:T(8,128)(2,1)S(1)} %collective-permute-done.1.refs_2_), channel_id=1, source_target_pairs={{0,32},{32,0},{1,33},{33,1},{2,34},{34,2},{3,35},{35,3},{4,36},{36... | collective-permute-start | bytes 393224 | tf_op jit(solution)/shard_map/ppermute | solution.py:24
  35.6 5.5 %collective-permute-start.10 = (bf16[64,1024]{1,0:T(8,128)(2,1)S(1)}, bf16[64,1024]{1,0:T(8,128)(2,1)S(1)}, u32[]{:S(2)}, u32[]{:S(2)}) collective-permute-start(bf16[64,1024]{1,0:T(8,128)(2,1)S(1)} %collective-permute-done.2.refs_3_), channel_id=1, source_target_pairs={{0,32},{32,0},{1,33},{33,1},{2,34},{34,2},{3,35},{35,3},{4,36},{36... | collective-permute-start | bytes 393224 | tf_op jit(solution)/shard_map/ppermute | solution.py:24
  36.5 4.5 %collective-permute-start.12 = (bf16[64,1024]{1,0:T(8,128)(2,1)S(1)}, bf16[64,1024]{1,0:T(8,128)(2,1)S(1)}, u32[]{:S(2)}, u32[]{:S(2)}) collective-permute-start(bf16[64,1024]{1,0:T(8,128)(2,1)S(1)} %collective-permute-done.6.refs_5_), channel_id=1, source_target_pairs={{0,32},{32,0},{1,33},{33,1},{2,34},{34,2},{3,35},{35,3},{4,36},{36... | collective-permute-start | bytes 393224 | tf_op jit(solution)/shard_map/ppermute | solution.py:24
  37.6 3.5 %collective-permute-start.11 = (bf16[64,1024]{1,0:T(8,128)(2,1)S(1)}, bf16[64,1024]{1,0:T(8,128)(2,1)S(1)}, u32[]{:S(2)}, u32[]{:S(2)}) collective-permute-start(bf16[64,1024]{1,0:T(8,128)(2,1)S(1)} %collective-permute-done.3.refs_4_), channel_id=1, source_target_pairs={{0,32},{32,0},{1,33},{33,1},{2,34},{34,2},{3,35},{35,3},{4,36},{36... | collective-permute-start | bytes 393224 | tf_op jit(solution)/shard_map/ppermute | solution.py:24
  41.1 36.4 %collective-permute-start.16 = (bf16[1024,1024]{1,0:T(8,128)(2,1)}, bf16[1024,1024]{1,0:T(8,128)(2,1)}, u32[]{:S(2)}, u32[]{:S(2)}) collective-permute-start(bf16[1024,1024]{1,0:T(8,128)(2,1)} %bitcast.rows_ref), channel_id=1, source_target_pairs={{0,32},{32,0},{1,33},{33,1},{2,34},{34,2},{3,35},{35,3},{4,36},{36... | collective-permute-start | bytes 6291464 | tf_op jit(solution)/shard_map/ppermute | solution.py:24
  48.4 29.1 %collective-permute-start.15 = (f32[1024,512]{1,0:T(8,128)}, f32[1024,512]{1,0:T(8,128)}, u32[]{:S(2)}, u32[]{:S(2)}) collective-permute-start(f32[1024,512]{1,0:T(8,128)} %get-tuple-element.17.far_ref), channel_id=1, source_target_pairs={{0,32},{32,0},{1,33},{33,1},{2,34},{34,2},{3,35},{35,3},{4,36},{36... | collective-permute-start | bytes 6291464 | tf_op jit(solution)/shard_map/ppermute | solution.py:24
  49.0 8.6 %collective-permute-start.17 = (f32[8,128]{1,0:T(8,128)S(1)}, f32[8,128]{1,0:T(8,128)S(1)}, u32[]{:S(2)}, u32[]{:S(2)}) collective-permute-start(f32[8,128]{1,0:T(8,128)S(1)} %get-tuple-element.19), channel_id=1, source_target_pairs={{0,32},{32,0},{1,33},{33,1},{2,34},{34,2},{3,35},{35,3},{4,36},{36... | collective-permute-start | bytes 12296 | tf_op jit(solution)/shard_map/ppermute | solution.py:24
  49.1 16.5 %all-to-all-start.2 = ((f32[8,8,128]{2,1,0:T(8,128)}), f32[8,8,128]{2,1,0:T(8,128)S(1)}, u32[]{:S(2)}, u32[]{:S(2)}) async-start(f32[8,8,128]{2,1,0:T(8,128)} %get-tuple-element.20), calls=%async_computation.2 | async-start | bytes 65536 | tf_op jit(solution)/shard_map/all_to_all | solution.py:415
  66.2 11.2 %all-to-all-start.1 = ((f32[16,2,8,128]{3,2,1,0:T(8,128)}), f32[16,2,8,128]{3,2,1,0:T(8,128)S(1)}, u32[]{:S(2)}, u32[]{:S(2)}) async-start(f32[16,2,8,128]{3,2,1,0:T(8,128)} %broadcast_in_dim.2), calls=%async_computation.1 | async-start | bytes 262144 | tf_op jit(solution)/shard_map/all_to_all | solution.py:416
  71.1 1.2 %collective-permute-start.18 = (f32[8,8,128]{2,1,0:T(8,128)S(1)}, f32[8,8,128]{2,1,0:T(8,128)S(1)}, u32[]{:S(2)}, u32[]{:S(2)}) collective-permute-start(f32[8,8,128]{2,1,0:T(8,128)S(1)} %all-to-all-done.2.col_parts), channel_id=1, source_target_pairs={{0,32},{32,0},{1,33},{33,1},{2,34},{34,2},{3,35},{35,3},{4,36},{36... | collective-permute-start | bytes 98312 | tf_op jit(solution)/shard_map/ppermute | solution.py:24
  86.8 30.6 %all-to-all-start.3 = ((bf16[16,64,1024]{2,1,0:T(8,128)(2,1)}), bf16[16,64,1024]{2,1,0:T(8,128)(2,1)S(1)}, u32[]{:S(2)}, u32[]{:S(2)}) async-start(bf16[16,64,1024]{2,1,0:T(8,128)(2,1)} %bitcast.7), calls=%async_computation.3 | async-start | bytes 4194304 | tf_op jit(solution)/shard_map/all_to_all | solution.py:422
  92.1 14.6 %collective-permute-start.19 = (bf16[64,1024]{1,0:T(8,128)(2,1)S(1)}, bf16[64,1024]{1,0:T(8,128)(2,1)S(1)}, u32[]{:S(2)}, u32[]{:S(2)}) collective-permute-start(bf16[64,1024]{1,0:T(8,128)(2,1)S(1)} %get-tuple-element.23), channel_id=1, source_target_pairs={{0,4},{1,5},{2,6},{3,7},{4,0},{5,1},{6,2},{7,3},{8,12},{9,13},{10,... | collective-permute-start | bytes 393224 | tf_op jit(solution)/shard_map/ppermute | solution.py:29
  92.6 17.3 %collective-permute-start.20 = (bf16[64,1024]{1,0:T(8,128)(2,1)S(1)}, bf16[64,1024]{1,0:T(8,128)(2,1)S(1)}, u32[]{:S(2)}, u32[]{:S(2)}) collective-permute-start(bf16[64,1024]{1,0:T(8,128)(2,1)S(1)} %get-tuple-element.24), channel_id=1, source_target_pairs={{0,3},{1,4},{2,5},{3,6},{4,7},{5,0},{6,1},{7,2},{8,11},{9,12},{10,... | collective-permute-start | bytes 393224 | tf_op jit(solution)/shard_map/ppermute | solution.py:29
  95.7 18.3 %collective-permute-start.21 = (bf16[64,1024]{1,0:T(8,128)(2,1)}, bf16[64,1024]{1,0:T(8,128)(2,1)S(1)}, u32[]{:S(2)}, u32[]{:S(2)}) collective-permute-start(bf16[64,1024]{1,0:T(8,128)(2,1)} %get-tuple-element.25), channel_id=1, source_target_pairs={{0,5},{1,6},{2,7},{3,0},{4,1},{5,2},{6,3},{7,4},{8,13},{9,14},{10,... | collective-permute-start | bytes 393224 | tf_op jit(solution)/shard_map/ppermute | solution.py:29
  97.6 17.7 %collective-permute-start.22 = (bf16[64,1024]{1,0:T(8,128)(2,1)}, bf16[64,1024]{1,0:T(8,128)(2,1)S(1)}, u32[]{:S(2)}, u32[]{:S(2)}) collective-permute-start(bf16[64,1024]{1,0:T(8,128)(2,1)} %get-tuple-element.26), channel_id=1, source_target_pairs={{0,2},{1,3},{2,4},{3,5},{4,6},{5,7},{6,0},{7,1},{8,10},{9,11},{10,... | collective-permute-start | bytes 393224 | tf_op jit(solution)/shard_map/ppermute | solution.py:29
  100.0 15.9 %collective-permute-start.23 = (bf16[64,1024]{1,0:T(8,128)(2,1)}, bf16[64,1024]{1,0:T(8,128)(2,1)S(1)}, u32[]{:S(2)}, u32[]{:S(2)}) collective-permute-start(bf16[64,1024]{1,0:T(8,128)(2,1)} %get-tuple-element.27), channel_id=1, source_target_pairs={{0,6},{1,7},{2,0},{3,1},{4,2},{5,3},{6,4},{7,5},{8,14},{9,15},{10,... | collective-permute-start | bytes 393224 | tf_op jit(solution)/shard_map/ppermute | solution.py:29
  106.7 10.0 %collective-permute-start.24 = (bf16[64,1024]{1,0:T(8,128)(2,1)S(1)}, bf16[64,1024]{1,0:T(8,128)(2,1)S(1)}, u32[]{:S(2)}, u32[]{:S(2)}) collective-permute-start(bf16[64,1024]{1,0:T(8,128)(2,1)S(1)} %get-tuple-element.28), channel_id=1, source_target_pairs={{0,1},{1,2},{2,3},{3,4},{4,5},{5,6},{6,7},{7,0},{8,9},{9,10},{10,1... | collective-permute-start | bytes 393224 | tf_op jit(solution)/shard_map/ppermute | solution.py:29
  109.8 7.0 %collective-permute-start.25 = (bf16[64,1024]{1,0:T(8,128)(2,1)S(1)}, bf16[64,1024]{1,0:T(8,128)(2,1)S(1)}, u32[]{:S(2)}, u32[]{:S(2)}) collective-permute-start(bf16[64,1024]{1,0:T(8,128)(2,1)S(1)} %get-tuple-element.29), channel_id=1, source_target_pairs={{0,7},{1,0},{2,1},{3,2},{4,3},{5,4},{6,5},{7,6},{8,15},{9,8},{10,9... | collective-permute-start | bytes 393224 | tf_op jit(solution)/shard_map/ppermute | solution.py:29

commit v6 on v5

--- a/solution.py
+++ b/solution.py
@@ -15,7 +15,7 @@
 block = 256
 
 axes = ("y", "core", "x", "z")
-plane = ("y", "x")
+plane = ("x", "y")
 in_vmem = pl.BlockSpec(memory_space=pltpu.VMEM)
 in_hbm = pl.BlockSpec(memory_space=pltpu.HBM)
 
@@ -81,8 +81,8 @@
     y, core, x, z = place
     at = start + lax.broadcasted_iota(jnp.int32, (count, 1), 0)
     member = at // span
-    n_x, n_z, n_core = 4, 8, 2
-    return (((member // n_x * n_core + core) * n_x + member % n_x) * n_z + z) * span + at % span
+    n_y, n_x, n_z, n_core = 4, 4, 8, 2
+    return (((member % n_y * n_core + core) * n_x + member // n_y) * n_z + z) * span + at % span
 
 
 def col_ids(place, count, span):
@@ -103,14 +103,14 @@
 
 def group_rows(place, group_ref):
     y, core, x, z = place
-    n_x, n_z, n_plane = 4, 8, 16
+    n_y, n_z, n_plane = 4, 8, 16
 
     def ids(at):
         return group_ref[pl.ds(at, 1), :].astype(jnp.float32)
 
     rows = []
     for j in range(n_plane // 2):
-        a, b = [ids(((m // n_x) * 2 + core) * 16 + (m % n_x) * 4 + z // 2) for m in (2 * j, 2 * j + 1)]
+        a, b = [ids(((m % n_y) * 2 + core) * 16 + (m // n_y) * 4 + z // 2) for m in (2 * j, 2 * j + 1)]
         rows.append(halves(a, b, lax.rem(z, 2)))
     cols = []
     for side in (core, 1 - core):

time: 121 us -> 119 us (0.983); the launches traced: 119 us -> 119 us
    all_to_all x1, waiting for transfers between devices: 3.46 us -> 2.12 us  [per_device(): rows = lax.all_to_all(repeat(image_emb, n_plane), plane, 0, 0)]
    all_to_all x1, waiting for transfers between devices: 0.61 us -> 1.93 us  [per_device(): lax.all_to_all(image_part.reshape(n_plane, span, width), plane, 0, 0)]
where the time goes in v6:
time: 119 us
  starting transfers between devices  58.9 us (49%)
  waiting for transfers between devices  38.3 us (32%)
  Pallas kernels  20.2 us (17%)
    ppermute x14, starting transfers between devices, shift(): lax.ppermute(values, axis, [(i, (i + step) % size) for i in range(size)])  30.8 us
    ppermute x14, waiting for transfers between devices, shift(): lax.ppermute(values, axis, [(i, (i + step) % size) for i in range(size)])  19.8 us
    pallas_call x1, Pallas kernels, block_grad(): pl.pallas_call(grad_kernel, in_specs=[in_hbm] * 6 + [in_vmem] * len(parts...  9.33 us
    all_to_all x1, starting transfers between devices, per_device(): col_parts = lax.all_to_all(col_part, 'z', 0, 0)  8.47 us
    all_to_all x1, waiting for transfers between devices, per_device(): col_parts = lax.all_to_all(col_part, 'z', 0, 0)  8.01 us
    all_to_all x1, starting transfers between devices, per_device(): rows = lax.all_to_all(repeat(image_emb, n_plane), plane, 0, 0)  7.54 us
    pallas_call x1, Pallas kernels, block_stats(): pl.pallas_call(stats_kernel, in_specs=[in_hbm] * 2 + [in_vmem] * len(shar...  7.27 us
    all_to_all x1, starting transfers between devices, per_device(): lax.all_to_all(image_part.reshape(n_plane, span, width), plane, 0, 0)  5.28 us
  transfers between devices with their start and end apart: 30, of which 16 were waited for; matrix products, arithmetic and copies ran while one was open for 1% of the time, Pallas kernels for 6%

profile of v6, /device:TPU:8, one launch (start us, length us, event | category | flops | bytes accessed | tf_op | source)
XLA Modules:
  0.0 119.0 jit_solution(15769378868427436087)
XLA Ops:
  0.6 2.4 %repeat.1 = bf16[16,64,1024]{2,1,0:T(8,128)(2,1)} custom-call(bf16[64,1024]{1,0:T(8,128)(2,1)} %in_ref.1), custom_call_target="tpu_custom_call" | custom-call | bytes 2097152 | tf_op jit(solution)/shard_map/repeat/pallas_call | solution.py:135
  3.1 7.5 %all-to-all-start = ((bf16[16,64,1024]{2,1,0:T(8,128)(2,1)}), bf16[16,64,1024]{2,1,0:T(8,128)(2,1)}, u32[]{:S(2)}, u32[]{:S(2)}) async-start(bf16[16,64,1024]{2,1,0:T(8,128)(2,1)} %repeat.1), calls=%async_computation | async-start | bytes 4194304 | tf_op jit(solution)/shard_map/all_to_all | solution.py:403
  10.6 5.9 %collective-permute-start = (bf16[64,1024]{1,0:T(8,128)(2,1)S(1)}, bf16[64,1024]{1,0:T(8,128)(2,1)S(1)}, u32[]{:S(2)}, u32[]{:S(2)}) collective-permute-start(bf16[64,1024]{1,0:T(8,128)(2,1)S(1)} %copy-done), channel_id=1, source_target_pairs={{0,7},{1,0},{2,1},{3,2},{4,3},{5,4},{6,5},{7,6},{8,15},{9,8},{10,9... | collective-permute-start | bytes 393224 | tf_op jit(solution)/shard_map/ppermute | solution.py:29
  16.5 2.5 %collective-permute-done.refs_1_ = bf16[64,1024]{1,0:T(8,128)(2,1)S(1)} collective-permute-done((bf16[64,1024]{1,0:T(8,128)(2,1)S(1)}, bf16[64,1024]{1,0:T(8,128)(2,1)S(1)}, u32[]{:S(2)}, u32[]{:S(2)}) %collective-permute-start) | collective-permute-done | bytes 131104 | tf_op jit(solution)/shard_map/ppermute | solution.py:29
  19.0 3.7 %collective-permute-start.1 = (bf16[64,1024]{1,0:T(8,128)(2,1)S(1)}, bf16[64,1024]{1,0:T(8,128)(2,1)S(1)}, u32[]{:S(2)}, u32[]{:S(2)}) collective-permute-start(bf16[64,1024]{1,0:T(8,128)(2,1)S(1)} %collective-permute-done.refs_1_), channel_id=1, source_target_pairs={{0,7},{1,0},{2,1},{3,2},{4,3},{5,4},{6,5},{7,6},{8,15},{9,8},{10,9... | collective-permute-start | bytes 393224 | tf_op jit(solution)/shard_map/ppermute | solution.py:29
  22.7 2.5 %collective-permute-done.1.refs_2_ = bf16[64,1024]{1,0:T(8,128)(2,1)S(1)} collective-permute-done((bf16[64,1024]{1,0:T(8,128)(2,1)S(1)}, bf16[64,1024]{1,0:T(8,128)(2,1)S(1)}, u32[]{:S(2)}, u32[]{:S(2)}) %collective-permute-start.1) | collective-permute-done | bytes 131104 | tf_op jit(solution)/shard_map/ppermute | solution.py:29
  25.2 3.7 %collective-permute-start.2 = (bf16[64,1024]{1,0:T(8,128)(2,1)S(1)}, bf16[64,1024]{1,0:T(8,128)(2,1)S(1)}, u32[]{:S(2)}, u32[]{:S(2)}) collective-permute-start(bf16[64,1024]{1,0:T(8,128)(2,1)S(1)} %collective-permute-done.1.refs_2_), channel_id=1, source_target_pairs={{0,7},{1,0},{2,1},{3,2},{4,3},{5,4},{6,5},{7,6},{8,15},{9,8},{10,9... | collective-permute-start | bytes 393224 | tf_op jit(solution)/shard_map/ppermute | solution.py:29
  29.4 2.0 %collective-permute-done.2.refs_3_ = bf16[64,1024]{1,0:T(8,128)(2,1)S(1)} collective-permute-done((bf16[64,1024]{1,0:T(8,128)(2,1)S(1)}, bf16[64,1024]{1,0:T(8,128)(2,1)S(1)}, u32[]{:S(2)}, u32[]{:S(2)}) %collective-permute-start.2) | collective-permute-done | bytes 131104 | tf_op jit(solution)/shard_map/ppermute | solution.py:29
  31.4 3.7 %collective-permute-start.3 = (bf16[64,1024]{1,0:T(8,128)(2,1)S(1)}, bf16[64,1024]{1,0:T(8,128)(2,1)S(1)}, u32[]{:S(2)}, u32[]{:S(2)}) collective-permute-start(bf16[64,1024]{1,0:T(8,128)(2,1)S(1)} %collective-permute-done.2.refs_3_), channel_id=1, source_target_pairs={{0,7},{1,0},{2,1},{3,2},{4,3},{5,4},{6,5},{7,6},{8,15},{9,8},{10,9... | collective-permute-start | bytes 393224 | tf_op jit(solution)/shard_map/ppermute | solution.py:29
  35.7 0.8 collective-permute-done.6.refs_5_
  36.5 1.1 collective-permute-done.3.refs_4_
  37.6 2.1 %all-to-all-done = bf16[16,64,1024]{2,1,0:T(8,128)(2,1)} async-done(((bf16[16,64,1024]{2,1,0:T(8,128)(2,1)}), bf16[16,64,1024]{2,1,0:T(8,128)(2,1)}, u32[]{:S(2)}, u32[]{:S(2)}) %all-to-all-start) | async-done | bytes 2097184 | tf_op jit(solution)/shard_map/all_to_all | solution.py:403
  39.8 7.3 %stats.1 = (f32[1024,512]{1,0:T(8,128)}, f32[1024,512]{1,0:T(8,128)}, bf16[1024,1024]{1,0:T(8,128)(2,1)}, f32[8,128]{1,0:T(8,128)S(1)}, f32[8,8,128]{2,1,0:T(8,128)}) custom-call(bf16[1024,1024]{1,0:T(8,128)(2,1)} %bitcast.rows_ref, s32[128,128]{1,0:T(8,128)S(1)} %bitcast.6, bf16[64,1024]{1,0:T(8,128)(2,1)S(1)} %copy-done, ...), custom_call_target="tpu_custom_call" | custom-call | flops 2147483648 | bytes 8388608 | tf_op jit(solution)/shard_map/stats/pallas_call | solution.py:219
  47.7 8.5 %all-to-all-start.2 = ((f32[8,8,128]{2,1,0:T(8,128)}), f32[8,8,128]{2,1,0:T(8,128)S(1)}, u32[]{:S(2)}, u32[]{:S(2)}) async-start(f32[8,8,128]{2,1,0:T(8,128)} %get-tuple-element.20), calls=%async_computation.2 | async-start | bytes 65536 | tf_op jit(solution)/shard_map/all_to_all | solution.py:415
  56.2 8.0 %all-to-all-done.2.col_parts = f32[8,8,128]{2,1,0:T(8,128)S(1)} async-done(((f32[8,8,128]{2,1,0:T(8,128)}), f32[8,8,128]{2,1,0:T(8,128)S(1)}, u32[]{:S(2)}, u32[]{:S(2)}) %all-to-all-start.2) | async-done | bytes 32800 | tf_op jit(solution)/shard_map/all_to_all | solution.py:415
  64.9 5.0 %all-to-all-start.1 = ((f32[16,2,8,128]{3,2,1,0:T(8,128)}), f32[16,2,8,128]{3,2,1,0:T(8,128)S(1)}, u32[]{:S(2)}, u32[]{:S(2)}) async-start(f32[16,2,8,128]{3,2,1,0:T(8,128)} %broadcast_in_dim.2), calls=%async_computation.1 | async-start | bytes 262144 | tf_op jit(solution)/shard_map/all_to_all | solution.py:416
  69.9 1.2 %collective-permute-done.18.col_others = f32[8,8,128]{2,1,0:T(8,128)S(1)} collective-permute-done((f32[8,8,128]{2,1,0:T(8,128)S(1)}, f32[8,8,128]{2,1,0:T(8,128)S(1)}, u32[]{:S(2)}, u32[]{:S(2)}) %collective-permute-start.18) | collective-permute-done | bytes 32800 | tf_op jit(solution)/shard_map/ppermute | solution.py:24
  71.1 5.2 %all-to-all-done.1.row_parts = f32[16,2,8,128]{3,2,1,0:T(8,128)S(1)} async-done(((f32[16,2,8,128]{3,2,1,0:T(8,128)}), f32[16,2,8,128]{3,2,1,0:T(8,128)S(1)}, u32[]{:S(2)}, u32[]{:S(2)}) %all-to-all-start.1) | async-done | bytes 131104 | tf_op jit(solution)/shard_map/all_to_all | solution.py:416
  76.3 9.3 %grad.1 = (bf16[1024,1024]{1,0:T(8,128)(2,1)}, f32[64,1024]{1,0:T(8,128)S(1)}, bf16[64,1024]{1,0:T(8,128)(2,1)S(1)}, bf16[64,1024]{1,0:T(8,128)(2,1)}, bf16[64,1...) custom-call(f32[1024,512]{1,0:T(8,128)} %get-tuple-element.16.near_r, ...), custom_call_target="tpu_custom_call" | custom-call | flops 4294967296 | bytes 14680064 | tf_op jit(solution)/shard_map/grad/pallas_call | solution.py:341
  85.6 5.3 %all-to-all-start.3 = ((bf16[16,64,1024]{2,1,0:T(8,128)(2,1)}), bf16[16,64,1024]{2,1,0:T(8,128)(2,1)S(1)}, u32[]{:S(2)}, u32[]{:S(2)}) async-start(bf16[16,64,1024]{2,1,0:T(8,128)(2,1)} %bitcast.7), calls=%async_computation.3 | async-start | bytes 4194304 | tf_op jit(solution)/shard_map/all_to_all | solution.py:422
  91.4 3.1 %collective-permute-start.20 = (bf16[64,1024]{1,0:T(8,128)(2,1)S(1)}, bf16[64,1024]{1,0:T(8,128)(2,1)S(1)}, u32[]{:S(2)}, u32[]{:S(2)}) collective-permute-start(bf16[64,1024]{1,0:T(8,128)(2,1)S(1)} %get-tuple-element.24), channel_id=1, source_target_pairs={{0,3},{1,4},{2,5},{3,6},{4,7},{5,0},{6,1},{7,2},{8,11},{9,12},{10,... | collective-permute-start | bytes 393224 | tf_op jit(solution)/shard_map/ppermute | solution.py:29
  94.5 1.9 %collective-permute-start.21 = (bf16[64,1024]{1,0:T(8,128)(2,1)}, bf16[64,1024]{1,0:T(8,128)(2,1)S(1)}, u32[]{:S(2)}, u32[]{:S(2)}) collective-permute-start(bf16[64,1024]{1,0:T(8,128)(2,1)} %get-tuple-element.25), channel_id=1, source_target_pairs={{0,5},{1,6},{2,7},{3,0},{4,1},{5,2},{6,3},{7,4},{8,13},{9,14},{10,... | collective-permute-start | bytes 393224 | tf_op jit(solution)/shard_map/ppermute | solution.py:29
  96.4 2.4 %collective-permute-start.22 = (bf16[64,1024]{1,0:T(8,128)(2,1)}, bf16[64,1024]{1,0:T(8,128)(2,1)S(1)}, u32[]{:S(2)}, u32[]{:S(2)}) collective-permute-start(bf16[64,1024]{1,0:T(8,128)(2,1)} %get-tuple-element.26), channel_id=1, source_target_pairs={{0,2},{1,3},{2,4},{3,5},{4,6},{5,7},{6,0},{7,1},{8,10},{9,11},{10,... | collective-permute-start | bytes 393224 | tf_op jit(solution)/shard_map/ppermute | solution.py:29
  98.8 1.8 %collective-permute-start.23 = (bf16[64,1024]{1,0:T(8,128)(2,1)}, bf16[64,1024]{1,0:T(8,128)(2,1)S(1)}, u32[]{:S(2)}, u32[]{:S(2)}) collective-permute-start(bf16[64,1024]{1,0:T(8,128)(2,1)} %get-tuple-element.27), channel_id=1, source_target_pairs={{0,6},{1,7},{2,0},{3,1},{4,2},{5,3},{6,4},{7,5},{8,14},{9,15},{10,... | collective-permute-start | bytes 393224 | tf_op jit(solution)/shard_map/ppermute | solution.py:29
  100.6 4.8 %collective-permute-done.19.refs_0_ = bf16[64,1024]{1,0:T(8,128)(2,1)S(1)} collective-permute-done((bf16[64,1024]{1,0:T(8,128)(2,1)S(1)}, bf16[64,1024]{1,0:T(8,128)(2,1)S(1)}, u32[]{:S(2)}, u32[]{:S(2)}) %collective-permute-start.19) | collective-permute-done | bytes 131104 | tf_op jit(solution)/shard_map/ppermute | solution.py:29
  105.3 3.3 %collective-permute-done.20.refs_1_ = bf16[64,1024]{1,0:T(8,128)(2,1)S(1)} collective-permute-done((bf16[64,1024]{1,0:T(8,128)(2,1)S(1)}, bf16[64,1024]{1,0:T(8,128)(2,1)S(1)}, u32[]{:S(2)}, u32[]{:S(2)}) %collective-permute-start.20) | collective-permute-done | bytes 131104 | tf_op jit(solution)/shard_map/ppermute | solution.py:29
  108.7 4.2 %collective-permute-start.25 = (bf16[64,1024]{1,0:T(8,128)(2,1)S(1)}, bf16[64,1024]{1,0:T(8,128)(2,1)S(1)}, u32[]{:S(2)}, u32[]{:S(2)}) collective-permute-start(bf16[64,1024]{1,0:T(8,128)(2,1)S(1)} %get-tuple-element.29), channel_id=1, source_target_pairs={{0,7},{1,0},{2,1},{3,2},{4,3},{5,4},{6,5},{7,6},{8,15},{9,8},{10,9... | collective-permute-start | bytes 393224 | tf_op jit(solution)/shard_map/ppermute | solution.py:29
  112.8 1.3 %collective-permute-done.22.refs_3_ = bf16[64,1024]{1,0:T(8,128)(2,1)S(1)} collective-permute-done((bf16[64,1024]{1,0:T(8,128)(2,1)}, bf16[64,1024]{1,0:T(8,128)(2,1)S(1)}, u32[]{:S(2)}, u32[]{:S(2)}) %collective-permute-start.22) | collective-permute-done | bytes 131104 | tf_op jit(solution)/shard_map/ppermute | solution.py:29
  114.1 0.7 collective-permute-done.23.refs_4_
  114.8 0.7 collective-permute-done.24.refs_5_
  115.6 1.9 %all-to-all-done.3.image_parts = bf16[16,64,1024]{2,1,0:T(8,128)(2,1)S(1)} async-done(((bf16[16,64,1024]{2,1,0:T(8,128)(2,1)}), bf16[16,64,1024]{2,1,0:T(8,128)(2,1)S(1)}, u32[]{:S(2)}, u32[]{:S(2)}) %all-to-all-start.3) | async-done | bytes 2097184 | tf_op jit(solution)/shard_map/all_to_all | solution.py:422
  117.6 1.2 %sums.1 = (f32[64,1024]{1,0:T(8,128)}, f32[64,1024]{1,0:T(8,128)}) custom-call(bf16[16,64,1024]{2,1,0:T(8,128)(2,1)S(1)} %all-to-all-done.3.image_parts, f32[64,1024]{1,0:T(8,128)S(1)} %get-tuple-element.22.own_ref, bf16[64,1024]{1,0:T(8,128)(2,1)S(1)} %collective-permute-done.19.refs_0_, bf16[64,1024]{1,0:T(8,128)(2,1)S(1)} %collective-permute-done.20.refs_1_, ...), custom_call_target="tpu_custom_call" | custom-call | flops 1572864 | bytes 4194304 | tf_op jit(solution)/shard_map/sums/pallas_call | solution.py:385
  (38 shorter events, 3.3 us)
Async XLA Ops:
  3.0 7.6 %copy-start = (bf16[64,1024]{1,0:T(8,128)(2,1)S(1)}, bf16[64,1024]{1,0:T(8,128)(2,1)}, u32[]{:S(2)}) copy-start(bf16[64,1024]{1,0:T(8,128)(2,1)} %refs_0_.1) | copy-start | bytes 393220
  3.0 36.7 %copy-start.1 = (s32[16384]{0:T(1024)S(1)}, s32[16384]{0:T(1024)}, u32[]{:S(2)}) copy-start(s32[16384]{0:T(1024)} %param.5) | copy-start | bytes 196612
  3.1 36.7 %all-to-all-start = ((bf16[16,64,1024]{2,1,0:T(8,128)(2,1)}), bf16[16,64,1024]{2,1,0:T(8,128)(2,1)}, u32[]{:S(2)}, u32[]{:S(2)}) async-start(bf16[16,64,1024]{2,1,0:T(8,128)(2,1)} %repeat.1), calls=%async_computation | async-start | bytes 4194304 | tf_op jit(solution)/shard_map/all_to_all | solution.py:403
  10.6 8.5 %collective-permute-start = (bf16[64,1024]{1,0:T(8,128)(2,1)S(1)}, bf16[64,1024]{1,0:T(8,128)(2,1)S(1)}, u32[]{:S(2)}, u32[]{:S(2)}) collective-permute-start(bf16[64,1024]{1,0:T(8,128)(2,1)S(1)} %copy-done), channel_id=1, source_target_pairs={{0,7},{1,0},{2,1},{3,2},{4,3},{5,4},{6,5},{7,6},{8,15},{9,8},{10,9... | collective-permute-start | bytes 393224 | tf_op jit(solution)/shard_map/ppermute | solution.py:29
  16.5 6.2 %collective-permute-start.4 = (bf16[64,1024]{1,0:T(8,128)(2,1)S(1)}, bf16[64,1024]{1,0:T(8,128)(2,1)S(1)}, u32[]{:S(2)}, u32[]{:S(2)}) collective-permute-start(bf16[64,1024]{1,0:T(8,128)(2,1)S(1)} %copy-done), channel_id=1, source_target_pairs={{0,1},{1,2},{2,3},{3,4},{4,5},{5,6},{6,7},{7,0},{8,9},{9,10},{10,1... | collective-permute-start | bytes 393224 | tf_op jit(solution)/shard_map/ppermute | solution.py:29
  19.0 6.2 %collective-permute-start.1 = (bf16[64,1024]{1,0:T(8,128)(2,1)S(1)}, bf16[64,1024]{1,0:T(8,128)(2,1)S(1)}, u32[]{:S(2)}, u32[]{:S(2)}) collective-permute-start(bf16[64,1024]{1,0:T(8,128)(2,1)S(1)} %collective-permute-done.refs_1_), channel_id=1, source_target_pairs={{0,7},{1,0},{2,1},{3,2},{4,3},{5,4},{6,5},{7,6},{8,15},{9,8},{10,9... | collective-permute-start | bytes 393224 | tf_op jit(solution)/shard_map/ppermute | solution.py:29
  22.7 6.7 %collective-permute-start.5 = (bf16[64,1024]{1,0:T(8,128)(2,1)S(1)}, bf16[64,1024]{1,0:T(8,128)(2,1)S(1)}, u32[]{:S(2)}, u32[]{:S(2)}) collective-permute-start(bf16[64,1024]{1,0:T(8,128)(2,1)S(1)} %collective-permute-done.4.refs_7_), channel_id=1, source_target_pairs={{0,1},{1,2},{2,3},{3,4},{4,5},{5,6},{6,7},{7,0},{8,9},{9,10},{10,1... | collective-permute-start | bytes 393224 | tf_op jit(solution)/shard_map/ppermute | solution.py:29
  25.2 6.2 %collective-permute-start.2 = (bf16[64,1024]{1,0:T(8,128)(2,1)S(1)}, bf16[64,1024]{1,0:T(8,128)(2,1)S(1)}, u32[]{:S(2)}, u32[]{:S(2)}) collective-permute-start(bf16[64,1024]{1,0:T(8,128)(2,1)S(1)} %collective-permute-done.1.refs_2_), channel_id=1, source_target_pairs={{0,7},{1,0},{2,1},{3,2},{4,3},{5,4},{6,5},{7,6},{8,15},{9,8},{10,9... | collective-permute-start | bytes 393224 | tf_op jit(solution)/shard_map/ppermute | solution.py:29
  28.9 6.2 %collective-permute-start.7 = (bf16[64,1024]{1,0:T(8,128)(2,1)S(1)}, bf16[64,1024]{1,0:T(8,128)(2,1)S(1)}, u32[]{:S(2)}, u32[]{:S(2)}) collective-permute-start(bf16[64,1024]{1,0:T(8,128)(2,1)S(1)} %copy-done), channel_id=1, source_target_pairs={{0,32},{32,0},{1,33},{33,1},{2,34},{34,2},{3,35},{35,3},{4,36},{36... | collective-permute-start | bytes 393224 | tf_op jit(solution)/shard_map/ppermute | solution.py:24
  28.9 6.2 %collective-permute-start.14 = (bf16[64,1024]{1,0:T(8,128)(2,1)S(1)}, bf16[64,1024]{1,0:T(8,128)(2,1)S(1)}, u32[]{:S(2)}, u32[]{:S(2)}) collective-permute-start(bf16[64,1024]{1,0:T(8,128)(2,1)S(1)} %collective-permute-done.4.refs_7_), channel_id=1, source_target_pairs={{0,32},{32,0},{1,33},{33,1},{2,34},{34,2},{3,35},{35,3},{4,36},{36... | collective-permute-start | bytes 393224 | tf_op jit(solution)/shard_map/ppermute | solution.py:24
  29.4 6.2 %collective-permute-start.8 = (bf16[64,1024]{1,0:T(8,128)(2,1)S(1)}, bf16[64,1024]{1,0:T(8,128)(2,1)S(1)}, u32[]{:S(2)}, u32[]{:S(2)}) collective-permute-start(bf16[64,1024]{1,0:T(8,128)(2,1)S(1)} %collective-permute-done.refs_1_), channel_id=1, source_target_pairs={{0,32},{32,0},{1,33},{33,1},{2,34},{34,2},{3,35},{35,3},{4,36},{36... | collective-permute-start | bytes 393224 | tf_op jit(solution)/shard_map/ppermute | solution.py:24
  29.4 7.1 %collective-permute-start.6 = (bf16[64,1024]{1,0:T(8,128)(2,1)S(1)}, bf16[64,1024]{1,0:T(8,128)(2,1)S(1)}, u32[]{:S(2)}, u32[]{:S(2)}) collective-permute-start(bf16[64,1024]{1,0:T(8,128)(2,1)S(1)} %collective-permute-done.5.refs_6_), channel_id=1, source_target_pairs={{0,1},{1,2},{2,3},{3,4},{4,5},{5,6},{6,7},{7,0},{8,9},{9,10},{10,1... | collective-permute-start | bytes 393224 | tf_op jit(solution)/shard_map/ppermute | solution.py:29
  31.4 6.2 %collective-permute-start.3 = (bf16[64,1024]{1,0:T(8,128)(2,1)S(1)}, bf16[64,1024]{1,0:T(8,128)(2,1)S(1)}, u32[]{:S(2)}, u32[]{:S(2)}) collective-permute-start(bf16[64,1024]{1,0:T(8,128)(2,1)S(1)} %collective-permute-done.2.refs_3_), channel_id=1, source_target_pairs={{0,7},{1,0},{2,1},{3,2},{4,3},{5,4},{6,5},{7,6},{8,15},{9,8},{10,9... | collective-permute-start | bytes 393224 | tf_op jit(solution)/shard_map/ppermute | solution.py:29
  35.1 2.5 %collective-permute-start.13 = (bf16[64,1024]{1,0:T(8,128)(2,1)S(1)}, bf16[64,1024]{1,0:T(8,128)(2,1)S(1)}, u32[]{:S(2)}, u32[]{:S(2)}) collective-permute-start(bf16[64,1024]{1,0:T(8,128)(2,1)S(1)} %collective-permute-done.5.refs_6_), channel_id=1, source_target_pairs={{0,32},{32,0},{1,33},{33,1},{2,34},{34,2},{3,35},{35,3},{4,36},{36... | collective-permute-start | bytes 393224 | tf_op jit(solution)/shard_map/ppermute | solution.py:24
  35.1 4.6 %collective-permute-start.9 = (bf16[64,1024]{1,0:T(8,128)(2,1)S(1)}, bf16[64,1024]{1,0:T(8,128)(2,1)S(1)}, u32[]{:S(2)}, u32[]{:S(2)}) collective-permute-start(bf16[64,1024]{1,0:T(8,128)(2,1)S(1)} %collective-permute-done.1.refs_2_), channel_id=1, source_target_pairs={{0,32},{32,0},{1,33},{33,1},{2,34},{34,2},{3,35},{35,3},{4,36},{36... | collective-permute-start | bytes 393224 | tf_op jit(solution)/shard_map/ppermute | solution.py:24
  35.6 4.1 %collective-permute-start.10 = (bf16[64,1024]{1,0:T(8,128)(2,1)S(1)}, bf16[64,1024]{1,0:T(8,128)(2,1)S(1)}, u32[]{:S(2)}, u32[]{:S(2)}) collective-permute-start(bf16[64,1024]{1,0:T(8,128)(2,1)S(1)} %collective-permute-done.2.refs_3_), channel_id=1, source_target_pairs={{0,32},{32,0},{1,33},{33,1},{2,34},{34,2},{3,35},{35,3},{4,36},{36... | collective-permute-start | bytes 393224 | tf_op jit(solution)/shard_map/ppermute | solution.py:24
  36.5 3.2 %collective-permute-start.12 = (bf16[64,1024]{1,0:T(8,128)(2,1)S(1)}, bf16[64,1024]{1,0:T(8,128)(2,1)S(1)}, u32[]{:S(2)}, u32[]{:S(2)}) collective-permute-start(bf16[64,1024]{1,0:T(8,128)(2,1)S(1)} %collective-permute-done.6.refs_5_), channel_id=1, source_target_pairs={{0,32},{32,0},{1,33},{33,1},{2,34},{34,2},{3,35},{35,3},{4,36},{36... | collective-permute-start | bytes 393224 | tf_op jit(solution)/shard_map/ppermute | solution.py:24
  37.6 2.2 %collective-permute-start.11 = (bf16[64,1024]{1,0:T(8,128)(2,1)S(1)}, bf16[64,1024]{1,0:T(8,128)(2,1)S(1)}, u32[]{:S(2)}, u32[]{:S(2)}) collective-permute-start(bf16[64,1024]{1,0:T(8,128)(2,1)S(1)} %collective-permute-done.3.refs_4_), channel_id=1, source_target_pairs={{0,32},{32,0},{1,33},{33,1},{2,34},{34,2},{3,35},{35,3},{4,36},{36... | collective-permute-start | bytes 393224 | tf_op jit(solution)/shard_map/ppermute | solution.py:24
  39.7 36.5 %collective-permute-start.16 = (bf16[1024,1024]{1,0:T(8,128)(2,1)}, bf16[1024,1024]{1,0:T(8,128)(2,1)}, u32[]{:S(2)}, u32[]{:S(2)}) collective-permute-start(bf16[1024,1024]{1,0:T(8,128)(2,1)} %bitcast.rows_ref), channel_id=1, source_target_pairs={{0,32},{32,0},{1,33},{33,1},{2,34},{34,2},{3,35},{35,3},{4,36},{36... | collective-permute-start | bytes 6291464 | tf_op jit(solution)/shard_map/ppermute | solution.py:24
  47.0 29.2 %collective-permute-start.15 = (f32[1024,512]{1,0:T(8,128)}, f32[1024,512]{1,0:T(8,128)}, u32[]{:S(2)}, u32[]{:S(2)}) collective-permute-start(f32[1024,512]{1,0:T(8,128)} %get-tuple-element.17.far_ref), channel_id=1, source_target_pairs={{0,32},{32,0},{1,33},{33,1},{2,34},{34,2},{3,35},{35,3},{4,36},{36... | collective-permute-start | bytes 6291464 | tf_op jit(solution)/shard_map/ppermute | solution.py:24
  47.6 8.6 %collective-permute-start.17 = (f32[8,128]{1,0:T(8,128)S(1)}, f32[8,128]{1,0:T(8,128)S(1)}, u32[]{:S(2)}, u32[]{:S(2)}) collective-permute-start(f32[8,128]{1,0:T(8,128)S(1)} %get-tuple-element.19), channel_id=1, source_target_pairs={{0,32},{32,0},{1,33},{33,1},{2,34},{34,2},{3,35},{35,3},{4,36},{36... | collective-permute-start | bytes 12296 | tf_op jit(solution)/shard_map/ppermute | solution.py:24
  47.7 16.5 %all-to-all-start.2 = ((f32[8,8,128]{2,1,0:T(8,128)}), f32[8,8,128]{2,1,0:T(8,128)S(1)}, u32[]{:S(2)}, u32[]{:S(2)}) async-start(f32[8,8,128]{2,1,0:T(8,128)} %get-tuple-element.20), calls=%async_computation.2 | async-start | bytes 65536 | tf_op jit(solution)/shard_map/all_to_all | solution.py:415
  64.9 11.4 %all-to-all-start.1 = ((f32[16,2,8,128]{3,2,1,0:T(8,128)}), f32[16,2,8,128]{3,2,1,0:T(8,128)S(1)}, u32[]{:S(2)}, u32[]{:S(2)}) async-start(f32[16,2,8,128]{3,2,1,0:T(8,128)} %broadcast_in_dim.2), calls=%async_computation.1 | async-start | bytes 262144 | tf_op jit(solution)/shard_map/all_to_all | solution.py:416
  69.9 1.2 %collective-permute-start.18 = (f32[8,8,128]{2,1,0:T(8,128)S(1)}, f32[8,8,128]{2,1,0:T(8,128)S(1)}, u32[]{:S(2)}, u32[]{:S(2)}) collective-permute-start(f32[8,8,128]{2,1,0:T(8,128)S(1)} %all-to-all-done.2.col_parts), channel_id=1, source_target_pairs={{0,32},{32,0},{1,33},{33,1},{2,34},{34,2},{3,35},{35,3},{4,36},{36... | collective-permute-start | bytes 98312 | tf_op jit(solution)/shard_map/ppermute | solution.py:24
  85.6 32.0 %all-to-all-start.3 = ((bf16[16,64,1024]{2,1,0:T(8,128)(2,1)}), bf16[16,64,1024]{2,1,0:T(8,128)(2,1)S(1)}, u32[]{:S(2)}, u32[]{:S(2)}) async-start(bf16[16,64,1024]{2,1,0:T(8,128)(2,1)} %bitcast.7), calls=%async_computation.3 | async-start | bytes 4194304 | tf_op jit(solution)/shard_map/all_to_all | solution.py:422
  90.9 14.4 %collective-permute-start.19 = (bf16[64,1024]{1,0:T(8,128)(2,1)S(1)}, bf16[64,1024]{1,0:T(8,128)(2,1)S(1)}, u32[]{:S(2)}, u32[]{:S(2)}) collective-permute-start(bf16[64,1024]{1,0:T(8,128)(2,1)S(1)} %get-tuple-element.23), channel_id=1, source_target_pairs={{0,4},{1,5},{2,6},{3,7},{4,0},{5,1},{6,2},{7,3},{8,12},{9,13},{10,... | collective-permute-start | bytes 393224 | tf_op jit(solution)/shard_map/ppermute | solution.py:29
  91.4 17.3 %collective-permute-start.20 = (bf16[64,1024]{1,0:T(8,128)(2,1)S(1)}, bf16[64,1024]{1,0:T(8,128)(2,1)S(1)}, u32[]{:S(2)}, u32[]{:S(2)}) collective-permute-start(bf16[64,1024]{1,0:T(8,128)(2,1)S(1)} %get-tuple-element.24), channel_id=1, source_target_pairs={{0,3},{1,4},{2,5},{3,6},{4,7},{5,0},{6,1},{7,2},{8,11},{9,12},{10,... | collective-permute-start | bytes 393224 | tf_op jit(solution)/shard_map/ppermute | solution.py:29
  94.5 18.3 %collective-permute-start.21 = (bf16[64,1024]{1,0:T(8,128)(2,1)}, bf16[64,1024]{1,0:T(8,128)(2,1)S(1)}, u32[]{:S(2)}, u32[]{:S(2)}) collective-permute-start(bf16[64,1024]{1,0:T(8,128)(2,1)} %get-tuple-element.25), channel_id=1, source_target_pairs={{0,5},{1,6},{2,7},{3,0},{4,1},{5,2},{6,3},{7,4},{8,13},{9,14},{10,... | collective-permute-start | bytes 393224 | tf_op jit(solution)/shard_map/ppermute | solution.py:29
  96.4 17.7 %collective-permute-start.22 = (bf16[64,1024]{1,0:T(8,128)(2,1)}, bf16[64,1024]{1,0:T(8,128)(2,1)S(1)}, u32[]{:S(2)}, u32[]{:S(2)}) collective-permute-start(bf16[64,1024]{1,0:T(8,128)(2,1)} %get-tuple-element.26), channel_id=1, source_target_pairs={{0,2},{1,3},{2,4},{3,5},{4,6},{5,7},{6,0},{7,1},{8,10},{9,11},{10,... | collective-permute-start | bytes 393224 | tf_op jit(solution)/shard_map/ppermute | solution.py:29
  98.8 15.9 %collective-permute-start.23 = (bf16[64,1024]{1,0:T(8,128)(2,1)}, bf16[64,1024]{1,0:T(8,128)(2,1)S(1)}, u32[]{:S(2)}, u32[]{:S(2)}) collective-permute-start(bf16[64,1024]{1,0:T(8,128)(2,1)} %get-tuple-element.27), channel_id=1, source_target_pairs={{0,6},{1,7},{2,0},{3,1},{4,2},{5,3},{6,4},{7,5},{8,14},{9,15},{10,... | collective-permute-start | bytes 393224 | tf_op jit(solution)/shard_map/ppermute | solution.py:29
  105.3 10.1 %collective-permute-start.24 = (bf16[64,1024]{1,0:T(8,128)(2,1)S(1)}, bf16[64,1024]{1,0:T(8,128)(2,1)S(1)}, u32[]{:S(2)}, u32[]{:S(2)}) collective-permute-start(bf16[64,1024]{1,0:T(8,128)(2,1)S(1)} %get-tuple-element.28), channel_id=1, source_target_pairs={{0,1},{1,2},{2,3},{3,4},{4,5},{5,6},{6,7},{7,0},{8,9},{9,10},{10,1... | collective-permute-start | bytes 393224 | tf_op jit(solution)/shard_map/ppermute | solution.py:29
  108.7 7.0 %collective-permute-start.25 = (bf16[64,1024]{1,0:T(8,128)(2,1)S(1)}, bf16[64,1024]{1,0:T(8,128)(2,1)S(1)}, u32[]{:S(2)}, u32[]{:S(2)}) collective-permute-start(bf16[64,1024]{1,0:T(8,128)(2,1)S(1)} %get-tuple-element.29), channel_id=1, source_target_pairs={{0,7},{1,0},{2,1},{3,2},{4,3},{5,4},{6,5},{7,6},{8,15},{9,8},{10,9... | collective-permute-start | bytes 393224 | tf_op jit(solution)/shard_map/ppermute | solution.py:29

commit v7 on v6

--- a/solution.py
+++ b/solution.py
@@ -34,10 +34,10 @@
 
 
 def z_steps(size):
-    steps = [size // 2]
-    for step in range(size // 2 - 1, 0, -1):
+    steps = []
+    for step in range(1, size // 2):
         steps += [step, size - step]
-    return steps
+    return steps + [size // 2]
 
 
 def contract(a, b, dim_a, dim_b):

time: 119 us -> 119 us (level)
    ppermute x14, waiting for transfers between devices: 19.8 us -> 21 us  [shift(): lax.ppermute(values, axis, [(i, (i + step) % size) for i in range(size)])]
  transfers between devices with their start and end apart: 30 -> 30, of which waited for: 16 -> 13; matrix products, arithmetic and copies ran while one was open for 1% -> 1% of each run, Pallas kernels for 6% -> 6%
where the time goes in v7:
time: 119 us
  starting transfers between devices  57.9 us (49%)
  waiting for transfers between devices  39.2 us (33%)
  Pallas kernels  20.2 us (17%)
    ppermute x14, starting transfers between devices, shift(): lax.ppermute(values, axis, [(i, (i + step) % size) for i in range(size)])  29.8 us
    ppermute x14, waiting for transfers between devices, shift(): lax.ppermute(values, axis, [(i, (i + step) % size) for i in range(size)])  21 us
    pallas_call x1, Pallas kernels, block_grad(): pl.pallas_call(grad_kernel, in_specs=[in_hbm] * 6 + [in_vmem] * len(parts...  9.33 us
    all_to_all x1, starting transfers between devices, per_device(): col_parts = lax.all_to_all(col_part, 'z', 0, 0)  8.47 us
    all_to_all x1, waiting for transfers between devices, per_device(): col_parts = lax.all_to_all(col_part, 'z', 0, 0)  8.01 us
    all_to_all x1, starting transfers between devices, per_device(): rows = lax.all_to_all(repeat(image_emb, n_plane), plane, 0, 0)  7.54 us
    pallas_call x1, Pallas kernels, block_stats(): pl.pallas_call(stats_kernel, in_specs=[in_hbm] * 2 + [in_vmem] * len(shar...  7.27 us
    all_to_all x1, starting transfers between devices, per_device(): lax.all_to_all(image_part.reshape(n_plane, span, width), plane, 0, 0)  5.28 us
  transfers between devices with their start and end apart: 30, of which 13 were waited for; matrix products, arithmetic and copies ran while one was open for 1% of the time, Pallas kernels for 6%

profile of v7, /device:TPU:8, one launch (start us, length us, event | category | flops | bytes accessed | tf_op | source)
XLA Modules:
  0.0 119.0 jit_solution(11722716859815888205)
XLA Ops:
  0.6 2.4 %repeat.1 = bf16[16,64,1024]{2,1,0:T(8,128)(2,1)} custom-call(bf16[64,1024]{1,0:T(8,128)(2,1)} %in_ref.1), custom_call_target="tpu_custom_call" | custom-call | bytes 2097152 | tf_op jit(solution)/shard_map/repeat/pallas_call | solution.py:135
  3.1 7.5 %all-to-all-start = ((bf16[16,64,1024]{2,1,0:T(8,128)(2,1)}), bf16[16,64,1024]{2,1,0:T(8,128)(2,1)}, u32[]{:S(2)}, u32[]{:S(2)}) async-start(bf16[16,64,1024]{2,1,0:T(8,128)(2,1)} %repeat.1), calls=%async_computation | async-start | bytes 4194304 | tf_op jit(solution)/shard_map/all_to_all | solution.py:403
  10.6 5.9 %collective-permute-start = (bf16[64,1024]{1,0:T(8,128)(2,1)S(1)}, bf16[64,1024]{1,0:T(8,128)(2,1)S(1)}, u32[]{:S(2)}, u32[]{:S(2)}) collective-permute-start(bf16[64,1024]{1,0:T(8,128)(2,1)S(1)} %copy-done), channel_id=1, source_target_pairs={{0,7},{1,0},{2,1},{3,2},{4,3},{5,4},{6,5},{7,6},{8,15},{9,8},{10,9... | collective-permute-start | bytes 393224 | tf_op jit(solution)/shard_map/ppermute | solution.py:29
  16.5 2.5 %collective-permute-done.refs_1_ = bf16[64,1024]{1,0:T(8,128)(2,1)S(1)} collective-permute-done((bf16[64,1024]{1,0:T(8,128)(2,1)S(1)}, bf16[64,1024]{1,0:T(8,128)(2,1)S(1)}, u32[]{:S(2)}, u32[]{:S(2)}) %collective-permute-start) | collective-permute-done | bytes 131104 | tf_op jit(solution)/shard_map/ppermute | solution.py:29
  19.0 3.7 %collective-permute-start.1 = (bf16[64,1024]{1,0:T(8,128)(2,1)S(1)}, bf16[64,1024]{1,0:T(8,128)(2,1)S(1)}, u32[]{:S(2)}, u32[]{:S(2)}) collective-permute-start(bf16[64,1024]{1,0:T(8,128)(2,1)S(1)} %collective-permute-done.refs_1_), channel_id=1, source_target_pairs={{0,7},{1,0},{2,1},{3,2},{4,3},{5,4},{6,5},{7,6},{8,15},{9,8},{10,9... | collective-permute-start | bytes 393224 | tf_op jit(solution)/shard_map/ppermute | solution.py:29
  22.7 2.5 %collective-permute-done.1.refs_2_ = bf16[64,1024]{1,0:T(8,128)(2,1)S(1)} collective-permute-done((bf16[64,1024]{1,0:T(8,128)(2,1)S(1)}, bf16[64,1024]{1,0:T(8,128)(2,1)S(1)}, u32[]{:S(2)}, u32[]{:S(2)}) %collective-permute-start.1) | collective-permute-done | bytes 131104 | tf_op jit(solution)/shard_map/ppermute | solution.py:29
  25.2 3.7 %collective-permute-start.2 = (bf16[64,1024]{1,0:T(8,128)(2,1)S(1)}, bf16[64,1024]{1,0:T(8,128)(2,1)S(1)}, u32[]{:S(2)}, u32[]{:S(2)}) collective-permute-start(bf16[64,1024]{1,0:T(8,128)(2,1)S(1)} %collective-permute-done.1.refs_2_), channel_id=1, source_target_pairs={{0,7},{1,0},{2,1},{3,2},{4,3},{5,4},{6,5},{7,6},{8,15},{9,8},{10,9... | collective-permute-start | bytes 393224 | tf_op jit(solution)/shard_map/ppermute | solution.py:29
  29.4 2.0 %collective-permute-done.2.refs_3_ = bf16[64,1024]{1,0:T(8,128)(2,1)S(1)} collective-permute-done((bf16[64,1024]{1,0:T(8,128)(2,1)S(1)}, bf16[64,1024]{1,0:T(8,128)(2,1)S(1)}, u32[]{:S(2)}, u32[]{:S(2)}) %collective-permute-start.2) | collective-permute-done | bytes 131104 | tf_op jit(solution)/shard_map/ppermute | solution.py:29
  31.4 3.7 %collective-permute-start.3 = (bf16[64,1024]{1,0:T(8,128)(2,1)S(1)}, bf16[64,1024]{1,0:T(8,128)(2,1)S(1)}, u32[]{:S(2)}, u32[]{:S(2)}) collective-permute-start(bf16[64,1024]{1,0:T(8,128)(2,1)S(1)} %collective-permute-done.2.refs_3_), channel_id=1, source_target_pairs={{0,7},{1,0},{2,1},{3,2},{4,3},{5,4},{6,5},{7,6},{8,15},{9,8},{10,9... | collective-permute-start | bytes 393224 | tf_op jit(solution)/shard_map/ppermute | solution.py:29
  35.7 0.8 collective-permute-done.6.refs_5_
  36.5 1.1 collective-permute-done.3.refs_4_
  37.6 2.1 %all-to-all-done = bf16[16,64,1024]{2,1,0:T(8,128)(2,1)} async-done(((bf16[16,64,1024]{2,1,0:T(8,128)(2,1)}), bf16[16,64,1024]{2,1,0:T(8,128)(2,1)}, u32[]{:S(2)}, u32[]{:S(2)}) %all-to-all-start) | async-done | bytes 2097184 | tf_op jit(solution)/shard_map/all_to_all | solution.py:403
  39.8 7.3 %stats.1 = (f32[1024,512]{1,0:T(8,128)}, f32[1024,512]{1,0:T(8,128)}, bf16[1024,1024]{1,0:T(8,128)(2,1)}, f32[8,128]{1,0:T(8,128)S(1)}, f32[8,8,128]{2,1,0:T(8,128)}) custom-call(bf16[1024,1024]{1,0:T(8,128)(2,1)} %bitcast.rows_ref, s32[128,128]{1,0:T(8,128)S(1)} %bitcast.6, bf16[64,1024]{1,0:T(8,128)(2,1)S(1)} %copy-done, ...), custom_call_target="tpu_custom_call" | custom-call | flops 2147483648 | bytes 8388608 | tf_op jit(solution)/shard_map/stats/pallas_call | solution.py:219
  47.0 0.6 collective-permute-start.15
  47.7 8.5 %all-to-all-start.2 = ((f32[8,8,128]{2,1,0:T(8,128)}), f32[8,8,128]{2,1,0:T(8,128)S(1)}, u32[]{:S(2)}, u32[]{:S(2)}) async-start(f32[8,8,128]{2,1,0:T(8,128)} %get-tuple-element.20), calls=%async_computation.2 | async-start | bytes 65536 | tf_op jit(solution)/shard_map/all_to_all | solution.py:415
  56.2 8.0 %all-to-all-done.2.col_parts = f32[8,8,128]{2,1,0:T(8,128)S(1)} async-done(((f32[8,8,128]{2,1,0:T(8,128)}), f32[8,8,128]{2,1,0:T(8,128)S(1)}, u32[]{:S(2)}, u32[]{:S(2)}) %all-to-all-start.2) | async-done | bytes 32800 | tf_op jit(solution)/shard_map/all_to_all | solution.py:415
  64.2 0.7 broadcast_in_dim.2
  64.9 5.0 %all-to-all-start.1 = ((f32[16,2,8,128]{3,2,1,0:T(8,128)}), f32[16,2,8,128]{3,2,1,0:T(8,128)S(1)}, u32[]{:S(2)}, u32[]{:S(2)}) async-start(f32[16,2,8,128]{3,2,1,0:T(8,128)} %broadcast_in_dim.2), calls=%async_computation.1 | async-start | bytes 262144 | tf_op jit(solution)/shard_map/all_to_all | solution.py:416
  69.9 1.2 %collective-permute-done.18.col_others = f32[8,8,128]{2,1,0:T(8,128)S(1)} collective-permute-done((f32[8,8,128]{2,1,0:T(8,128)S(1)}, f32[8,8,128]{2,1,0:T(8,128)S(1)}, u32[]{:S(2)}, u32[]{:S(2)}) %collective-permute-start.18) | collective-permute-done | bytes 32800 | tf_op jit(solution)/shard_map/ppermute | solution.py:24
  71.1 5.2 %all-to-all-done.1.row_parts = f32[16,2,8,128]{3,2,1,0:T(8,128)S(1)} async-done(((f32[16,2,8,128]{3,2,1,0:T(8,128)}), f32[16,2,8,128]{3,2,1,0:T(8,128)S(1)}, u32[]{:S(2)}, u32[]{:S(2)}) %all-to-all-start.1) | async-done | bytes 131104 | tf_op jit(solution)/shard_map/all_to_all | solution.py:416
  76.3 9.3 %grad.1 = (bf16[1024,1024]{1,0:T(8,128)(2,1)}, f32[64,1024]{1,0:T(8,128)S(1)}, bf16[64,1024]{1,0:T(8,128)(2,1)S(1)}, bf16[64,1024]{1,0:T(8,128)(2,1)}, bf16[64,1...) custom-call(f32[1024,512]{1,0:T(8,128)} %get-tuple-element.16.near_r, ...), custom_call_target="tpu_custom_call" | custom-call | flops 4294967296 | bytes 14680064 | tf_op jit(solution)/shard_map/grad/pallas_call | solution.py:341
  85.6 5.3 %all-to-all-start.3 = ((bf16[16,64,1024]{2,1,0:T(8,128)(2,1)}), bf16[16,64,1024]{2,1,0:T(8,128)(2,1)S(1)}, u32[]{:S(2)}, u32[]{:S(2)}) async-start(bf16[16,64,1024]{2,1,0:T(8,128)(2,1)} %bitcast.7), calls=%async_computation.3 | async-start | bytes 4194304 | tf_op jit(solution)/shard_map/all_to_all | solution.py:422
  90.9 0.6 collective-permute-start.19
  91.5 2.7 %collective-permute-start.20 = (bf16[64,1024]{1,0:T(8,128)(2,1)S(1)}, bf16[64,1024]{1,0:T(8,128)(2,1)S(1)}, u32[]{:S(2)}, u32[]{:S(2)}) collective-permute-start(bf16[64,1024]{1,0:T(8,128)(2,1)S(1)} %get-tuple-element.24), channel_id=1, source_target_pairs={{0,7},{1,0},{2,1},{3,2},{4,3},{5,4},{6,5},{7,6},{8,15},{9,8},{10,9... | collective-permute-start | bytes 393224 | tf_op jit(solution)/shard_map/ppermute | solution.py:29
  94.1 4.1 %collective-permute-start.22 = (bf16[64,1024]{1,0:T(8,128)(2,1)}, bf16[64,1024]{1,0:T(8,128)(2,1)S(1)}, u32[]{:S(2)}, u32[]{:S(2)}) collective-permute-start(bf16[64,1024]{1,0:T(8,128)(2,1)} %get-tuple-element.26), channel_id=1, source_target_pairs={{0,6},{1,7},{2,0},{3,1},{4,2},{5,3},{6,4},{7,5},{8,14},{9,15},{10,... | collective-permute-start | bytes 393224 | tf_op jit(solution)/shard_map/ppermute | solution.py:29
  98.3 5.0 %collective-permute-start.24 = (bf16[64,1024]{1,0:T(8,128)(2,1)S(1)}, bf16[64,1024]{1,0:T(8,128)(2,1)S(1)}, u32[]{:S(2)}, u32[]{:S(2)}) collective-permute-start(bf16[64,1024]{1,0:T(8,128)(2,1)S(1)} %get-tuple-element.28), channel_id=1, source_target_pairs={{0,5},{1,6},{2,7},{3,0},{4,1},{5,2},{6,3},{7,4},{8,13},{9,14},{10,... | collective-permute-start | bytes 393224 | tf_op jit(solution)/shard_map/ppermute | solution.py:29
  103.3 0.5 collective-permute-start.25
  103.8 5.4 %collective-permute-done.21.refs_2_ = bf16[64,1024]{1,0:T(8,128)(2,1)S(1)} collective-permute-done((bf16[64,1024]{1,0:T(8,128)(2,1)}, bf16[64,1024]{1,0:T(8,128)(2,1)S(1)}, u32[]{:S(2)}, u32[]{:S(2)}) %collective-permute-start.21) | collective-permute-done | bytes 131104 | tf_op jit(solution)/shard_map/ppermute | solution.py:29
  109.3 1.1 collective-permute-done.23.refs_4_
  110.4 5.5 %collective-permute-done.24.refs_5_ = bf16[64,1024]{1,0:T(8,128)(2,1)S(1)} collective-permute-done((bf16[64,1024]{1,0:T(8,128)(2,1)S(1)}, bf16[64,1024]{1,0:T(8,128)(2,1)S(1)}, u32[]{:S(2)}, u32[]{:S(2)}) %collective-permute-start.24) | collective-permute-done | bytes 131104 | tf_op jit(solution)/shard_map/ppermute | solution.py:29
  115.9 1.7 %all-to-all-done.3.image_parts = bf16[16,64,1024]{2,1,0:T(8,128)(2,1)S(1)} async-done(((bf16[16,64,1024]{2,1,0:T(8,128)(2,1)}), bf16[16,64,1024]{2,1,0:T(8,128)(2,1)S(1)}, u32[]{:S(2)}, u32[]{:S(2)}) %all-to-all-start.3) | async-done | bytes 2097184 | tf_op jit(solution)/shard_map/all_to_all | solution.py:422
  117.6 1.2 %sums.1 = (f32[64,1024]{1,0:T(8,128)}, f32[64,1024]{1,0:T(8,128)}) custom-call(bf16[16,64,1024]{2,1,0:T(8,128)(2,1)S(1)} %all-to-all-done.3.image_parts, f32[64,1024]{1,0:T(8,128)S(1)} %get-tuple-element.22.own_ref, bf16[64,1024]{1,0:T(8,128)(2,1)S(1)} %collective-permute-done.19.refs_0_, bf16[64,1024]{1,0:T(8,128)(2,1)S(1)} %collective-permute-done.20.refs_1_, ...), custom_call_target="tpu_custom_call" | custom-call | flops 1572864 | bytes 4194304 | tf_op jit(solution)/shard_map/sums/pallas_call | solution.py:385
  (38 shorter events, 1.3 us)
Async XLA Ops:
  3.0 7.6 %copy-start = (bf16[64,1024]{1,0:T(8,128)(2,1)S(1)}, bf16[64,1024]{1,0:T(8,128)(2,1)}, u32[]{:S(2)}) copy-start(bf16[64,1024]{1,0:T(8,128)(2,1)} %refs_0_.1) | copy-start | bytes 393220
  3.0 36.7 %copy-start.1 = (s32[16384]{0:T(1024)S(1)}, s32[16384]{0:T(1024)}, u32[]{:S(2)}) copy-start(s32[16384]{0:T(1024)} %param.5) | copy-start | bytes 196612
  3.1 36.7 %all-to-all-start = ((bf16[16,64,1024]{2,1,0:T(8,128)(2,1)}), bf16[16,64,1024]{2,1,0:T(8,128)(2,1)}, u32[]{:S(2)}, u32[]{:S(2)}) async-start(bf16[16,64,1024]{2,1,0:T(8,128)(2,1)} %repeat.1), calls=%async_computation | async-start | bytes 4194304 | tf_op jit(solution)/shard_map/all_to_all | solution.py:403
  10.6 8.5 %collective-permute-start = (bf16[64,1024]{1,0:T(8,128)(2,1)S(1)}, bf16[64,1024]{1,0:T(8,128)(2,1)S(1)}, u32[]{:S(2)}, u32[]{:S(2)}) collective-permute-start(bf16[64,1024]{1,0:T(8,128)(2,1)S(1)} %copy-done), channel_id=1, source_target_pairs={{0,7},{1,0},{2,1},{3,2},{4,3},{5,4},{6,5},{7,6},{8,15},{9,8},{10,9... | collective-permute-start | bytes 393224 | tf_op jit(solution)/shard_map/ppermute | solution.py:29
  16.5 6.2 %collective-permute-start.4 = (bf16[64,1024]{1,0:T(8,128)(2,1)S(1)}, bf16[64,1024]{1,0:T(8,128)(2,1)S(1)}, u32[]{:S(2)}, u32[]{:S(2)}) collective-permute-start(bf16[64,1024]{1,0:T(8,128)(2,1)S(1)} %copy-done), channel_id=1, source_target_pairs={{0,1},{1,2},{2,3},{3,4},{4,5},{5,6},{6,7},{7,0},{8,9},{9,10},{10,1... | collective-permute-start | bytes 393224 | tf_op jit(solution)/shard_map/ppermute | solution.py:29
  19.0 6.2 %collective-permute-start.1 = (bf16[64,1024]{1,0:T(8,128)(2,1)S(1)}, bf16[64,1024]{1,0:T(8,128)(2,1)S(1)}, u32[]{:S(2)}, u32[]{:S(2)}) collective-permute-start(bf16[64,1024]{1,0:T(8,128)(2,1)S(1)} %collective-permute-done.refs_1_), channel_id=1, source_target_pairs={{0,7},{1,0},{2,1},{3,2},{4,3},{5,4},{6,5},{7,6},{8,15},{9,8},{10,9... | collective-permute-start | bytes 393224 | tf_op jit(solution)/shard_map/ppermute | solution.py:29
  22.7 6.7 %collective-permute-start.5 = (bf16[64,1024]{1,0:T(8,128)(2,1)S(1)}, bf16[64,1024]{1,0:T(8,128)(2,1)S(1)}, u32[]{:S(2)}, u32[]{:S(2)}) collective-permute-start(bf16[64,1024]{1,0:T(8,128)(2,1)S(1)} %collective-permute-done.4.refs_7_), channel_id=1, source_target_pairs={{0,1},{1,2},{2,3},{3,4},{4,5},{5,6},{6,7},{7,0},{8,9},{9,10},{10,1... | collective-permute-start | bytes 393224 | tf_op jit(solution)/shard_map/ppermute | solution.py:29
  25.2 6.2 %collective-permute-start.2 = (bf16[64,1024]{1,0:T(8,128)(2,1)S(1)}, bf16[64,1024]{1,0:T(8,128)(2,1)S(1)}, u32[]{:S(2)}, u32[]{:S(2)}) collective-permute-start(bf16[64,1024]{1,0:T(8,128)(2,1)S(1)} %collective-permute-done.1.refs_2_), channel_id=1, source_target_pairs={{0,7},{1,0},{2,1},{3,2},{4,3},{5,4},{6,5},{7,6},{8,15},{9,8},{10,9... | collective-permute-start | bytes 393224 | tf_op jit(solution)/shard_map/ppermute | solution.py:29
  28.9 6.2 %collective-permute-start.7 = (bf16[64,1024]{1,0:T(8,128)(2,1)S(1)}, bf16[64,1024]{1,0:T(8,128)(2,1)S(1)}, u32[]{:S(2)}, u32[]{:S(2)}) collective-permute-start(bf16[64,1024]{1,0:T(8,128)(2,1)S(1)} %copy-done), channel_id=1, source_target_pairs={{0,32},{32,0},{1,33},{33,1},{2,34},{34,2},{3,35},{35,3},{4,36},{36... | collective-permute-start | bytes 393224 | tf_op jit(solution)/shard_map/ppermute | solution.py:24
  28.9 6.2 %collective-permute-start.14 = (bf16[64,1024]{1,0:T(8,128)(2,1)S(1)}, bf16[64,1024]{1,0:T(8,128)(2,1)S(1)}, u32[]{:S(2)}, u32[]{:S(2)}) collective-permute-start(bf16[64,1024]{1,0:T(8,128)(2,1)S(1)} %collective-permute-done.4.refs_7_), channel_id=1, source_target_pairs={{0,32},{32,0},{1,33},{33,1},{2,34},{34,2},{3,35},{35,3},{4,36},{36... | collective-permute-start | bytes 393224 | tf_op jit(solution)/shard_map/ppermute | solution.py:24
  29.4 6.2 %collective-permute-start.8 = (bf16[64,1024]{1,0:T(8,128)(2,1)S(1)}, bf16[64,1024]{1,0:T(8,128)(2,1)S(1)}, u32[]{:S(2)}, u32[]{:S(2)}) collective-permute-start(bf16[64,1024]{1,0:T(8,128)(2,1)S(1)} %collective-permute-done.refs_1_), channel_id=1, source_target_pairs={{0,32},{32,0},{1,33},{33,1},{2,34},{34,2},{3,35},{35,3},{4,36},{36... | collective-permute-start | bytes 393224 | tf_op jit(solution)/shard_map/ppermute | solution.py:24
  29.4 7.1 %collective-permute-start.6 = (bf16[64,1024]{1,0:T(8,128)(2,1)S(1)}, bf16[64,1024]{1,0:T(8,128)(2,1)S(1)}, u32[]{:S(2)}, u32[]{:S(2)}) collective-permute-start(bf16[64,1024]{1,0:T(8,128)(2,1)S(1)} %collective-permute-done.5.refs_6_), channel_id=1, source_target_pairs={{0,1},{1,2},{2,3},{3,4},{4,5},{5,6},{6,7},{7,0},{8,9},{9,10},{10,1... | collective-permute-start | bytes 393224 | tf_op jit(solution)/shard_map/ppermute | solution.py:29
  31.4 6.2 %collective-permute-start.3 = (bf16[64,1024]{1,0:T(8,128)(2,1)S(1)}, bf16[64,1024]{1,0:T(8,128)(2,1)S(1)}, u32[]{:S(2)}, u32[]{:S(2)}) collective-permute-start(bf16[64,1024]{1,0:T(8,128)(2,1)S(1)} %collective-permute-done.2.refs_3_), channel_id=1, source_target_pairs={{0,7},{1,0},{2,1},{3,2},{4,3},{5,4},{6,5},{7,6},{8,15},{9,8},{10,9... | collective-permute-start | bytes 393224 | tf_op jit(solution)/shard_map/ppermute | solution.py:29
  35.1 2.5 %collective-permute-start.13 = (bf16[64,1024]{1,0:T(8,128)(2,1)S(1)}, bf16[64,1024]{1,0:T(8,128)(2,1)S(1)}, u32[]{:S(2)}, u32[]{:S(2)}) collective-permute-start(bf16[64,1024]{1,0:T(8,128)(2,1)S(1)} %collective-permute-done.5.refs_6_), channel_id=1, source_target_pairs={{0,32},{32,0},{1,33},{33,1},{2,34},{34,2},{3,35},{35,3},{4,36},{36... | collective-permute-start | bytes 393224 | tf_op jit(solution)/shard_map/ppermute | solution.py:24
  35.1 4.6 %collective-permute-start.9 = (bf16[64,1024]{1,0:T(8,128)(2,1)S(1)}, bf16[64,1024]{1,0:T(8,128)(2,1)S(1)}, u32[]{:S(2)}, u32[]{:S(2)}) collective-permute-start(bf16[64,1024]{1,0:T(8,128)(2,1)S(1)} %collective-permute-done.1.refs_2_), channel_id=1, source_target_pairs={{0,32},{32,0},{1,33},{33,1},{2,34},{34,2},{3,35},{35,3},{4,36},{36... | collective-permute-start | bytes 393224 | tf_op jit(solution)/shard_map/ppermute | solution.py:24
  35.6 4.1 %collective-permute-start.10 = (bf16[64,1024]{1,0:T(8,128)(2,1)S(1)}, bf16[64,1024]{1,0:T(8,128)(2,1)S(1)}, u32[]{:S(2)}, u32[]{:S(2)}) collective-permute-start(bf16[64,1024]{1,0:T(8,128)(2,1)S(1)} %collective-permute-done.2.refs_3_), channel_id=1, source_target_pairs={{0,32},{32,0},{1,33},{33,1},{2,34},{34,2},{3,35},{35,3},{4,36},{36... | collective-permute-start | bytes 393224 | tf_op jit(solution)/shard_map/ppermute | solution.py:24
  36.5 3.2 %collective-permute-start.12 = (bf16[64,1024]{1,0:T(8,128)(2,1)S(1)}, bf16[64,1024]{1,0:T(8,128)(2,1)S(1)}, u32[]{:S(2)}, u32[]{:S(2)}) collective-permute-start(bf16[64,1024]{1,0:T(8,128)(2,1)S(1)} %collective-permute-done.6.refs_5_), channel_id=1, source_target_pairs={{0,32},{32,0},{1,33},{33,1},{2,34},{34,2},{3,35},{35,3},{4,36},{36... | collective-permute-start | bytes 393224 | tf_op jit(solution)/shard_map/ppermute | solution.py:24
  37.6 2.2 %collective-permute-start.11 = (bf16[64,1024]{1,0:T(8,128)(2,1)S(1)}, bf16[64,1024]{1,0:T(8,128)(2,1)S(1)}, u32[]{:S(2)}, u32[]{:S(2)}) collective-permute-start(bf16[64,1024]{1,0:T(8,128)(2,1)S(1)} %collective-permute-done.3.refs_4_), channel_id=1, source_target_pairs={{0,32},{32,0},{1,33},{33,1},{2,34},{34,2},{3,35},{35,3},{4,36},{36... | collective-permute-start | bytes 393224 | tf_op jit(solution)/shard_map/ppermute | solution.py:24
  39.7 36.5 %collective-permute-start.16 = (bf16[1024,1024]{1,0:T(8,128)(2,1)}, bf16[1024,1024]{1,0:T(8,128)(2,1)}, u32[]{:S(2)}, u32[]{:S(2)}) collective-permute-start(bf16[1024,1024]{1,0:T(8,128)(2,1)} %bitcast.rows_ref), channel_id=1, source_target_pairs={{0,32},{32,0},{1,33},{33,1},{2,34},{34,2},{3,35},{35,3},{4,36},{36... | collective-permute-start | bytes 6291464 | tf_op jit(solution)/shard_map/ppermute | solution.py:24
  47.0 29.2 %collective-permute-start.15 = (f32[1024,512]{1,0:T(8,128)}, f32[1024,512]{1,0:T(8,128)}, u32[]{:S(2)}, u32[]{:S(2)}) collective-permute-start(f32[1024,512]{1,0:T(8,128)} %get-tuple-element.17.far_ref), channel_id=1, source_target_pairs={{0,32},{32,0},{1,33},{33,1},{2,34},{34,2},{3,35},{35,3},{4,36},{36... | collective-permute-start | bytes 6291464 | tf_op jit(solution)/shard_map/ppermute | solution.py:24
  47.6 8.6 %collective-permute-start.17 = (f32[8,128]{1,0:T(8,128)S(1)}, f32[8,128]{1,0:T(8,128)S(1)}, u32[]{:S(2)}, u32[]{:S(2)}) collective-permute-start(f32[8,128]{1,0:T(8,128)S(1)} %get-tuple-element.19), channel_id=1, source_target_pairs={{0,32},{32,0},{1,33},{33,1},{2,34},{34,2},{3,35},{35,3},{4,36},{36... | collective-permute-start | bytes 12296 | tf_op jit(solution)/shard_map/ppermute | solution.py:24
  47.7 16.5 %all-to-all-start.2 = ((f32[8,8,128]{2,1,0:T(8,128)}), f32[8,8,128]{2,1,0:T(8,128)S(1)}, u32[]{:S(2)}, u32[]{:S(2)}) async-start(f32[8,8,128]{2,1,0:T(8,128)} %get-tuple-element.20), calls=%async_computation.2 | async-start | bytes 65536 | tf_op jit(solution)/shard_map/all_to_all | solution.py:415
  64.9 11.4 %all-to-all-start.1 = ((f32[16,2,8,128]{3,2,1,0:T(8,128)}), f32[16,2,8,128]{3,2,1,0:T(8,128)S(1)}, u32[]{:S(2)}, u32[]{:S(2)}) async-start(f32[16,2,8,128]{3,2,1,0:T(8,128)} %broadcast_in_dim.2), calls=%async_computation.1 | async-start | bytes 262144 | tf_op jit(solution)/shard_map/all_to_all | solution.py:416
  69.9 1.2 %collective-permute-start.18 = (f32[8,8,128]{2,1,0:T(8,128)S(1)}, f32[8,8,128]{2,1,0:T(8,128)S(1)}, u32[]{:S(2)}, u32[]{:S(2)}) collective-permute-start(f32[8,8,128]{2,1,0:T(8,128)S(1)} %all-to-all-done.2.col_parts), channel_id=1, source_target_pairs={{0,32},{32,0},{1,33},{33,1},{2,34},{34,2},{3,35},{35,3},{4,36},{36... | collective-permute-start | bytes 98312 | tf_op jit(solution)/shard_map/ppermute | solution.py:24
  85.6 32.0 %all-to-all-start.3 = ((bf16[16,64,1024]{2,1,0:T(8,128)(2,1)}), bf16[16,64,1024]{2,1,0:T(8,128)(2,1)S(1)}, u32[]{:S(2)}, u32[]{:S(2)}) async-start(bf16[16,64,1024]{2,1,0:T(8,128)(2,1)} %bitcast.7), calls=%async_computation.3 | async-start | bytes 4194304 | tf_op jit(solution)/shard_map/all_to_all | solution.py:422
  90.9 7.4 %collective-permute-start.19 = (bf16[64,1024]{1,0:T(8,128)(2,1)S(1)}, bf16[64,1024]{1,0:T(8,128)(2,1)S(1)}, u32[]{:S(2)}, u32[]{:S(2)}) collective-permute-start(bf16[64,1024]{1,0:T(8,128)(2,1)S(1)} %get-tuple-element.23), channel_id=1, source_target_pairs={{0,1},{1,2},{2,3},{3,4},{4,5},{5,6},{6,7},{7,0},{8,9},{9,10},{10,1... | collective-permute-start | bytes 393224 | tf_op jit(solution)/shard_map/ppermute | solution.py:29
  91.5 11.8 %collective-permute-start.20 = (bf16[64,1024]{1,0:T(8,128)(2,1)S(1)}, bf16[64,1024]{1,0:T(8,128)(2,1)S(1)}, u32[]{:S(2)}, u32[]{:S(2)}) collective-permute-start(bf16[64,1024]{1,0:T(8,128)(2,1)S(1)} %get-tuple-element.24), channel_id=1, source_target_pairs={{0,7},{1,0},{2,1},{3,2},{4,3},{5,4},{6,5},{7,6},{8,15},{9,8},{10,9... | collective-permute-start | bytes 393224 | tf_op jit(solution)/shard_map/ppermute | solution.py:29
  94.1 15.2 %collective-permute-start.21 = (bf16[64,1024]{1,0:T(8,128)(2,1)}, bf16[64,1024]{1,0:T(8,128)(2,1)S(1)}, u32[]{:S(2)}, u32[]{:S(2)}) collective-permute-start(bf16[64,1024]{1,0:T(8,128)(2,1)} %get-tuple-element.25), channel_id=1, source_target_pairs={{0,2},{1,3},{2,4},{3,5},{4,6},{5,7},{6,0},{7,1},{8,10},{9,11},{10,... | collective-permute-start | bytes 393224 | tf_op jit(solution)/shard_map/ppermute | solution.py:29
  94.1 15.2 %collective-permute-start.22 = (bf16[64,1024]{1,0:T(8,128)(2,1)}, bf16[64,1024]{1,0:T(8,128)(2,1)S(1)}, u32[]{:S(2)}, u32[]{:S(2)}) collective-permute-start(bf16[64,1024]{1,0:T(8,128)(2,1)} %get-tuple-element.26), channel_id=1, source_target_pairs={{0,6},{1,7},{2,0},{3,1},{4,2},{5,3},{6,4},{7,5},{8,14},{9,15},{10,... | collective-permute-start | bytes 393224 | tf_op jit(solution)/shard_map/ppermute | solution.py:29
  98.3 12.1 %collective-permute-start.23 = (bf16[64,1024]{1,0:T(8,128)(2,1)}, bf16[64,1024]{1,0:T(8,128)(2,1)S(1)}, u32[]{:S(2)}, u32[]{:S(2)}) collective-permute-start(bf16[64,1024]{1,0:T(8,128)(2,1)} %get-tuple-element.27), channel_id=1, source_target_pairs={{0,3},{1,4},{2,5},{3,6},{4,7},{5,0},{6,1},{7,2},{8,11},{9,12},{10,... | collective-permute-start | bytes 393224 | tf_op jit(solution)/shard_map/ppermute | solution.py:29
  98.3 17.6 %collective-permute-start.24 = (bf16[64,1024]{1,0:T(8,128)(2,1)S(1)}, bf16[64,1024]{1,0:T(8,128)(2,1)S(1)}, u32[]{:S(2)}, u32[]{:S(2)}) collective-permute-start(bf16[64,1024]{1,0:T(8,128)(2,1)S(1)} %get-tuple-element.28), channel_id=1, source_target_pairs={{0,5},{1,6},{2,7},{3,0},{4,1},{5,2},{6,3},{7,4},{8,13},{9,14},{10,... | collective-permute-start | bytes 393224 | tf_op jit(solution)/shard_map/ppermute | solution.py:29
  103.3 12.6 %collective-permute-start.25 = (bf16[64,1024]{1,0:T(8,128)(2,1)S(1)}, bf16[64,1024]{1,0:T(8,128)(2,1)S(1)}, u32[]{:S(2)}, u32[]{:S(2)}) collective-permute-start(bf16[64,1024]{1,0:T(8,128)(2,1)S(1)} %get-tuple-element.29), channel_id=1, source_target_pairs={{0,4},{1,5},{2,6},{3,7},{4,0},{5,1},{6,2},{7,3},{8,12},{9,13},{10,... | collective-permute-start | bytes 393224 | tf_op jit(solution)/shard_map/ppermute | solution.py:29
